TPU v7x, 32 devices: a whole 2x2x4 slice. The times are simulated.
32 devices in a mesh: dp: 8 (over y, x, core), mp: 4 (over z).
Axes of the slice: x: 2, y: 2, z: 4, core: 2. Of those that a mesh axis runs over, the one named last changes fastest.
Arguments:
- tokens: bfloat16 [320, 48, 1024], P('mp', 'dp'), may hold values from -6 to 6
- counts: int32 [48], P('dp'), may hold values from 1 to 256, as said below
- norm_gains: float32 [2, 1024], replicated, may hold values from 0.1 to 1.9
- norm_shifts: float32 [2, 1024], replicated, may hold values from -1 to 1
- qkv_weight: bfloat16 [3, 1024, 1024], P(None, 'dp', 'mp'), may hold values from -0.1875 to 0.1875
- qkv_bias: float32 [2, 1024], P(None, 'mp'), may hold values from -1.5 to 1.5
- proj_weight: bfloat16 [1024, 1024], P('mp', 'dp'), may hold values from -2 to 2
- out_biases: float32 [2, 1024], replicated, may hold values from -1.5 to 1.5
- up_weight: bfloat16 [1024, 4096], P('dp', 'mp'), may hold values from -0.1875 to 0.1875
- up_bias: float32 [4096], P('mp'), may hold values from -1.5 to 1.5
- down_weight: bfloat16 [4096, 1024], P('mp', 'dp'), may hold values from -0.09375 to 0.09375
- cotangent: bfloat16 [320, 48, 1024], P('mp', 'dp'), may hold values from -6 to 6
Outputs:
- block_out: bfloat16 [320, 48, 1024], P('mp', 'dp')
- input_grad: bfloat16 [320, 48, 1024], P('mp', 'dp')
- gains_grad: float32 [2, 1024], replicated
- shifts_grad: float32 [2, 1024], replicated
- qkv_grad: float32 [3, 1024, 1024], P(None, 'dp', 'mp')
- bias_grad: float32 [2, 1024], P(None, 'mp')
- proj_grad: float32 [1024, 1024], P('mp', 'dp')
- outbias_grad: float32 [2, 1024], replicated
- up_grad: float32 [1024, 4096], P('dp', 'mp')
- upbias_grad: float32 [4096], P('mp')
- down_grad: float32 [4096, 1024], P('mp', 'dp')
Inputs may be any that keep to these rules, and one draw needn't show every extreme that they name: `counts`: in each aligned block of 6 images one image has exactly 256 kept tokens.
All inputs are finite; a program needn't handle non-finite values.
Results may differ from a plain program's by a relative error of at most 0.012.
The roundings to bfloat16 on the way count: a program that leaves them out, or rounds other values in their place, can miss the bound.
Values may be sent and summed in bfloat16 or wider, within the bound.
No kernel may reach another device: no remote copies, remote signals or barrier semaphores. Data moves between devices by JAX's collectives and lax.ppermute only.
A program may use at most 128 MiB of HBM per device.

v0:
```python
import functools

import jax
import jax.numpy as jnp
from jax import lax
from jax.experimental import pallas as pl
from jax.experimental.pallas import tpu as pltpu
from jax.sharding import PartitionSpec as P

HEAD = 64
BUF = 64
BF = jnp.bfloat16
F32 = jnp.float32
epsilon = 1e-06
masked_score = -1e30
MIB = 1 << 20
NT = (((1,), (1,)), ((), ()))
NN = (((1,), (0,)), ((), ()))
TN = (((0,), (0,)), ((), ()))
factor = HEAD ** (-0.5)
VMEM_SPEC = pl.BlockSpec(memory_space=pltpu.VMEM)
ANY_SPEC = pl.BlockSpec(memory_space=pl.ANY)
SMEM_SPEC = pl.BlockSpec(memory_space=pltpu.SMEM)


def mm(a, b, dims=NN):
    return lax.dot_general(a, b, dims, preferred_element_type=F32)


def normalise(values):
    average = jnp.mean(values, axis=-1, keepdims=True)
    centred = values - average
    spread = jnp.mean(centred * centred, axis=-1, keepdims=True)
    inv = lax.rsqrt(spread + epsilon)
    return centred * inv, inv


def norm_back(n, inv, scales, grad):
    e = grad * scales
    mean_e = jnp.mean(e, axis=-1, keepdims=True)
    mean_en = jnp.mean(e * n, axis=-1, keepdims=True)
    return (e - mean_e - n * mean_en) * inv


def gelu_parts(inputs):
    normal_cdf = 0.5 + 0.5 * lax.erf(inputs * 0.7071067811865476)
    density = jnp.exp(-0.5 * inputs * inputs) * 0.3989422804014327
    return inputs * normal_cdf, normal_cdf + inputs * density


def for_each(count, step):
    if count <= 4:
        for index in range(count):
            step(index)
    else:
        pl.loop(0, count)(step)


def valid_slots(meta_ref, image, slots, axis):
    shape = (slots, 1) if axis == 0 else (1, slots)
    row = lax.broadcasted_iota(jnp.int32, shape, axis)
    n = slots // 4
    k = (row >= n).astype(jnp.int32) + (row >= 2 * n) + (row >= 3 * n)
    slot = (k ^ meta_ref[3]) * n + (row - k * n)
    return slot < BUF + meta_ref[image]


def block_rows(jj, size):
    start = jj * size
    return pl.ds(start if isinstance(jj, int) else pl.multiple_of(start, size), size)


def load_blocks(parts, refs, q, kinds, wq, wanted, place, sem):
    for (j0, i0, t0, count, absolute), ref in zip(parts, refs):
        nj, ni = ref.shape[:2]

        def one(jj, ref=ref, j0=j0, i0=i0, t0=t0, count=count, absolute=absolute, ni=ni):
            source = jj ^ q if absolute else jj
            for ii in range(ni):
                if i0 + ii not in wanted:
                    continue
                for t in range(t0, t0 + count):
                    if t in kinds:
                        pltpu.make_async_copy(
                            ref.at[source, ii, pl.ds((t - t0) * wq, wq)],
                            place(block_rows(j0 + jj, wq), i0 + ii, t),
                            sem,
                        ).start()

        for_each(nj, one)


def store_blocks(refs, q, n_j, block, i, sem, pair=0):
    def start(views, target):
        for t, view in enumerate(views):
            pltpu.make_async_copy(view, target.at[t], sem).start()

    if len(refs) == 1:
        for_each(n_j, lambda jj: start(block(jj), refs[0].at[jj ^ q, 2 * pair + i]))
        return
    own, to_x, to_y, keep_x, keep_y = refs
    start(block(0), own.at[2 * pair + i])
    if i == 0:
        start(block(1), keep_x.at[pair])
        start(block(2), to_y.at[2 * pair + 1])
        start(block(3), to_y.at[2 * pair])
    else:
        start(block(1), to_x.at[2 * pair + 1])
        start(block(2), keep_y.at[pair])
        start(block(3), to_x.at[2 * pair])


def grad_shapes(n_j, n_i, absolute, block):
    shape = lambda *lead: jax.ShapeDtypeStruct(lead + block, BF)
    if absolute:
        return [shape(n_j, n_i)]
    return [shape(n_i), shape(n_i), shape(n_i), shape(n_i // 2), shape(n_i // 2)]


def att_column(n_i, i, t):
    he = 2 * HEAD
    if t == 3:
        return 3 * n_i * he + i * he
    return (i // 2) * 6 * he + (t * 2 + i % 2) * he


def att_fwd_kernel(parts, n_i, x_ref, g_ref, c_ref, bias_ref, meta_ref, *rest):
    w_refs = rest[: len(parts)]
    n1_ref, qkva_ref, qkvb_ref, mixa_ref, mixb_ref, part_ref, w_scr, m_scr, sem = rest[len(parts) :]
    he = 2 * HEAD
    width = w_scr.shape[0]
    image = pl.program_id(0)

    @pl.when(image == 0)
    def _():
        place = lambda rows, i, t: w_scr.at[rows, pl.ds(att_column(n_i, i, t), he)]
        wq = width // max(p[0] + r.shape[0] for p, r in zip(parts, w_refs))
        load_blocks(parts, w_refs, meta_ref[4], range(4), wq, range(n_i), place, sem)
        pltpu.make_async_copy(w_scr, w_scr, sem).wait()

    hat, _ = normalise(x_ref[0].astype(F32))
    n1 = (hat * g_ref[...] + c_ref[...]).astype(BF)
    n1_ref[...] = n1
    qkv_refs = (qkva_ref, qkvb_ref)
    for half in range(2):
        cols = pl.ds(half * 6 * he, 6 * he)
        res = (mm(n1, w_scr[:, cols]) + bias_ref[:, cols]).astype(BF)
        for n in range(6):
            qkv_refs[half][n] = res[:, n * he : (n + 1) * he]
    bias = jnp.where(valid_slots(meta_ref, image, x_ref.shape[1], 1), 0.0, masked_score)
    lane = lax.broadcasted_iota(jnp.int32, (1, he), 1)
    low_half = lane < HEAD
    for i in range(n_i):
        ref = qkv_refs[i // 2]
        q2, k2, v2 = (ref[t * 2 + i % 2] for t in range(3))
        outs = []
        for h in range(2):
            qm = jnp.where(low_half if h == 0 else ~low_half, q2, jnp.zeros_like(q2))
            s = mm(qm, k2, NT) * factor + bias
            top = jnp.max(s, axis=-1, keepdims=True)
            p = jnp.exp(s - top)
            w = (p / jnp.sum(p, axis=-1, keepdims=True)).astype(BF)
            outs.append(mm(w, v2))
        mixed = jnp.where(low_half, outs[0], outs[1]).astype(BF)
        m_scr[:, i * he : (i + 1) * he] = mixed
    mixa_ref[...] = m_scr[:, : 2 * he]
    mixb_ref[...] = m_scr[:, 2 * he :]
    part_ref[...] = mm(m_scr[...], w_scr[:, 3 * n_i * he :], NT).astype(BF)


def att_forward(x, gain, shift, bias, meta, parts, arrays):
    images, slots, width = x.shape
    n_i = 4
    he = 2 * HEAD
    rows = images * slots
    row_block = lambda last: pl.BlockSpec((slots, last), lambda a: (a, 0))
    whole = lambda *shape: pl.BlockSpec(shape, lambda a: (0,) * len(shape))
    qkv_block = pl.BlockSpec((6, slots, he), lambda a: (0, a, 0))
    return pl.pallas_call(
        functools.partial(att_fwd_kernel, parts, n_i),
        grid=(images,),
        in_specs=[
            pl.BlockSpec((1, slots, width), lambda a: (a, 0, 0)),
            whole(1, width),
            whole(1, width),
            whole(1, 3 * n_i * he),
            SMEM_SPEC,
        ]
        + [ANY_SPEC] * len(arrays),
        out_specs=[row_block(width), qkv_block, qkv_block, row_block(2 * he), row_block(2 * he), row_block(width)],
        out_shape=[
            jax.ShapeDtypeStruct((rows, width), BF),
            jax.ShapeDtypeStruct((6, rows, he), BF),
            jax.ShapeDtypeStruct((6, rows, he), BF),
            jax.ShapeDtypeStruct((rows, 2 * he), BF),
            jax.ShapeDtypeStruct((rows, 2 * he), BF),
            jax.ShapeDtypeStruct((rows, width), BF),
        ],
        scratch_shapes=[
            pltpu.VMEM((width, 4 * n_i * he), BF),
            pltpu.VMEM((slots, n_i * he), BF),
            pltpu.SemaphoreType.DMA,
        ],
        compiler_params=pltpu.CompilerParams(vmem_limit_bytes=48 * MIB),
        cost_estimate=pl.CostEstimate(flops=16_000_000_000, bytes_accessed=20_000_000, transcendentals=2_500_000),
        name="att_forward",
    )(x, gain, shift, bias, meta, *arrays)


def ffn_kernel(parts, n_i, n_j, n_out, first, *refs):
    if first:
        x_ref, pa_ref, pb_ref, b_ref, g_ref, c_ref = refs[:6]
        refs = refs[6:]
    else:
        kept, refs = refs[:5], refs[5:]
    go_ref, upb_ref, meta_ref = refs[:3]
    w_refs, refs = refs[3 : 3 + len(parts)], refs[3 + len(parts) :]
    q = meta_ref[4]
    if first:
        hidden_out, refs = refs[0], refs[1:]
        kept, refs = refs[:5], refs[5:]
        sum_outs = kept[3:]
    else:
        sum_outs, refs = refs[:2], refs[2:]
    upg_ref, refs = refs[0], refs[1:]
    grad_refs, refs = refs[:n_out], refs[n_out:]
    n2, n2t, got, run_b, run_g, wbuf, gbuf, act_s, pre_s, wsem, gsem, ksem, ssem = refs[:13]
    held = (n2, n2t, got, run_b, run_g)
    if first:
        hidden, hsem = refs[13:]
        low_sums = (run_b, run_g)
    else:
        low_sums = refs[13:]
    rows, width = go_ref.shape
    wq = width // n_j
    rb = rows // 3

    def fetch(i, slot):
        place = lambda rws, _, t: wbuf.at[slot, t, rws]
        load_blocks(parts, w_refs, q, range(2), wq, (i,), place, wsem.at[slot])

    def fetched(slot):
        pltpu.make_async_copy(wbuf.at[slot], wbuf.at[slot], wsem.at[slot]).wait()

    def put(i, slot):
        block = lambda jj: [gbuf.at[slot, t, block_rows(jj, wq)] for t in range(2)]
        store_blocks(grad_refs, q, n_j, block, i, gsem.at[slot])

    def stored(slot):
        pltpu.make_async_copy(gbuf.at[slot], gbuf.at[slot], gsem.at[slot]).wait()

    def keep(n):
        if first:
            return pltpu.make_async_copy(held[n], kept[n], ksem.at[n])
        return pltpu.make_async_copy(kept[n], held[n], ksem.at[n])

    fetch(0, 0)
    if first:
        block = 192

        @pl.loop(0, rows // block)
        def _(r):
            rw = pl.ds(pl.multiple_of(r * block, block), block)
            h = (
                x_ref[rw, :].astype(F32)
                + (pa_ref[rw, :].astype(F32) + pb_ref[rw, :].astype(F32))
                + b_ref[...]
            )
            hidden[rw, :] = h
            hat, _ = normalise(h)
            n2[rw, :] = (hat * g_ref[...] + c_ref[...]).astype(BF)

        pltpu.make_async_copy(hidden, hidden_out, hsem).start()
        keep(0).start()
        n2t[...] = n2[...].T
        keep(1).start()
        got[...] = go_ref[...].T
        keep(2).start()
    else:
        for n in (0, 3, 4, 1, 2):
            keep(n).start()
        keep(0).wait()
    for i in range(n_i):
        slot = i % 2
        if i + 1 < n_i:
            fetch(i + 1, 1 - slot)
        fetched(slot)
        if i == 0 and not first:
            keep(3).wait()
            keep(4).wait()

        @pl.loop(0, 3)
        def _(r, i=i, slot=slot):
            rw = pl.ds(pl.multiple_of(r * rb, rb), rb)
            u, w = wbuf[slot, 0], wbuf[slot, 1]
            up = mm(n2[rw, :], u) + upb_ref[i : i + 1, :]
            act, slope = gelu_parts(up)
            act = act.astype(BF)
            act_s[rw, :] = act
            pre = (mm(go_ref[rw, :], w) * slope).astype(BF)
            pre_s[rw, :] = pre
            down = mm(act, w, NT)
            back = mm(pre, u, NT)
            if i > 0 or not first:
                down += run_b[rw, :]
                back += run_g[rw, :]
            if i < n_i - 1:
                run_b[rw, :] = down
                run_g[rw, :] = back
            else:
                for n, total in enumerate((down, back)):
                    low_sums[n][rw, :] = total.astype(low_sums[n].dtype)
                    pltpu.make_async_copy(low_sums[n].at[rw], sum_outs[n].at[rw], ssem.at[n]).start()

        if i == 0 and not first:
            keep(1).wait()
            keep(2).wait()
        upg_ref[i : i + 1, :] = jnp.sum(pre_s[...].astype(F32), axis=0, keepdims=True)
        if i >= 2:
            stored(slot)
        gbuf[slot, 0] = mm(n2t[...], pre_s[...]).astype(BF)
        gbuf[slot, 1] = mm(got[...], act_s[...]).astype(BF)
        put(i, slot)
    for n in range(2):
        pltpu.make_async_copy(low_sums[n], sum_outs[n], ssem.at[n]).wait()
    if first:
        pltpu.make_async_copy(hidden, hidden_out, hsem).wait()
        for n in range(3):
            keep(n).wait()
    for i in range(max(n_i - 2, 0), n_i):
        stored(i % 2)


def ffn_call(ins, n_j, n_i, fh, parts, arrays, first, absolute):
    go = ins[-3]
    rows, width = go.shape
    wq = width // n_j
    wide, low, turned = (rows, width, F32), (rows, width, BF), (width, rows, BF)
    outs = [wide, low, turned, turned, wide, wide] if first else [low, low]
    grads = grad_shapes(n_j, n_i, absolute, (2, wq, fh))
    if first:
        in_specs = [VMEM_SPEC] * (len(ins) - 1)
    else:
        in_specs = [ANY_SPEC] * 5 + [VMEM_SPEC] * 2
    extra = (
        [pltpu.VMEM((rows, width), F32), pltpu.SemaphoreType.DMA]
        if first
        else [pltpu.VMEM((rows, width), BF)] * 2
    )
    return pl.pallas_call(
        functools.partial(ffn_kernel, parts, n_i, n_j, len(grads), first),
        in_specs=in_specs + [SMEM_SPEC] + [ANY_SPEC] * len(arrays),
        out_specs=[ANY_SPEC] * len(outs) + [VMEM_SPEC] + [ANY_SPEC] * len(grads),
        out_shape=[jax.ShapeDtypeStruct((m, n), kind) for m, n, kind in outs]
        + [jax.ShapeDtypeStruct((n_i, fh), F32)]
        + grads,
        scratch_shapes=[
            pltpu.VMEM((rows, width), BF),
            pltpu.VMEM((width, rows), BF),
            pltpu.VMEM((width, rows), BF),
            pltpu.VMEM((rows, width), F32),
            pltpu.VMEM((rows, width), F32),
            pltpu.VMEM((2, 2, width, fh), BF),
            pltpu.VMEM((2, 2, width, fh), BF),
            pltpu.VMEM((rows, fh), BF),
            pltpu.VMEM((rows, fh), BF),
            pltpu.SemaphoreType.DMA((2,)),
            pltpu.SemaphoreType.DMA((2,)),
            pltpu.SemaphoreType.DMA((5,)),
            pltpu.SemaphoreType.DMA((2,)),
        ]
        + extra,
        compiler_params=pltpu.CompilerParams(vmem_limit_bytes=56 * MIB),
        cost_estimate=pl.CostEstimate(
            flops=12_000_000_000 * n_i, bytes_accessed=30_000_000, transcendentals=1_000_000 * n_i
        ),
        name="ffn_first" if first else "ffn_last",
    )(*ins, *arrays)


def att_back_blocks(meta_ref, qkv_ref, gmix, gq, rows, which):
    he = 2 * HEAD
    images = 3
    slots = rows // images
    lane = lax.broadcasted_iota(jnp.int32, (1, he), 1)
    low_half = lane < HEAD

    @pl.loop(0, images)
    def _(a):
        rw = pl.ds(pl.multiple_of(a * slots, slots), slots)
        bias = jnp.where(valid_slots(meta_ref, a, slots, 0), 0.0, masked_score)
        for i in range(2):
            q2, k2, v2 = (qkv_ref[t * 2 + i, rw, :] for t in range(3))
            g2 = gmix[which + i, rw, :]
            dq, dk, dv = [], [], []
            for h in range(2):
                here = low_half if h == 0 else ~low_half
                qm = jnp.where(here, q2, jnp.zeros_like(q2))
                gm = jnp.where(here, g2, jnp.zeros_like(g2))
                st = mm(k2, qm, NT) * factor + bias
                top = jnp.max(st, axis=0, keepdims=True)
                p = jnp.exp(st - top)
                p = p / jnp.sum(p, axis=0, keepdims=True)
                dpt = mm(v2, gm, NT)
                dot = jnp.sum(p * dpt, axis=0, keepdims=True)
                ds = (p * (dpt - dot)).astype(BF)
                dk.append(mm(ds, q2))
                dv.append(mm(p.astype(BF), g2))
                dq.append(mm(ds, k2, TN))
            for t, (pair, scale) in enumerate(((dq, factor), (dk, factor), (dv, 1.0))):
                both = jnp.where(low_half, pair[0], pair[1])
                gq[rw, (t * 2 + i) * he : (t * 2 + i + 1) * he] = (both * scale).astype(BF)


def put_att_grads(grad_refs, q, n_j, wq, gbuf, gsem, pair):
    he = 2 * HEAD
    for i in range(2):
        block = lambda jj, i=i: [
            gbuf.at[t, block_rows(jj, wq), pl.ds(i * he, he)] for t in range(4)
        ]
        store_blocks(grad_refs, q, n_j, block, i, gsem, pair)


def hidden_back_kernel(
    parts, n_i, n_j, meta_ref, hid_ref, ga_ref, gb_ref, g_ref, go_ref, *rest
):
    w_refs = rest[: len(parts)]
    gh_ref, ght, gmixa, gmixb, sums_ref = rest[len(parts) : len(parts) + 5]
    ghb, w_scr, sem = rest[len(parts) + 5 :]
    rows, width = hid_ref.shape
    he = 2 * HEAD
    place = lambda rws, i, t: w_scr.at[rws, pl.ds(i * he, he)]
    load_blocks(parts, w_refs, meta_ref[4], (3,), width // n_j, range(n_i), place, sem)
    sums_ref[...] = jnp.zeros_like(sums_ref)
    pltpu.make_async_copy(w_scr, w_scr, sem).wait()
    block = 192

    @pl.loop(0, rows // block)
    def _(r):
        rw = pl.ds(pl.multiple_of(r * block, block), block)
        hat, inv = normalise(hid_ref[rw, :])
        grad = ga_ref[rw, :].astype(F32) + gb_ref[rw, :].astype(F32)
        gout = go_ref[rw, :].astype(F32)
        gh = gout + norm_back(hat, inv, g_ref[...], grad)
        gh_ref[rw, :] = gh
        low = gh.astype(BF)
        ghb[rw, :] = low
        sums_ref[0:1, :] += jnp.sum(grad * hat, axis=0, keepdims=True)
        sums_ref[1:2, :] += jnp.sum(grad, axis=0, keepdims=True)
        sums_ref[2:3, :] += jnp.sum(gh, axis=0, keepdims=True)
        sums_ref[3:4, :] += jnp.sum(gout, axis=0, keepdims=True)
        res = mm(low, w_scr[...]).astype(BF)
        for i in range(n_i):
            (gmixa, gmixb)[i // 2][i % 2, rw, :] = res[:, i * he : (i + 1) * he]

    ght[...] = ghb[...].T


def hidden_backward(meta, hidden, ga, gb, gain, go, n_j, parts, arrays):
    rows, width = hidden.shape
    n_i, he = 4, 2 * HEAD
    return pl.pallas_call(
        functools.partial(hidden_back_kernel, parts, n_i, n_j),
        in_specs=[SMEM_SPEC] + [VMEM_SPEC] * 5 + [ANY_SPEC] * len(arrays),
        out_specs=[VMEM_SPEC] * 5,
        out_shape=[
            jax.ShapeDtypeStruct((rows, width), F32),
            jax.ShapeDtypeStruct((width, rows), BF),
            jax.ShapeDtypeStruct((2, rows, he), BF),
            jax.ShapeDtypeStruct((2, rows, he), BF),
            jax.ShapeDtypeStruct((8, width), F32),
        ],
        scratch_shapes=[
            pltpu.VMEM((rows, width), BF),
            pltpu.VMEM((width, n_i * he), BF),
            pltpu.SemaphoreType.DMA,
        ],
        compiler_params=pltpu.CompilerParams(vmem_limit_bytes=48 * MIB),
        cost_estimate=pl.CostEstimate(flops=10_000_000_000, bytes_accessed=20_000_000, transcendentals=0),
        name="hidden_backward",
    )(meta, hidden, ga, gb, gain, go, *arrays)


def att_bwd_first_kernel(n_i, n_j, n_out, meta_ref, gmix, ght, n1_ref, qkv_ref, mix_ref, *rest):
    n1t, gq, bias_ref = rest[:3]
    grad_refs = rest[3 : 3 + n_out]
    gbuf, gsem = rest[3 + n_out :]
    width, rows = ght.shape
    he = 2 * HEAD
    gbuf[3] = mm(ght[...], mix_ref[...]).astype(BF)
    att_back_blocks(meta_ref, qkv_ref, gmix, gq, rows, 0)
    n1t[...] = n1_ref[...].T
    for t in range(3):
        gbuf[t] = mm(n1t[...], gq[:, 2 * t * he : 2 * (t + 1) * he]).astype(BF)
    put_att_grads(grad_refs, meta_ref[4], n_j, width // n_j, gbuf, gsem, 0)
    bias_ref[...] = jnp.sum(gq[...].astype(F32), axis=0, keepdims=True)
    pltpu.make_async_copy(gbuf, gbuf, gsem).wait()


def att_backward_first(meta, gmix, ght, n1, qkv, mix, n_j, absolute):
    width, rows = ght.shape
    n_i, he = 4, 2 * HEAD
    wq = width // n_j
    grads = grad_shapes(n_j, n_i, absolute, (4, wq, he))
    return pl.pallas_call(
        functools.partial(att_bwd_first_kernel, n_i, n_j, len(grads)),
        in_specs=[SMEM_SPEC] + [VMEM_SPEC] * 5,
        out_specs=[VMEM_SPEC] * 3 + [ANY_SPEC] * len(grads),
        out_shape=[
            jax.ShapeDtypeStruct((width, rows), BF),
            jax.ShapeDtypeStruct((rows, 6 * he), BF),
            jax.ShapeDtypeStruct((1, 6 * he), F32),
        ]
        + grads,
        scratch_shapes=[pltpu.VMEM((4, width, 2 * he), BF), pltpu.SemaphoreType.DMA],
        compiler_params=pltpu.CompilerParams(vmem_limit_bytes=60 * MIB),
        cost_estimate=pl.CostEstimate(flops=16_000_000_000, bytes_accessed=20_000_000, transcendentals=1_250_000),
        name="att_backward_first",
    )(meta, gmix, ght, n1, qkv, mix)


def att_bwd_last_kernel(
    parts, n_i, n_j, n_out, meta_ref, x_ref, gmix, ght, n1t, gqa_ref, qkv_ref, mix_ref, *rest
):
    w_refs = rest[: len(parts)]
    rest = rest[len(parts) + n_out :]
    gn1_ref, bias_ref, sums_ref = rest[:3]
    rest = rest[3:]
    grad_refs = rest[:n_out]
    gq, w_scr, gbuf, sem, gsem = rest[n_out:]
    rows, width = x_ref.shape
    he = 2 * HEAD
    wq = width // n_j
    q = meta_ref[4]
    place = lambda rws, i, t: w_scr.at[rws, pl.ds(att_column(n_i, i, t), he)]
    load_blocks(parts, w_refs, q, (0, 1, 2), wq, range(n_i), place, sem)
    gbuf[3] = mm(ght[...], mix_ref[...]).astype(BF)
    att_back_blocks(meta_ref, qkv_ref, gmix, gq, rows, 0)
    for t in range(3):
        gbuf[t] = mm(n1t[...], gq[:, 2 * t * he : 2 * (t + 1) * he]).astype(BF)
    put_att_grads(grad_refs, q, n_j, wq, gbuf, gsem, 1)
    bias_ref[...] = jnp.sum(gq[...].astype(F32), axis=0, keepdims=True)
    sums_ref[...] = jnp.zeros_like(sums_ref)
    pltpu.make_async_copy(w_scr, w_scr, sem).wait()
    rb = rows // 3

    @pl.loop(0, 3)
    def _(r):
        rw = pl.ds(pl.multiple_of(r * rb, rb), rb)
        grad = mm(gqa_ref[rw, :], w_scr[:, : 6 * he], NT) + mm(gq[rw, :], w_scr[:, 6 * he :], NT)
        gn1_ref[rw, :] = grad.astype(BF)
        hat, _ = normalise(x_ref[rw, :].astype(F32))
        sums_ref[0:1, :] += jnp.sum(grad * hat, axis=0, keepdims=True)
        sums_ref[1:2, :] += jnp.sum(grad, axis=0, keepdims=True)

    pltpu.make_async_copy(gbuf, gbuf, gsem).wait()


def att_backward_last(meta, x, gmix, ght, n1t, gqa, qkv, mix, n_j, parts, arrays, first_grads):
    rows, width = x.shape
    n_i, he = 4, 2 * HEAD
    grads = [jax.ShapeDtypeStruct(v.shape, v.dtype) for v in first_grads]
    return pl.pallas_call(
        functools.partial(att_bwd_last_kernel, parts, n_i, n_j, len(grads)),
        in_specs=[SMEM_SPEC] + [VMEM_SPEC] * 7 + [ANY_SPEC] * (len(arrays) + len(grads)),
        out_specs=[VMEM_SPEC] * 3 + [ANY_SPEC] * len(grads),
        out_shape=[
            jax.ShapeDtypeStruct((rows, width), BF),
            jax.ShapeDtypeStruct((1, 6 * he), F32),
            jax.ShapeDtypeStruct((8, width), F32),
        ]
        + grads,
        scratch_shapes=[
            pltpu.VMEM((rows, 6 * he), BF),
            pltpu.VMEM((width, 3 * n_i * he), BF),
            pltpu.VMEM((4, width, 2 * he), BF),
            pltpu.SemaphoreType.DMA,
            pltpu.SemaphoreType.DMA,
        ],
        compiler_params=pltpu.CompilerParams(vmem_limit_bytes=56 * MIB),
        cost_estimate=pl.CostEstimate(flops=20_000_000_000, bytes_accessed=30_000_000, transcendentals=1_250_000),
        input_output_aliases={8 + len(arrays) + n: 3 + n for n in range(len(grads))},
        name="att_backward_last",
    )(meta, x, gmix, ght, n1t, gqa, qkv, mix, *arrays, *first_grads)


def swap(x, axis, bits, what):
    n = lax.axis_size(axis)
    with jax.named_scope(what):
        return lax.ppermute(x, axis, [(i, i ^ bits) for i in range(n)])


def after(x, *deps):
    return lax.optimization_barrier((x,) + deps)[0] if deps else x


def add(*parts):
    total = parts[0].astype(F32)
    for part in parts[1:]:
        total = total + part.astype(F32)
    return total.astype(parts[0].dtype)


def planes():
    n_dp = lax.axis_size("dp")
    return [list(range(core, n_dp, 2)) for core in range(2)]


def gather_plane(block, what):
    with jax.named_scope(what):
        return lax.all_gather(block, "dp", axis_index_groups=planes())


def scatter_plane(blocks, what):
    flat = blocks.reshape(-1, blocks.shape[-1])
    with jax.named_scope(what):
        mine = lax.psum_scatter(
            flat, "dp", scatter_dimension=0, axis_index_groups=planes(), tiled=True
        )
    return mine.reshape(blocks.shape[1:])


def gather_near(own, what):
    return swap(own, "dp", 2, what + "_x1"), swap(own, "dp", 4, what + "_y1")


def gather_far(one, two, what):
    half = one.shape[0] // 2
    return swap(one[:half], "dp", 4, what + "_y2"), swap(two[half:], "dp", 2, what + "_x2")


def scatter_reach(grads, what):
    if len(grads) == 1:
        return (scatter_plane(grads[0], what),)
    _, to_x, to_y, _, _ = grads
    return swap(to_x, "dp", 2, what + "_x1"), swap(to_y, "dp", 4, what + "_y1")


def scatter_last(grads, reach, what):
    if len(grads) == 1:
        return ()
    from_x, from_y = reach
    _, _, _, keep_x, keep_y = grads
    on_x, on_y = add(keep_x, from_y[0::2]), add(keep_y, from_x[0::2])
    return swap(on_x, "dp", 2, what + "_x2"), swap(on_y, "dp", 4, what + "_y2")


def scatter_sum(grads, reach, last):
    if len(grads) == 1:
        return [reach[0][i] for i in range(reach[0].shape[0])]
    own = grads[0]
    return [
        add(own[i], reach[1 - i % 2][i + 1 - i % 2], last[i % 2][i // 2]) for i in range(own.shape[0])
    ]


def gather_z(own, what):
    two = swap(own, "mp", 2, what + "_z2")
    one = swap(own, "mp", 1, what + "_z1")
    return one, two, swap(two, "mp", 1, what + "_z3")


def scatter_z(zero, one, two, three, what):
    two = add(two, swap(three, "mp", 1, what + "_z3"))
    return add(zero, swap(one, "mp", 1, what + "_z1"), swap(two, "mp", 2, what + "_z2"))


def ordered_pair(own, other, core, axis=0):
    return jnp.stack(
        [jnp.where(core == 0, own, other), jnp.where(core == 0, other, own)], axis
    )


def image_routes(n_dp, n_mp, odd):
    pairs = []
    for plane in range(n_dp // 2):
        for core in range(2):
            for z in range(n_mp):
                shift = 2 * core + odd
                worker = (plane * 2 + core) * n_mp + z
                holder = (plane * 2 + (z >> 1)) * n_mp + (z ^ shift)
                pairs.append((holder, worker))
    return pairs


def image_groups(x):
    slots, images, width = x.shape
    return jnp.transpose(x, (1, 0, 2)).reshape(2, images // 2, slots, width)


def for_route(groups, z, odd):
    return lax.dynamic_index_in_dim(groups, (z ^ odd) & 1, 0, False)


def to_image(send, odd, what):
    n_dp, n_mp = lax.axis_size("dp"), lax.axis_size("mp")
    with jax.named_scope(what + "_route" + str(odd)):
        return lax.ppermute(send, ("dp", "mp"), image_routes(n_dp, n_mp, odd))


def from_image(y, z, odd, what):
    n_dp, n_mp = lax.axis_size("dp"), lax.axis_size("mp")
    routes = [(b, a) for a, b in image_routes(n_dp, n_mp, odd)]
    with jax.named_scope(what + "_route" + str(odd)):
        return lax.ppermute(y[:, odd], ("dp", "mp"), routes)


def joined_images(back, z):
    flip = (z & 1) == 1
    groups = jnp.concatenate([jnp.where(flip, back[1], back[0]), jnp.where(flip, back[0], back[1])])
    return jnp.transpose(groups, (1, 0, 2))


def local(
    tokens,
    counts,
    norm_gains,
    norm_shifts,
    qkv_weight,
    qkv_bias,
    proj_weight,
    out_biases,
    up_weight,
    up_bias,
    down_weight,
    cotangent,
):
    slots, images, width = tokens.shape
    n_dp, n_mp = lax.axis_size("dp"), lax.axis_size("mp")
    n_q = n_dp // 2
    wq = width // n_q
    dp, z = lax.axis_index("dp"), lax.axis_index("mp")
    q, core = dp >> 1, dp & 1
    own_images = images // 2
    all_slots = slots * n_mp
    rows = own_images * all_slots

    def rel(v):
        blocks = [lax.dynamic_slice_in_dim(v, (q ^ j) * wq, wq, v.ndim - 1) for j in range(n_q)]
        return jnp.concatenate(blocks, -1)

    def half_of(v, which, axis):
        size = v.shape[axis] // 2
        return lax.dynamic_slice_in_dim(v, which * size, size, axis)

    att = jnp.concatenate([qkv_weight, jnp.transpose(proj_weight)[None]])
    ffn_w = jnp.stack([up_weight, jnp.transpose(down_weight)])
    he, fh = att.shape[-1] // 2, ffn_w.shape[-1] // 2

    count_rows = jnp.pad(counts.astype(BF)[None], ((0, 15), (0, he - images)))
    sent = jnp.concatenate([half_of(att, 1 - core, 2).reshape(-1, he), count_rows])
    got = swap(sent, "dp", 1, "att_w_core")
    other_counts = got[-16, :images].astype(jnp.int32)
    got = got[:-16].reshape(4, wq // 2, he)
    att_own = ordered_pair(half_of(att, core, 2), got, core, 1).reshape(-1, he)
    got = swap(half_of(ffn_w, 1 - core, 2), "dp", 1, "ffn_w_core")
    ffn_own = ordered_pair(half_of(ffn_w, core, 2), got, core, 1).reshape(2, wq, fh)
    left = jnp.concatenate(
        [half_of(qkv_bias, core, 1), half_of(up_bias, core, 0).reshape(-1, he)]
    )
    n_bias = left.shape[0]
    terms = []
    for _ in range(3):
        term = lax.reduce_precision(left, 8, 7)
        terms.append(term.astype(BF))
        left = left - term
    bias_pad = -(-3 * n_bias // 16) * 16
    bias_terms = jnp.pad(jnp.concatenate(terms), ((0, bias_pad - 3 * n_bias), (0, 0)))

    counts_here = jnp.where((z >> 1) == core, counts, other_counts)
    counts_here = lax.dynamic_slice_in_dim(counts_here, (z & 1) * own_images, own_images, 0)
    meta = jnp.concatenate([counts_here, z[None], q[None]])
    slot_ids = jnp.arange(slots, dtype=jnp.int32)
    keep_mine = ((z * slots + slot_ids)[:, None] < BUF + counts[None, :])[:, :, None]

    def whole_rows(got, what):
        return ordered_pair(got, swap(got, "dp", 1, what), core, 1).reshape(rows, width)

    n_i = n_mp
    gains, shifts, out_b = rel(norm_gains), rel(norm_shifts), rel(out_biases)
    square = n_q == 4
    pair_places = [(j, i, 0, 2, False) for j, i in ((0, 0), (1, 0), (2, 0), (3, 0), (3, 1))]
    both = lax.optimization_barrier

    def flat(v):
        return v.reshape(v.shape[:-3] + (-1, v.shape[-1]))

    row_half = lambda v, which: half_of(v.reshape(own_images, n_mp, slots, width), which, 1)

    att_mine = jnp.concatenate([att_own, bias_terms])
    two = swap(att_mine, "mp", 2, "att_w_z2")
    one = swap(att_mine, "mp", 1, "att_w_z1")
    token_groups = image_groups(rel(tokens))
    sends = [for_route(token_groups, z, odd) for odd in (0, 1)]
    one, two, sends, ffn_own = both((one, two, sends, ffn_own))
    three = swap(two, "mp", 1, "att_w_z3")
    far_one, far_two = swap(ffn_own, "mp", 1, "ffn_w_z1"), swap(ffn_own, "mp", 2, "ffn_w_z2")
    att_z = jnp.stack([att_mine, one, two, three])
    bias_all = att_z[:, 4 * wq : 4 * wq + 3 * n_bias].astype(F32).reshape(n_i, 3, n_bias, he)
    bias_all = bias_all[:, 0] + (bias_all[:, 1] + bias_all[:, 2])
    bias_three = jnp.stack([bias_all[:, 0], jnp.zeros((n_i, he), F32), bias_all[:, 1]])
    bias_rows = jnp.transpose(bias_three.reshape(3, 2, 2, he), (1, 0, 2, 3)).reshape(1, -1)
    att_near = gather_near(att_z, "att_w") if square else ()
    far_one, far_two, sends, bias_rows = both((far_one, far_two, sends, bias_rows))
    far_three = swap(far_two, "mp", 1, "ffn_w_z3")
    token_rows = [to_image(sends[odd], odd, "tokens") for odd in (0, 1)]

    if square:
        att_far = gather_far(*att_near, "att_w")
        att_places = [(j, i, 0, 4, False) for j, i in ((0, 0), (1, 0), (2, 0), (3, 0), (3, 2))]
    else:
        att_far, att_places = (gather_plane(att_z, "att_w"),), [(0, 0, 0, 4, True)]
    cot = rel(jnp.where(keep_mine, cotangent, jnp.zeros_like(cotangent)))
    cot_groups = image_groups(cot)
    sends = [for_route(cot_groups, z, odd) for odd in (0, 1)]
    token_rows, att_far, far_three, sends = both((token_rows, att_far, far_three, sends))
    att_parts = [v[None] for v in (att_z, *att_near, *att_far)] if square else list(att_far)
    x = whole_rows(jnp.stack(token_rows, 1), "tokens_core")
    ffn_far = flat(jnp.stack([far_two, far_three]))
    x, ffn_far, sends = both((x, ffn_far, sends))
    far_near = gather_near(ffn_far, "ffn_w2") if square else ()
    cot_rows = [to_image(sends[odd], odd, "cotangent") for odd in (0, 1)]
    n1, qkva, qkvb, mixa, mixb, part = att_forward(
        x.reshape(own_images, all_slots, width),
        gains[0:1],
        shifts[0:1],
        bias_rows,
        meta,
        att_places,
        att_parts,
    )
    part, n1, x, far_near, cot_rows = both((part, n1, x, far_near, cot_rows))
    part_other = swap(part, "dp", 1, "attended")
    if square:
        far_far = gather_far(*far_near, "ffn_w2")
        parts0 = [v[None] for v in (ffn_far, *far_near, *far_far)]
        places = pair_places
    else:
        parts0, places = [gather_plane(ffn_far, "ffn_w2")], [(0, 0, 0, 2, True)]
    go = whole_rows(jnp.stack(cot_rows, 1), "cotangent_core")
    ffn_here = flat(jnp.stack([ffn_own, far_one]))
    go, parts0, part_other, ffn_here = both((go, parts0, part_other, ffn_here))
    here_near = gather_near(ffn_here, "ffn_w0") if square else ()
    up_rows = bias_all[:, 2:].reshape(n_i, fh)
    hidden, n2, n2t, got, sum_b, sum_g, upg1, *ffn_g0 = ffn_call(
        [x, part, part_other, out_b[0:1], gains[1:2], shifts[1:2], go, up_rows[2:], meta],
        n_q,
        2,
        fh,
        places,
        parts0,
        True,
        not square,
    )
    n2, ffn_g0, here_near = both((n2, ffn_g0, here_near))
    if square:
        parts1 = [v[None] for v in (ffn_here, *here_near, *gather_far(*here_near, "ffn_w0"))]
    else:
        parts1 = [gather_plane(ffn_here, "ffn_w0")]
    n2, parts1, ffn_g0 = both((n2, parts1, ffn_g0))
    reach_f0 = scatter_reach(ffn_g0, "ffn_g0")
    branch, gn2, upg0, *ffn_g1 = ffn_call(
        [n2, n2t, got, sum_b, sum_g, go, up_rows[:2], meta],
        n_q,
        2,
        fh,
        places,
        parts1,
        False,
        not square,
    )
    branch, gn2, ffn_g1, reach_f0 = both((branch, gn2, ffn_g1, reach_f0))

    last_f0 = scatter_last(ffn_g0, reach_f0, "ffn_g0")
    reach_f1 = scatter_reach(ffn_g1, "ffn_g1")
    gn2_other = swap(gn2, "dp", 1, "grad_norm_two")
    theirs = swap(row_half(branch, 1 - core), "dp", 1, "branch")
    gn2_other, theirs = both((gn2_other, theirs))
    out_half = row_half(hidden, core) + row_half(branch, core).astype(F32) + theirs.astype(F32) + out_b[1]
    gn2_other, out_half = both((gn2_other, rel(out_half.astype(BF))))
    out_first = from_image(out_half, z, 0, "block_out")
    gh, ght, gmixa, gmixb, sums = hidden_backward(
        meta, hidden, gn2, gn2_other, gains[1:2], go, n_q, att_places, att_parts
    )
    gmixa, last_f0, out_first, out_half = both((gmixa, last_f0, out_first, out_half))
    ffn2, ffn3 = scatter_sum(ffn_g0, reach_f0, last_f0)
    ffn_three = swap(ffn3, "mp", 1, "ffn_g_z3")
    out_last = from_image(out_half, z, 1, "block_out")
    gmixa, ffn2 = both((gmixa, ffn2))
    n1t, gqa, bias_a, *att_g = att_backward_first(
        meta, gmixa, ght, n1, qkva, mixa, n_q, not square
    )
    n1t, gqa, reach_f1, ffn_three, out_last = both((n1t, gqa, reach_f1, ffn_three, out_last))
    last_f1 = scatter_last(ffn_g1, reach_f1, "ffn_g1")
    ffn_two = swap(add(ffn2, ffn_three), "mp", 2, "ffn_g_z2")
    gn1, bias_b, more_sums, *att_g = att_backward_last(
        meta, x, gmixb, ght, n1t, gqa, qkvb, mixb, n_q, att_places, att_parts, att_g
    )
    gn1, last_f1, att_g, x, ffn_two = both((gn1, last_f1, att_g, x, ffn_two))

    ffn0, ffn1 = scatter_sum(ffn_g1, reach_f1, last_f1)
    ffn_one = swap(ffn1, "mp", 1, "ffn_g_z1")
    gn1_other = swap(after(row_half(gn1, 1 - core), ffn1), "dp", 1, "grad_norm_one")
    reach_a = scatter_reach(att_g, "att_g")
    gn1 = row_half(gn1, core).astype(F32) + gn1_other.astype(F32)
    hat1, inv1 = normalise(after(row_half(x, core), gn1_other).astype(F32))
    input_half = row_half(gh, core) + norm_back(hat1, inv1, gains[0], gn1)
    input_half = rel(input_half.astype(BF))
    in_first = from_image(input_half, z, 0, "input_grad")
    reach_a, ffn_one, in_first, input_half, upg0, upg1, bias_a, bias_b, sums, more_sums = both(
        (reach_a, ffn_one, in_first, input_half, upg0, upg1, bias_a, bias_b, sums, more_sums)
    )
    in_last = from_image(input_half, z, 1, "input_grad")
    last_a = scatter_last(att_g, reach_a, "att_g")

    def placed(values):
        mine = jnp.concatenate([lax.dynamic_slice_in_dim(values, z ^ i, 1, 0) for i in range(n_i)])
        return jnp.stack([jnp.where(core == c, mine, jnp.zeros_like(mine)) for c in range(2)], 1)

    bias_a, bias_b = (v.reshape(3, 2, he) for v in (bias_a, bias_b))
    wide = [placed(jnp.concatenate([bias_a[t], bias_b[t]])) for t in (0, 2)]
    wide.append(placed(jnp.concatenate([upg0, upg1])))
    values = [*wide, rel(sums), rel(more_sums)]
    vector = jnp.concatenate([v.reshape(-1, 128) for v in values])
    vector = vector + swap(vector, "dp", 1, "sums_core")
    last_a, vector = both((last_a, vector))
    att0, att1, att2, att3 = scatter_sum(att_g, reach_a, last_a)
    att_three = swap(att3, "mp", 1, "att_g_z3")
    att_one = swap(att1, "mp", 1, "att_g_z1")
    vector = vector + swap(vector, "dp", 2, "sums_dp2")
    att_three, vector = both((att_three, vector))
    att_two = swap(add(att2, att_three), "mp", 2, "att_g_z2")
    bit = 4
    while bit < n_dp:
        vector = vector + swap(vector, "dp", bit, "sums_dp" + str(bit))
        bit *= 2
    for bit in (1, 2):
        vector = vector + swap(vector, "mp", bit, "sums_z" + str(bit))
    att_grad = add(att0, att_one, att_two)
    ffn_grad = add(ffn0, ffn_one, ffn_two)
    in_routes = [in_first, in_last]
    block_out = joined_images([out_first, out_last], z)
    block_out = jnp.where(keep_mine, block_out, jnp.zeros_like(block_out))
    input_grad = joined_images(in_routes, z)

    def own_shard(grad, what):
        kinds, _, last = grad.shape
        pair = grad.reshape(kinds, 2, wq // 2, last)
        keep = lax.dynamic_index_in_dim(pair, core, 1, False)
        got = swap(lax.dynamic_index_in_dim(pair, 1 - core, 1, False), "dp", 1, what)
        return ordered_pair(keep, got, core, 2).reshape(kinds, wq // 2, 2 * last).astype(F32)

    att_shard, ffn_shard = own_shard(att_grad, "att_g_core"), own_shard(ffn_grad, "ffn_g_core")
    qkv_owned, proj_owned = att_shard[:3], jnp.transpose(att_shard[3])
    up_owned, down_owned = ffn_shard[0], jnp.transpose(ffn_shard[1])

    ends = [0]
    for v in values:
        ends.append(ends[-1] + v.size // 128)
    *wide, sums, more_sums = [
        vector[start:end].reshape(v.shape) for v, start, end in zip(values, ends, ends[1:])
    ]
    wide = [lax.dynamic_index_in_dim(v, z, 0, False).reshape(-1) for v in wide]
    bias_grad, upbias_grad = jnp.stack(wide[:2]), wide[2]
    gains_grad = jnp.stack([more_sums[0], sums[0] * 0.5])
    shifts_grad = jnp.stack([more_sums[1], sums[1] * 0.5])
    outbias_grad = sums[2:4] * 0.5
    return (
        block_out,
        input_grad,
        gains_grad,
        shifts_grad,
        qkv_owned,
        bias_grad,
        proj_owned,
        outbias_grad,
        up_owned,
        upbias_grad,
        down_owned,
    )


def solution(mesh):
    split = P("mp", "dp", None)
    return jax.shard_map(
        local,
        mesh=mesh,
        in_specs=(
            split,
            P("dp"),
            P(),
            P(),
            P(None, "dp", "mp"),
            P(None, "mp"),
            P("mp", "dp"),
            P(),
            P("dp", "mp"),
            P("mp"),
            P("mp", "dp"),
            split,
        ),
        out_specs=(
            split,
            split,
            P(),
            P(),
            P(None, "dp", "mp"),
            P(None, "mp"),
            P("mp", "dp"),
            P(),
            P("dp", "mp"),
            P("mp"),
            P("mp", "dp"),
        ),
        check_vma=False,
    )
```

profile of v0, /device:TPU:0, one launch (start us, length us, event | category | flops | bytes accessed | tf_op | source)
XLA Modules:
  0.0 367.0 jit_solution(15976737045868045541)
XLA Ops:
  7.7 3.1 collective-permute-start.1
  10.7 2.6 collective-permute-start.2
  14.3 8.8 %collective-permute-done.1 = bf16[1056,128]{1,0:T(8,128)(2,1)S(1)} collective-permute-done((bf16[1056,128]{1,0:T(8,128)(2,1)S(1)}, bf16[1056,128]{1,0:T(8,128)(2,1)S(1)}, u32[]{:S(2)}, u32[]{:S(2)}) %collective-permute-start.1) | collective-permute-done | bytes 270368 | tf_op jit(solution)/shard_map/att_w_z1/ppermute | solution.py:590
  23.1 2.5 collective-permute-done.2
  26.2 5.9 %collective-permute-done.6 = bf16[1056,128]{1,0:T(8,128)(2,1)S(1)} collective-permute-done((bf16[1056,128]{1,0:T(8,128)(2,1)S(1)}, bf16[1056,128]{1,0:T(8,128)(2,1)S(1)}, u32[]{:S(2)}, u32[]{:S(2)}) %collective-permute-start.6) | collective-permute-done | bytes 270368 | tf_op jit(solution)/shard_map/att_w_z3/ppermute | solution.py:590
  32.3 1.6 collective-permute-start.9
  35.5 1.6 collective-permute-start.4
  37.0 2.4 collective-permute-start.5
  39.5 18.1 %collective-permute-done.4 = bf16[2,256,512]{2,1,0:T(8,128)(2,1)S(1)} collective-permute-done((bf16[2,256,512]{2,1,0:T(8,128)(2,1)S(1)}, bf16[2,256,512]{2,1,0:T(8,128)(2,1)S(1)}, u32[]{:S(2)}, u32[]{:S(2)}) %collective-permute-start.4) | collective-permute-done | bytes 524320 | tf_op jit(solution)/shard_map/ffn_w_z1/ppermute | solution.py:590
  57.6 3.0 collective-permute-done.5
  60.6 1.7 collective-permute-start.7
  62.3 2.0 collective-permute-start.8
  66.1 17.5 %collective-permute-done.8 = bf16[3,80,1024]{2,1,0:T(8,128)(2,1)S(1)} collective-permute-done((bf16[3,80,1024]{2,1,0:T(8,128)(2,1)}, bf16[3,80,1024]{2,1,0:T(8,128)(2,1)S(1)}, u32[]{:S(2)}, u32[]{:S(2)}) %collective-permute-start.8) | collective-permute-done | bytes 491552 | tf_op jit(solution)/shard_map/tokens_route1/ppermute | solution.py:698
  83.7 3.5 collective-permute-start.14
  92.8 1.6 collective-permute-start.18
  94.4 19.8 %att_forward.1 = (bf16[960,1024]{1,0:T(8,128)(2,1)}, bf16[6,960,128]{2,1,0:T(8,128)(2,1)}, bf16[6,960,128]{2,1,0:T(8,128)(2,1)}, bf16[960,256]{1,0:T(8,128)(2,1)...) custom-call(bf16[3,320,1024]{2,1,0:T(8,128)(2,1)} %bitcast.249, f32[1,1024]{1,0:T(1,128)S(1)} %get-tuple-element.419.g_ref, ...), custom_call_target="tpu_custom_call" | custom-call | flops 16000000000 | bytes 20000000 | tf_op jit(solution)/shard_map/att_forward/pallas_call | solution.py:179
  114.2 2.3 collective-permute-done.15
  118.8 1.6 collective-permute-start.20
  120.5 1.5 collective-permute-start.21
  124.1 9.2 %collective-permute-done.20 = bf16[1,512,512]{2,1,0:T(8,128)(2,1)S(1)} collective-permute-done((bf16[1,512,512]{2,1,0:T(8,128)(2,1)S(1)}, bf16[1,512,512]{2,1,0:T(8,128)(2,1)S(1)}, u32[]{:S(2)}, u32[]{:S(2)}) %collective-permute-start.20) | collective-permute-done | bytes 524320 | tf_op jit(solution)/shard_map/ffn_w2_y2/ppermute | solution.py:590
  136.8 23.0 %ffn_first.1 = (f32[960,1024]{1,0:T(8,128)}, bf16[960,1024]{1,0:T(8,128)(2,1)}, bf16[1024,960]{1,0:T(8,128)(2,1)}, bf16[1024,960]{1,0:T(8,128)(2,1)}, f32[960,10...) custom-call(bf16[960,1024]{1,0:T(8,128)(2,1)} %bitcast.250, ...), custom_call_target="tpu_custom_call" | custom-call | flops 24000000000 | bytes 30000000 | tf_op jit(solution)/shard_map/ffn_first/pallas_call | solution.py:350
  162.1 10.8 %collective-permute-done.25 = bf16[1,512,512]{2,1,0:T(8,128)(2,1)S(1)} collective-permute-done((bf16[1,512,512]{2,1,0:T(8,128)(2,1)S(1)}, bf16[1,512,512]{2,1,0:T(8,128)(2,1)S(1)}, u32[]{:S(2)}, u32[]{:S(2)}) %collective-permute-start.25) | collective-permute-done | bytes 524320 | tf_op jit(solution)/shard_map/ffn_w0_y2/ppermute | solution.py:590
  176.0 22.3 %ffn_last.1 = (bf16[960,1024]{1,0:T(8,128)(2,1)}, bf16[960,1024]{1,0:T(8,128)(2,1)}, f32[2,512]{1,0:T(2,128)}, bf16[2,2,256,512]{3,2,1,0:T(8,128)(2,1)}, bf16[2,...) custom-call(bf16[960,1024]{1,0:T(8,128)(2,1)} %get-tuple-element.219, ...), custom_call_target="tpu_custom_call" | custom-call | flops 24000000000 | bytes 30000000 | tf_op jit(solution)/shard_map/ffn_last/pallas_call | solution.py:350
  198.4 1.7 constant_dynamic-slice_fusion.36
  201.1 1.7 add_convert_fusion.9
  204.8 1.5 collective-permute-start.31
  210.1 11.4 %hidden_backward.1 = (f32[960,1024]{1,0:T(8,128)}, bf16[1024,960]{1,0:T(8,128)(2,1)}, bf16[2,960,128]{2,1,0:T(8,128)(2,1)S(1)}, bf16[2,960,128]{2,1,0:T(8,128)(2,1)S(1)}, f32[8,1024]{1,0:T(8,128)S(1)}) custom-call(s32[5]{0:T(128)S(1)} %copy-done.7, f32[960,1024]{1,0:T(8,128)} %get-tuple-element.203.hid_ref, bf16[960,1024]{1,0:T(8,128)(2,1)} %get-tuple-element.238.ga_ref, ...), custom_call_target="tpu_custom_call" | custom-call | flops 10000000000 | bytes 20000000 | tf_op jit(solution)/shard_map/hidden_backward/pallas_call | solution.py:462
  221.7 2.2 fusion.18
  223.9 1.7 collective-permute-start.36
  226.5 15.9 %att_backward_first.1 = (bf16[1024,960]{1,0:T(8,128)(2,1)}, bf16[960,768]{1,0:T(8,128)(2,1)}, f32[1,768]{1,0:T(1,128)}, bf16[4,4,256,128]{3,2,1,0:T(8,128)(2,1)}...) custom-call(s32[5]{0:T(128)} %copy-done.6, ...), custom_call_target="tpu_custom_call" | custom-call | flops 16000000000 | bytes 20000000 | tf_op jit(solution)/shard_map/att_backward_first/pallas_call | solution.py:505
  242.5 5.8 %collective-permute-done.37 = bf16[3,80,1024]{2,1,0:T(8,128)(2,1)S(1)} collective-permute-done((bf16[3,80,1024]{2,1,0:T(8,128)(2,1)S(1)}, bf16[3,80,1024]{2,1,0:T(8,128)(2,1)S(1)}, u32[]{:S(2)}, u32[]{:S(2)}) %collective-permute-start.37) | collective-permute-done | bytes 491552 | tf_op jit(solution)/shard_map/block_out_route1/ppermute | solution.py:705
  249.2 1.6 collective-permute-start.40
  254.0 1.6 collective-permute-start.38
  255.6 19.3 %att_backward_last.1 = (bf16[960,1024]{1,0:T(8,128)(2,1)}, f32[1,768]{1,0:T(1,128)}, f32[8,1024]{1,0:T(8,128)}, bf16[4,4,256,128]{3,2,1,0:T(8,128)(2,1)}, bf16[4...) custom-call(s32[5]{0:T(128)} %copy-done.6, ...), custom_call_target="tpu_custom_call", output_to_operand_aliasing={{3}: (13, {}), {4}: (14, {}), {5}: (15, {}), {6}: (16, {}),... | custom-call | flops 20000000000 | bytes 30000000 | tf_op jit(solution)/shard_map/att_backward_last/pallas_call | solution.py:563
  276.0 2.1 constant_dynamic-slice_fusion.30
  279.7 2.1 fusion.19
  281.9 2.2 collective-permute-start.43
  287.9 2.3 fusion.13
  290.2 2.1 fusion.8
  294.9 2.0 collective-permute-done.43
  296.9 13.7 %collective-permute-done.41 = bf16[4,4,256,128]{3,2,1,0:T(8,128)(2,1)S(1)} collective-permute-done((bf16[4,4,256,128]{3,2,1,0:T(8,128)(2,1)S(1)}, bf16[4,4,256,128]{3,2,1,0:T(8,128)(2,1)S(1)}, u32[]{:S(2)}, u32[]{:S(2)}) %collective-permute-start.41) | collective-permute-done | bytes 1048608 | tf_op jit(solution)/shard_map/att_g_x1/ppermute | solution.py:590
  311.0 1.9 fusion.15
  320.6 9.4 %collective-permute-done.48 = bf16[2,4,256,128]{3,2,1,0:T(8,128)(2,1)S(1)} collective-permute-done((bf16[2,4,256,128]{3,2,1,0:T(8,128)(2,1)S(1)}, bf16[2,4,256,128]{3,2,1,0:T(8,128)(2,1)S(1)}, u32[]{:S(2)}, u32[]{:S(2)}) %collective-permute-start.48) | collective-permute-done | bytes 524320 | tf_op jit(solution)/shard_map/att_g_y2/ppermute | solution.py:590
  336.3 1.7 collective-permute-start.55
  339.0 4.3 %collective-permute-done.50 = bf16[4,256,128]{2,1,0:T(8,128)(2,1)} collective-permute-done((bf16[4,256,128]{2,1,0:T(8,128)(2,1)}, bf16[4,256,128]{2,1,0:T(8,128)(2,1)}, u32[]{:S(2)}, u32[]{:S(2)}) %collective-permute-start.50) | collective-permute-done | bytes 262176 | tf_op jit(solution)/shard_map/att_g_z3/ppermute | solution.py:590
  348.1 2.1 collective-permute-done.52
  351.4 5.1 %collective-permute-done.53 = f32[176,128]{1,0:T(8,128)S(1)} collective-permute-done((f32[176,128]{1,0:T(8,128)S(1)}, f32[176,128]{1,0:T(8,128)S(1)}, u32[]{:S(2)}, u32[]{:S(2)}) %collective-permute-start.53) | collective-permute-done | bytes 90144 | tf_op jit(solution)/shard_map/sums_z1/ppermute | solution.py:590
  357.7 4.3 %collective-permute-done.54 = f32[176,128]{1,0:T(8,128)S(1)} collective-permute-done((f32[176,128]{1,0:T(8,128)S(1)}, f32[176,128]{1,0:T(8,128)S(1)}, u32[]{:S(2)}, u32[]{:S(2)}) %collective-permute-start.54) | collective-permute-done | bytes 90144 | tf_op jit(solution)/shard_map/sums_z2/ppermute | solution.py:590
  (381 shorter events, 78.4 us)
Async XLA Ops:
  5.9 7.5 %collective-permute-start.3 = (bf16[2,128,512]{2,1,0:T(8,128)(2,1)S(1)}, bf16[2,128,512]{2,1,0:T(8,128)(2,1)S(1)}, u32[]{:S(2)}, u32[]{:S(2)}) collective-permute-start(bf16[2,128,512]{2,1,0:T(8,128)(2,1)S(1)} %fusion.29), channel_id=1, source_target_pairs={{0,4},{4,0},{8,12},{12,8},{16,20},{20,16},{24,28},{28,24},{1,5},{5... | collective-permute-start | bytes 786440 | tf_op jit(solution)/shard_map/ffn_w_core/ppermute | solution.py:590
  7.7 15.5 %collective-permute-start.1 = (bf16[1056,128]{1,0:T(8,128)(2,1)S(1)}, bf16[1056,128]{1,0:T(8,128)(2,1)S(1)}, u32[]{:S(2)}, u32[]{:S(2)}) collective-permute-start(bf16[1056,128]{1,0:T(8,128)(2,1)S(1)} %get-tuple-element.391), channel_id=1, source_target_pairs={{0,1},{1,0},{2,3},{3,2},{4,5},{5,4},{6,7},{7,6},{8,9},{9,8},{10,11... | collective-permute-start | bytes 811016 | tf_op jit(solution)/shard_map/att_w_z1/ppermute | solution.py:590
  10.7 14.9 %collective-permute-start.2 = (bf16[1056,128]{1,0:T(8,128)(2,1)S(1)}, bf16[1056,128]{1,0:T(8,128)(2,1)S(1)}, u32[]{:S(2)}, u32[]{:S(2)}) collective-permute-start(bf16[1056,128]{1,0:T(8,128)(2,1)S(1)} %get-tuple-element.391), channel_id=1, source_target_pairs={{0,2},{1,3},{2,0},{3,1},{4,6},{5,7},{6,4},{7,5},{8,10},{9,11},{10,... | collective-permute-start | bytes 811016 | tf_op jit(solution)/shard_map/att_w_z2/ppermute | solution.py:590
  25.7 6.5 %collective-permute-start.6 = (bf16[1056,128]{1,0:T(8,128)(2,1)S(1)}, bf16[1056,128]{1,0:T(8,128)(2,1)S(1)}, u32[]{:S(2)}, u32[]{:S(2)}) collective-permute-start(bf16[1056,128]{1,0:T(8,128)(2,1)S(1)} %collective-permute-done.2), channel_id=1, source_target_pairs={{0,1},{1,0},{2,3},{3,2},{4,5},{5,4},{6,7},{7,6},{8,9},{9,8},{10,11... | collective-permute-start | bytes 811016 | tf_op jit(solution)/shard_map/att_w_z3/ppermute | solution.py:590
  32.3 31.9 %collective-permute-start.9 = (bf16[4,1056,128]{2,1,0:T(8,128)(2,1)S(1)}, bf16[4,1056,128]{2,1,0:T(8,128)(2,1)S(1)}, u32[]{:S(2)}, u32[]{:S(2)}) collective-permute-start(bf16[4,1056,128]{2,1,0:T(8,128)(2,1)S(1)} %get-tuple-element.353), channel_id=1, source_target_pairs={{0,8},{4,12},{8,0},{12,4},{16,24},{20,28},{24,16},{28,20},{1,9},{5... | collective-permute-start | bytes 3244040 | tf_op jit(solution)/shard_map/att_w_x1/ppermute | solution.py:590
  33.9 31.0 %collective-permute-start.11 = (bf16[4,1056,128]{2,1,0:T(8,128)(2,1)S(1)}, bf16[4,1056,128]{2,1,0:T(8,128)(2,1)S(1)}, u32[]{:S(2)}, u32[]{:S(2)}) collective-permute-start(bf16[4,1056,128]{2,1,0:T(8,128)(2,1)S(1)} %get-tuple-element.353), channel_id=1, source_target_pairs={{0,16},{4,20},{8,24},{12,28},{16,0},{20,4},{24,8},{28,12},{1,17},{... | collective-permute-start | bytes 3244040 | tf_op jit(solution)/shard_map/att_w_y1/ppermute | solution.py:590
  35.5 22.1 %collective-permute-start.4 = (bf16[2,256,512]{2,1,0:T(8,128)(2,1)S(1)}, bf16[2,256,512]{2,1,0:T(8,128)(2,1)S(1)}, u32[]{:S(2)}, u32[]{:S(2)}) collective-permute-start(bf16[2,256,512]{2,1,0:T(8,128)(2,1)S(1)} %bitcast.260), channel_id=1, source_target_pairs={{0,1},{1,0},{2,3},{3,2},{4,5},{5,4},{6,7},{7,6},{8,9},{9,8},{10,11... | collective-permute-start | bytes 1572872 | tf_op jit(solution)/shard_map/ffn_w_z1/ppermute | solution.py:590
  37.0 23.5 %collective-permute-start.5 = (bf16[2,256,512]{2,1,0:T(8,128)(2,1)S(1)}, bf16[2,256,512]{2,1,0:T(8,128)(2,1)S(1)}, u32[]{:S(2)}, u32[]{:S(2)}) collective-permute-start(bf16[2,256,512]{2,1,0:T(8,128)(2,1)S(1)} %bitcast.261), channel_id=1, source_target_pairs={{0,2},{1,3},{2,0},{3,1},{4,6},{5,7},{6,4},{7,5},{8,10},{9,11},{10,... | collective-permute-start | bytes 1572872 | tf_op jit(solution)/shard_map/ffn_w_z2/ppermute | solution.py:590
  60.6 23.0 %collective-permute-start.13 = (bf16[2,256,512]{2,1,0:T(8,128)(2,1)S(1)}, bf16[2,256,512]{2,1,0:T(8,128)(2,1)S(1)}, u32[]{:S(2)}, u32[]{:S(2)}) collective-permute-start(bf16[2,256,512]{2,1,0:T(8,128)(2,1)S(1)} %collective-permute-done.5), channel_id=1, source_target_pairs={{0,1},{1,0},{2,3},{3,2},{4,5},{5,4},{6,7},{7,6},{8,9},{9,8},{10,11... | collective-permute-start | bytes 1572872 | tf_op jit(solution)/shard_map/ffn_w_z3/ppermute | solution.py:590
  62.3 21.3 %collective-permute-start.8 = (bf16[3,80,1024]{2,1,0:T(8,128)(2,1)}, bf16[3,80,1024]{2,1,0:T(8,128)(2,1)S(1)}, u32[]{:S(2)}, u32[]{:S(2)}) collective-permute-start(bf16[3,80,1024]{2,1,0:T(8,128)(2,1)} %get-tuple-element.173), channel_id=1, source_target_pairs={{1,0},{0,1},{7,2},{6,3},{3,4},{2,5},{5,6},{4,7},{9,8},{8,9},{15,10... | collective-permute-start | bytes 1474568 | tf_op jit(solution)/shard_map/tokens_route1/ppermute | solution.py:698
  64.3 19.3 %collective-permute-start.10 = (bf16[2,1056,128]{2,1,0:T(8,128)(2,1)S(1)}, bf16[2,1056,128]{2,1,0:T(8,128)(2,1)S(1)}, u32[]{:S(2)}, u32[]{:S(2)}) collective-permute-start(bf16[2,1056,128]{2,1,0:T(8,128)(2,1)S(1)} %slice.326), channel_id=1, source_target_pairs={{0,16},{4,20},{8,24},{12,28},{16,0},{20,4},{24,8},{28,12},{1,17},{... | collective-permute-start | bytes 1622024 | tf_op jit(solution)/shard_map/att_w_y2/ppermute | solution.py:590
  64.9 18.7 %collective-permute-start.12 = (bf16[2,1056,128]{2,1,0:T(8,128)(2,1)S(1)}, bf16[2,1056,128]{2,1,0:T(8,128)(2,1)S(1)}, u32[]{:S(2)}, u32[]{:S(2)}) collective-permute-start(bf16[2,1056,128]{2,1,0:T(8,128)(2,1)S(1)} %slice.327), channel_id=1, source_target_pairs={{0,8},{4,12},{8,0},{12,4},{16,24},{20,28},{24,16},{28,20},{1,9},{5... | collective-permute-start | bytes 1622024 | tf_op jit(solution)/shard_map/att_w_x2/ppermute | solution.py:590
  91.0 25.4 %collective-permute-start.15 = (bf16[2,512,512]{2,1,0:T(8,128)(2,1)S(1)}, bf16[2,512,512]{2,1,0:T(8,128)(2,1)S(1)}, u32[]{:S(2)}, u32[]{:S(2)}) collective-permute-start(bf16[2,512,512]{2,1,0:T(8,128)(2,1)S(1)} %pad_maximum_fusion.3), channel_id=1, source_target_pairs={{0,8},{4,12},{8,0},{12,4},{16,24},{20,28},{24,16},{28,20},{1,9},{5... | collective-permute-start | bytes 3145736 | tf_op jit(solution)/shard_map/ffn_w2_x1/ppermute | solution.py:590
  91.6 25.1 %collective-permute-start.16 = (bf16[2,512,512]{2,1,0:T(8,128)(2,1)S(1)}, bf16[2,512,512]{2,1,0:T(8,128)(2,1)S(1)}, u32[]{:S(2)}, u32[]{:S(2)}) collective-permute-start(bf16[2,512,512]{2,1,0:T(8,128)(2,1)S(1)} %pad_maximum_fusion.3), channel_id=1, source_target_pairs={{0,16},{4,20},{8,24},{12,28},{16,0},{20,4},{24,8},{28,12},{1,17},{... | collective-permute-start | bytes 3145736 | tf_op jit(solution)/shard_map/ffn_w2_y1/ppermute | solution.py:590
  92.1 22.1 %collective-permute-start.17 = (bf16[3,80,1024]{2,1,0:T(8,128)(2,1)S(1)}, bf16[3,80,1024]{2,1,0:T(8,128)(2,1)S(1)}, u32[]{:S(2)}, u32[]{:S(2)}) collective-permute-start(bf16[3,80,1024]{2,1,0:T(8,128)(2,1)S(1)} %get-tuple-element.187), channel_id=1, source_target_pairs={{0,0},{1,1},{6,2},{7,3},{2,4},{3,5},{4,6},{5,7},{8,8},{9,9},{14,10... | collective-permute-start | bytes 1474568 | tf_op jit(solution)/shard_map/cotangent_route0/ppermute | solution.py:698
  92.8 21.4 %collective-permute-start.18 = (bf16[3,80,1024]{2,1,0:T(8,128)(2,1)S(1)}, bf16[3,80,1024]{2,1,0:T(8,128)(2,1)S(1)}, u32[]{:S(2)}, u32[]{:S(2)}) collective-permute-start(bf16[3,80,1024]{2,1,0:T(8,128)(2,1)S(1)} %get-tuple-element.188), channel_id=1, source_target_pairs={{1,0},{0,1},{7,2},{6,3},{3,4},{2,5},{5,6},{4,7},{9,8},{8,9},{15,10... | collective-permute-start | bytes 1474568 | tf_op jit(solution)/shard_map/cotangent_route1/ppermute | solution.py:698
  116.7 18.0 %collective-permute-start.22 = (bf16[960,1024]{1,0:T(8,128)(2,1)}, bf16[960,1024]{1,0:T(8,128)(2,1)S(1)}, u32[]{:S(2)}, u32[]{:S(2)}) collective-permute-start(bf16[960,1024]{1,0:T(8,128)(2,1)} %get-tuple-element.190.refs_1_), channel_id=1, source_target_pairs={{0,4},{4,0},{8,12},{12,8},{16,20},{20,16},{24,28},{28,24},{1,5},{5... | collective-permute-start | bytes 5898248 | tf_op jit(solution)/shard_map/attended/ppermute | solution.py:590
  118.8 14.5 %collective-permute-start.20 = (bf16[1,512,512]{2,1,0:T(8,128)(2,1)S(1)}, bf16[1,512,512]{2,1,0:T(8,128)(2,1)S(1)}, u32[]{:S(2)}, u32[]{:S(2)}) collective-permute-start(bf16[1,512,512]{2,1,0:T(8,128)(2,1)S(1)} %slice.257), channel_id=1, source_target_pairs={{0,16},{4,20},{8,24},{12,28},{16,0},{20,4},{24,8},{28,12},{1,17},{... | collective-permute-start | bytes 1572872 | tf_op jit(solution)/shard_map/ffn_w2_y2/ppermute | solution.py:590
  120.5 14.2 %collective-permute-start.21 = (bf16[1,512,512]{2,1,0:T(8,128)(2,1)S(1)}, bf16[1,512,512]{2,1,0:T(8,128)(2,1)S(1)}, u32[]{:S(2)}, u32[]{:S(2)}) collective-permute-start(bf16[1,512,512]{2,1,0:T(8,128)(2,1)S(1)} %slice.258), channel_id=1, source_target_pairs={{0,8},{4,12},{8,0},{12,4},{16,24},{20,28},{24,16},{28,20},{1,9},{5... | collective-permute-start | bytes 1572872 | tf_op jit(solution)/shard_map/ffn_w2_x2/ppermute | solution.py:590
  134.8 25.0 %collective-permute-start.23 = (bf16[2,512,512]{2,1,0:T(8,128)(2,1)S(1)}, bf16[2,512,512]{2,1,0:T(8,128)(2,1)S(1)}, u32[]{:S(2)}, u32[]{:S(2)}) collective-permute-start(bf16[2,512,512]{2,1,0:T(8,128)(2,1)S(1)} %pad_maximum_fusion.4), channel_id=1, source_target_pairs={{0,8},{4,12},{8,0},{12,4},{16,24},{20,28},{24,16},{28,20},{1,9},{5... | collective-permute-start | bytes 3145736 | tf_op jit(solution)/shard_map/ffn_w0_x1/ppermute | solution.py:590
  136.3 24.3 %collective-permute-start.24 = (bf16[2,512,512]{2,1,0:T(8,128)(2,1)S(1)}, bf16[2,512,512]{2,1,0:T(8,128)(2,1)S(1)}, u32[]{:S(2)}, u32[]{:S(2)}) collective-permute-start(bf16[2,512,512]{2,1,0:T(8,128)(2,1)S(1)} %pad_maximum_fusion.4), channel_id=1, source_target_pairs={{0,16},{4,20},{8,24},{12,28},{16,0},{20,4},{24,8},{28,12},{1,17},{... | collective-permute-start | bytes 3145736 | tf_op jit(solution)/shard_map/ffn_w0_y1/ppermute | solution.py:590
  160.7 12.2 %collective-permute-start.25 = (bf16[1,512,512]{2,1,0:T(8,128)(2,1)S(1)}, bf16[1,512,512]{2,1,0:T(8,128)(2,1)S(1)}, u32[]{:S(2)}, u32[]{:S(2)}) collective-permute-start(bf16[1,512,512]{2,1,0:T(8,128)(2,1)S(1)} %slice.264), channel_id=1, source_target_pairs={{0,16},{4,20},{8,24},{12,28},{16,0},{20,4},{24,8},{28,12},{1,17},{... | collective-permute-start | bytes 1572872 | tf_op jit(solution)/shard_map/ffn_w0_y2/ppermute | solution.py:590
  161.5 12.6 %collective-permute-start.26 = (bf16[1,512,512]{2,1,0:T(8,128)(2,1)S(1)}, bf16[1,512,512]{2,1,0:T(8,128)(2,1)S(1)}, u32[]{:S(2)}, u32[]{:S(2)}) collective-permute-start(bf16[1,512,512]{2,1,0:T(8,128)(2,1)S(1)} %slice.265), channel_id=1, source_target_pairs={{0,8},{4,12},{8,0},{12,4},{16,24},{20,28},{24,16},{28,20},{1,9},{5... | collective-permute-start | bytes 1572872 | tf_op jit(solution)/shard_map/ffn_w0_x2/ppermute | solution.py:590
  174.1 24.2 %collective-permute-start.27 = (bf16[2,2,256,512]{3,2,1,0:T(8,128)(2,1)}, bf16[2,2,256,512]{3,2,1,0:T(8,128)(2,1)}, u32[]{:S(2)}, u32[]{:S(2)}) collective-permute-start(bf16[2,2,256,512]{3,2,1,0:T(8,128)(2,1)} %get-tuple-element.236), channel_id=1, source_target_pairs={{0,8},{4,12},{8,0},{12,4},{16,24},{20,28},{24,16},{28,20},{1,9},{5... | collective-permute-start | bytes 3145736 | tf_op jit(solution)/shard_map/ffn_g0_x1/ppermute | solution.py:590
  174.6 23.7 %collective-permute-start.28 = (bf16[2,2,256,512]{3,2,1,0:T(8,128)(2,1)S(1)}, bf16[2,2,256,512]{3,2,1,0:T(8,128)(2,1)}, u32[]{:S(2)}, u32[]{:S(2)}) collective-permute-start(bf16[2,2,256,512]{3,2,1,0:T(8,128)(2,1)S(1)} %copy-done.67), channel_id=1, source_target_pairs={{0,16},{4,20},{8,24},{12,28},{16,0},{20,4},{24,8},{28,12},{1,17},{... | collective-permute-start | bytes 3145736 | tf_op jit(solution)/shard_map/ffn_g0_y1/ppermute | solution.py:590
  198.3 9.9 %collective-permute-start.29 = (bf16[960,1024]{1,0:T(8,128)(2,1)}, bf16[960,1024]{1,0:T(8,128)(2,1)}, u32[]{:S(2)}, u32[]{:S(2)}) collective-permute-start(bf16[960,1024]{1,0:T(8,128)(2,1)} %get-tuple-element.238.ga_ref), channel_id=1, source_target_pairs={{0,4},{4,0},{8,12},{12,8},{16,20},{20,16},{24,28},{28,24},{1,5},{5... | collective-permute-start | bytes 5898248 | tf_op jit(solution)/shard_map/grad_norm_two/ppermute | solution.py:590
  200.2 6.6 %collective-permute-start.30 = (bf16[3,2,80,1024]{3,2,0,1:T(8,128)(2,1)S(1)}, bf16[3,2,80,1024]{3,2,0,1:T(8,128)(2,1)S(1)}, u32[]{:S(2)}, u32[]{:S(2)}) collective-permute-start(bf16[3,2,80,1024]{3,2,0,1:T(8,128)(2,1)S(1)} %copy.86), channel_id=1, source_target_pairs={{0,4},{4,0},{8,12},{12,8},{16,20},{20,16},{24,28},{28,24},{1,5},{5... | collective-permute-start | bytes 2949128 | tf_op jit(solution)/shard_map/branch/ppermute | solution.py:590
  202.8 18.8 %collective-permute-start.32 = (bf16[1,2,256,512]{3,2,1,0:T(8,128)(2,1)S(1)}, bf16[1,2,256,512]{3,2,1,0:T(8,128)(2,1)S(1)}, u32[]{:S(2)}, u32[]{:S(2)}) collective-permute-start(bf16[1,2,256,512]{3,2,1,0:T(8,128)(2,1)S(1)} %add_convert_fusion.9), channel_id=1, source_target_pairs={{0,16},{4,20},{8,24},{12,28},{16,0},{20,4},{24,8},{28,12},{1,17},{... | collective-permute-start | bytes 1572872 | tf_op jit(solution)/shard_map/ffn_g0_y2/ppermute | solution.py:590
  204.8 16.9 %collective-permute-start.31 = (bf16[1,2,256,512]{3,2,1,0:T(8,128)(2,1)S(1)}, bf16[1,2,256,512]{3,2,1,0:T(8,128)(2,1)S(1)}, u32[]{:S(2)}, u32[]{:S(2)}) collective-permute-start(bf16[1,2,256,512]{3,2,1,0:T(8,128)(2,1)S(1)} %add_convert_fusion.10), channel_id=1, source_target_pairs={{0,8},{4,12},{8,0},{12,4},{16,24},{20,28},{24,16},{28,20},{1,9},{5... | collective-permute-start | bytes 1572872 | tf_op jit(solution)/shard_map/ffn_g0_x2/ppermute | solution.py:590
  206.3 36.1 %collective-permute-start.34 = (bf16[2,2,256,512]{3,2,1,0:T(8,128)(2,1)}, bf16[2,2,256,512]{3,2,1,0:T(8,128)(2,1)}, u32[]{:S(2)}, u32[]{:S(2)}) collective-permute-start(bf16[2,2,256,512]{3,2,1,0:T(8,128)(2,1)} %get-tuple-element.259), channel_id=1, source_target_pairs={{0,8},{4,12},{8,0},{12,4},{16,24},{20,28},{24,16},{28,20},{1,9},{5... | collective-permute-start | bytes 3145736 | tf_op jit(solution)/shard_map/ffn_g1_x1/ppermute | solution.py:590
  206.8 35.6 %collective-permute-start.35 = (bf16[2,2,256,512]{3,2,1,0:T(8,128)(2,1)}, bf16[2,2,256,512]{3,2,1,0:T(8,128)(2,1)}, u32[]{:S(2)}, u32[]{:S(2)}) collective-permute-start(bf16[2,2,256,512]{3,2,1,0:T(8,128)(2,1)} %get-tuple-element.260), channel_id=1, source_target_pairs={{0,16},{4,20},{8,24},{12,28},{16,0},{20,4},{24,8},{28,12},{1,17},{... | collective-permute-start | bytes 3145736 | tf_op jit(solution)/shard_map/ffn_g1_y1/ppermute | solution.py:590
  209.1 12.5 %collective-permute-start.33 = (bf16[3,80,1024]{2,1,0:T(8,128)(2,1)S(1)}, bf16[3,80,1024]{2,1,0:T(8,128)(2,1)S(1)}, u32[]{:S(2)}, u32[]{:S(2)}) collective-permute-start(bf16[3,80,1024]{2,1,0:T(8,128)(2,1)S(1)} %slice_bitcast_fusion.3), channel_id=1, source_target_pairs={{0,0},{1,1},{2,6},{3,7},{4,2},{5,3},{6,4},{7,5},{8,8},{9,9},{10,14... | collective-permute-start | bytes 1474568 | tf_op jit(solution)/shard_map/block_out_route0/ppermute | solution.py:705
  223.9 24.4 %collective-permute-start.36 = (bf16[2,256,512]{2,1,0:T(8,128)(2,1)S(1)}, bf16[2,256,512]{2,1,0:T(8,128)(2,1)S(1)}, u32[]{:S(2)}, u32[]{:S(2)}) collective-permute-start(bf16[2,256,512]{2,1,0:T(8,128)(2,1)S(1)} %get-tuple-element.356), channel_id=1, source_target_pairs={{0,1},{1,0},{2,3},{3,2},{4,5},{5,4},{6,7},{7,6},{8,9},{9,8},{10,11... | collective-permute-start | bytes 1572872 | tf_op jit(solution)/shard_map/ffn_g_z3/ppermute | solution.py:590
  225.7 22.6 %collective-permute-start.37 = (bf16[3,80,1024]{2,1,0:T(8,128)(2,1)S(1)}, bf16[3,80,1024]{2,1,0:T(8,128)(2,1)S(1)}, u32[]{:S(2)}, u32[]{:S(2)}) collective-permute-start(bf16[3,80,1024]{2,1,0:T(8,128)(2,1)S(1)} %slice_bitcast_fusion.2), channel_id=1, source_target_pairs={{0,1},{1,0},{2,7},{3,6},{4,3},{5,2},{6,5},{7,4},{8,9},{9,8},{10,15... | collective-permute-start | bytes 1474568 | tf_op jit(solution)/shard_map/block_out_route1/ppermute | solution.py:705
  249.2 26.8 %collective-permute-start.40 = (bf16[2,256,512]{2,1,0:T(8,128)(2,1)S(1)}, bf16[2,256,512]{2,1,0:T(8,128)(2,1)S(1)}, u32[]{:S(2)}, u32[]{:S(2)}) collective-permute-start(bf16[2,256,512]{2,1,0:T(8,128)(2,1)S(1)} %add_convert_fusion.4), channel_id=1, source_target_pairs={{0,2},{1,3},{2,0},{3,1},{4,6},{5,7},{6,4},{7,5},{8,10},{9,11},{10,... | collective-permute-start | bytes 1572872 | tf_op jit(solution)/shard_map/ffn_g_z2/ppermute | solution.py:590
  252.0 23.9 %collective-permute-start.39 = (bf16[1,2,256,512]{3,2,1,0:T(8,128)(2,1)S(1)}, bf16[1,2,256,512]{3,2,1,0:T(8,128)(2,1)S(1)}, u32[]{:S(2)}, u32[]{:S(2)}) collective-permute-start(bf16[1,2,256,512]{3,2,1,0:T(8,128)(2,1)S(1)} %add_convert_fusion.5), channel_id=1, source_target_pairs={{0,16},{4,20},{8,24},{12,28},{16,0},{20,4},{24,8},{28,12},{1,17},{... | collective-permute-start | bytes 1572872 | tf_op jit(solution)/shard_map/ffn_g1_y2/ppermute | solution.py:590
  254.0 22.0 %collective-permute-start.38 = (bf16[1,2,256,512]{3,2,1,0:T(8,128)(2,1)S(1)}, bf16[1,2,256,512]{3,2,1,0:T(8,128)(2,1)S(1)}, u32[]{:S(2)}, u32[]{:S(2)}) collective-permute-start(bf16[1,2,256,512]{3,2,1,0:T(8,128)(2,1)S(1)} %add_convert_fusion.6), channel_id=1, source_target_pairs={{0,8},{4,12},{8,0},{12,4},{16,24},{20,28},{24,16},{28,20},{1,9},{5... | collective-permute-start | bytes 1572872 | tf_op jit(solution)/shard_map/ffn_g1_x2/ppermute | solution.py:590
  281.9 15.0 %collective-permute-start.43 = (bf16[2,256,512]{2,1,0:T(8,128)(2,1)}, bf16[2,256,512]{2,1,0:T(8,128)(2,1)S(1)}, u32[]{:S(2)}, u32[]{:S(2)}) collective-permute-start(bf16[2,256,512]{2,1,0:T(8,128)(2,1)} %fusion.19), channel_id=1, source_target_pairs={{0,1},{1,0},{2,3},{3,2},{4,5},{5,4},{6,7},{7,6},{8,9},{9,8},{10,11... | collective-permute-start | bytes 1572872 | tf_op jit(solution)/shard_map/ffn_g_z1/ppermute | solution.py:590
  285.3 25.3 %collective-permute-start.41 = (bf16[4,4,256,128]{3,2,1,0:T(8,128)(2,1)S(1)}, bf16[4,4,256,128]{3,2,1,0:T(8,128)(2,1)S(1)}, u32[]{:S(2)}, u32[]{:S(2)}) collective-permute-start(bf16[4,4,256,128]{3,2,1,0:T(8,128)(2,1)S(1)} %copy-done.68), channel_id=1, source_target_pairs={{0,8},{4,12},{8,0},{12,4},{16,24},{20,28},{24,16},{28,20},{1,9},{5... | collective-permute-start | bytes 3145736 | tf_op jit(solution)/shard_map/att_g_x1/ppermute | solution.py:590
  285.9 25.1 %collective-permute-start.42 = (bf16[4,4,256,128]{3,2,1,0:T(8,128)(2,1)S(1)}, bf16[4,4,256,128]{3,2,1,0:T(8,128)(2,1)S(1)}, u32[]{:S(2)}, u32[]{:S(2)}) collective-permute-start(bf16[4,4,256,128]{3,2,1,0:T(8,128)(2,1)S(1)} %copy-done.69), channel_id=1, source_target_pairs={{0,16},{4,20},{8,24},{12,28},{16,0},{20,4},{24,8},{28,12},{1,17},{... | collective-permute-start | bytes 3145736 | tf_op jit(solution)/shard_map/att_g_y1/ppermute | solution.py:590
  292.7 18.2 %collective-permute-start.45 = (bf16[3,80,1024]{2,1,0:T(8,128)(2,1)S(1)}, bf16[3,80,1024]{2,1,0:T(8,128)(2,1)S(1)}, u32[]{:S(2)}, u32[]{:S(2)}) collective-permute-start(bf16[3,80,1024]{2,1,0:T(8,128)(2,1)S(1)} %slice_bitcast_fusion), channel_id=1, source_target_pairs={{0,0},{1,1},{2,6},{3,7},{4,2},{5,3},{6,4},{7,5},{8,8},{9,9},{10,14... | collective-permute-start | bytes 1474568 | tf_op jit(solution)/shard_map/input_grad_route0/ppermute | solution.py:705
  316.1 13.9 %collective-permute-start.48 = (bf16[2,4,256,128]{3,2,1,0:T(8,128)(2,1)S(1)}, bf16[2,4,256,128]{3,2,1,0:T(8,128)(2,1)S(1)}, u32[]{:S(2)}, u32[]{:S(2)}) collective-permute-start(bf16[2,4,256,128]{3,2,1,0:T(8,128)(2,1)S(1)} %add_convert_fusion.1), channel_id=1, source_target_pairs={{0,16},{4,20},{8,24},{12,28},{16,0},{20,4},{24,8},{28,12},{1,17},{... | collective-permute-start | bytes 1572872 | tf_op jit(solution)/shard_map/att_g_y2/ppermute | solution.py:590
  317.7 13.6 %collective-permute-start.47 = (bf16[2,4,256,128]{3,2,1,0:T(8,128)(2,1)S(1)}, bf16[2,4,256,128]{3,2,1,0:T(8,128)(2,1)S(1)}, u32[]{:S(2)}, u32[]{:S(2)}) collective-permute-start(bf16[2,4,256,128]{3,2,1,0:T(8,128)(2,1)S(1)} %add_convert_fusion.2), channel_id=1, source_target_pairs={{0,8},{4,12},{8,0},{12,4},{16,24},{20,28},{24,16},{28,20},{1,9},{5... | collective-permute-start | bytes 1572872 | tf_op jit(solution)/shard_map/att_g_x2/ppermute | solution.py:590
  319.2 27.8 %collective-permute-start.46 = (bf16[3,80,1024]{2,1,0:T(8,128)(2,1)}, bf16[3,80,1024]{2,1,0:T(8,128)(2,1)}, u32[]{:S(2)}, u32[]{:S(2)}) collective-permute-start(bf16[3,80,1024]{2,1,0:T(8,128)(2,1)} %slice_bitcast_fusion.1), channel_id=1, source_target_pairs={{0,1},{1,0},{2,7},{3,6},{4,3},{5,2},{6,5},{7,4},{8,9},{9,8},{10,15... | collective-permute-start | bytes 1474568 | tf_op jit(solution)/shard_map/input_grad_route1/ppermute | solution.py:705
  333.7 9.6 %collective-permute-start.50 = (bf16[4,256,128]{2,1,0:T(8,128)(2,1)}, bf16[4,256,128]{2,1,0:T(8,128)(2,1)}, u32[]{:S(2)}, u32[]{:S(2)}) collective-permute-start(bf16[4,256,128]{2,1,0:T(8,128)(2,1)} %get-tuple-element.343), channel_id=1, source_target_pairs={{0,1},{1,0},{2,3},{3,2},{4,5},{5,4},{6,7},{7,6},{8,9},{9,8},{10,11... | collective-permute-start | bytes 786440 | tf_op jit(solution)/shard_map/att_g_z3/ppermute | solution.py:590
  336.3 21.1 %collective-permute-start.55 = (bf16[4,256,128]{2,1,0:T(8,128)(2,1)}, bf16[4,256,128]{2,1,0:T(8,128)(2,1)S(1)}, u32[]{:S(2)}, u32[]{:S(2)}) collective-permute-start(bf16[4,256,128]{2,1,0:T(8,128)(2,1)} %get-tuple-element.342), channel_id=1, source_target_pairs={{0,1},{1,0},{2,3},{3,2},{4,5},{5,4},{6,7},{7,6},{8,9},{9,8},{10,11... | collective-permute-start | bytes 786440 | tf_op jit(solution)/shard_map/att_g_z1/ppermute | solution.py:590
  344.5 12.9 %collective-permute-start.56 = (bf16[4,256,128]{2,1,0:T(8,128)(2,1)S(1)}, bf16[4,256,128]{2,1,0:T(8,128)(2,1)S(1)}, u32[]{:S(2)}, u32[]{:S(2)}) collective-permute-start(bf16[4,256,128]{2,1,0:T(8,128)(2,1)S(1)} %fusion.21), channel_id=1, source_target_pairs={{0,2},{1,3},{2,0},{3,1},{4,6},{5,7},{6,4},{7,5},{8,10},{9,11},{10,... | collective-permute-start | bytes 786440 | tf_op jit(solution)/shard_map/att_g_z2/ppermute | solution.py:590
  357.7 7.5 %collective-permute-start.57 = (bf16[4,128,128]{2,1,0:T(8,128)(2,1)S(1)}, bf16[4,128,128]{2,1,0:T(8,128)(2,1)S(1)}, u32[]{:S(2)}, u32[]{:S(2)}) collective-permute-start(bf16[4,128,128]{2,1,0:T(8,128)(2,1)S(1)} %dynamic-slice_bitcast_fusion.5), channel_id=1, source_target_pairs={{0,4},{4,0},{8,12},{12,8},{16,20},{20,16},{24,28},{28,24},{1,5},{5... | collective-permute-start | bytes 393224 | tf_op jit(solution)/shard_map/att_g_core/ppermute | solution.py:590
  (85 other events, 1031.1 us)
where the time goes:
time: 371 us; the launch traced here: 367 us
  waiting for transfers between devices  132 us (36%)
  Pallas kernels  112 us (30%)
  starting transfers between devices  60.9 us (16%)
  other arithmetic  35.5 us (10%)
  local copies, waits for them, and re-layouts  24.1 us (6%)
    ppermute x51, waiting for transfers between devices, swap(): return lax.ppermute(x, axis, [(i, i ^ bits) for i in range(n)])  109 us
    ppermute x51, starting transfers between devices, swap(): return lax.ppermute(x, axis, [(i, i ^ bits) for i in range(n)])  52.3 us
    pallas_call x2, Pallas kernels, ffn_call(): pl.pallas_call(functools.partial(ffn_kernel, parts, n_i, n_j, len(grads),...  45.3 us
    pallas_call x1, Pallas kernels, att_forward(): pl.pallas_call(functools.partial(att_fwd_kernel, parts, n_i), grid=(image...  19.8 us
    pallas_call x1, Pallas kernels, att_backward_last(): pl.pallas_call(functools.partial(att_bwd_last_kernel, parts, n_i, n_j, le...  19.3 us
    ppermute x4, waiting for transfers between devices, to_image(): return lax.ppermute(send, ('dp', 'mp'), image_routes(n_dp, n_mp, odd))  17.5 us
    pallas_call x1, Pallas kernels, att_backward_first(): pl.pallas_call(functools.partial(att_bwd_first_kernel, n_i, n_j, len(grad...  15.9 us
    convert_element_type x13, other arithmetic, add(): return total.astype(parts[0].dtype)  15.5 us
  transfers between devices with their start and end apart: 59, of which 26 were waited for; matrix products, arithmetic and copies ran while one was open for 11% of the time, Pallas kernels for 30%

commit v1 on v0

--- a/solution.py
+++ b/solution.py
@@ -90,31 +90,31 @@
         for_each(nj, one)
 
 
-def store_blocks(refs, q, n_j, block, i, sem, pair=0):
+def store_blocks(refs, q, n_j, block, i, sem):
     def start(views, target):
         for t, view in enumerate(views):
             pltpu.make_async_copy(view, target.at[t], sem).start()
 
     if len(refs) == 1:
-        for_each(n_j, lambda jj: start(block(jj), refs[0].at[jj ^ q, 2 * pair + i]))
+        for_each(n_j, lambda jj: start(block(jj), refs[0].at[jj ^ q, i]))
         return
     own, to_x, to_y, keep_x, keep_y = refs
-    start(block(0), own.at[2 * pair + i])
+    start(block(0), own.at[i])
     if i == 0:
-        start(block(1), keep_x.at[pair])
-        start(block(2), to_y.at[2 * pair + 1])
-        start(block(3), to_y.at[2 * pair])
+        start(block(1), keep_x.at[0])
+        start(block(2), to_y.at[1])
+        start(block(3), to_y.at[0])
     else:
-        start(block(1), to_x.at[2 * pair + 1])
-        start(block(2), keep_y.at[pair])
-        start(block(3), to_x.at[2 * pair])
+        start(block(1), to_x.at[1])
+        start(block(2), keep_y.at[0])
+        start(block(3), to_x.at[0])
 
 
 def grad_shapes(n_j, n_i, absolute, block):
     shape = lambda *lead: jax.ShapeDtypeStruct(lead + block, BF)
     if absolute:
         return [shape(n_j, n_i)]
-    return [shape(n_i), shape(n_i), shape(n_i), shape(n_i // 2), shape(n_i // 2)]
+    return [shape(2), shape(2), shape(2), shape(1), shape(1)]
 
 
 def att_column(n_i, i, t):
@@ -412,13 +412,13 @@
                 gq[rw, (t * 2 + i) * he : (t * 2 + i + 1) * he] = (both * scale).astype(BF)
 
 
-def put_att_grads(grad_refs, q, n_j, wq, gbuf, gsem, pair):
+def put_att_grads(grad_refs, q, n_j, wq, gbuf, gsem):
     he = 2 * HEAD
     for i in range(2):
         block = lambda jj, i=i: [
             gbuf.at[t, block_rows(jj, wq), pl.ds(i * he, he)] for t in range(4)
         ]
-        store_blocks(grad_refs, q, n_j, block, i, gsem, pair)
+        store_blocks(grad_refs, q, n_j, block, i, gsem)
 
 
 def hidden_back_kernel(
@@ -492,7 +492,7 @@
     n1t[...] = n1_ref[...].T
     for t in range(3):
         gbuf[t] = mm(n1t[...], gq[:, 2 * t * he : 2 * (t + 1) * he]).astype(BF)
-    put_att_grads(grad_refs, meta_ref[4], n_j, width // n_j, gbuf, gsem, 0)
+    put_att_grads(grad_refs, meta_ref[4], n_j, width // n_j, gbuf, gsem)
     bias_ref[...] = jnp.sum(gq[...].astype(F32), axis=0, keepdims=True)
     pltpu.make_async_copy(gbuf, gbuf, gsem).wait()
 
@@ -501,7 +501,7 @@
     width, rows = ght.shape
     n_i, he = 4, 2 * HEAD
     wq = width // n_j
-    grads = grad_shapes(n_j, n_i, absolute, (4, wq, he))
+    grads = grad_shapes(n_j, 2, absolute, (4, wq, he))
     return pl.pallas_call(
         functools.partial(att_bwd_first_kernel, n_i, n_j, len(grads)),
         in_specs=[SMEM_SPEC] + [VMEM_SPEC] * 5,
@@ -523,9 +523,8 @@
     parts, n_i, n_j, n_out, meta_ref, x_ref, gmix, ght, n1t, gqa_ref, qkv_ref, mix_ref, *rest
 ):
     w_refs = rest[: len(parts)]
-    rest = rest[len(parts) + n_out :]
-    gn1_ref, bias_ref, sums_ref = rest[:3]
-    rest = rest[3:]
+    gn1_ref, bias_ref, sums_ref = rest[len(parts) : len(parts) + 3]
+    rest = rest[len(parts) + 3 :]
     grad_refs = rest[:n_out]
     gq, w_scr, gbuf, sem, gsem = rest[n_out:]
     rows, width = x_ref.shape
@@ -538,7 +537,7 @@
     att_back_blocks(meta_ref, qkv_ref, gmix, gq, rows, 0)
     for t in range(3):
         gbuf[t] = mm(n1t[...], gq[:, 2 * t * he : 2 * (t + 1) * he]).astype(BF)
-    put_att_grads(grad_refs, q, n_j, wq, gbuf, gsem, 1)
+    put_att_grads(grad_refs, q, n_j, wq, gbuf, gsem)
     bias_ref[...] = jnp.sum(gq[...].astype(F32), axis=0, keepdims=True)
     sums_ref[...] = jnp.zeros_like(sums_ref)
     pltpu.make_async_copy(w_scr, w_scr, sem).wait()
@@ -556,13 +555,14 @@
     pltpu.make_async_copy(gbuf, gbuf, gsem).wait()
 
 
-def att_backward_last(meta, x, gmix, ght, n1t, gqa, qkv, mix, n_j, parts, arrays, first_grads):
+def att_backward_last(meta, x, gmix, ght, n1t, gqa, qkv, mix, n_j, parts, arrays, absolute):
     rows, width = x.shape
     n_i, he = 4, 2 * HEAD
-    grads = [jax.ShapeDtypeStruct(v.shape, v.dtype) for v in first_grads]
+    wq = width // n_j
+    grads = grad_shapes(n_j, 2, absolute, (4, wq, he))
     return pl.pallas_call(
         functools.partial(att_bwd_last_kernel, parts, n_i, n_j, len(grads)),
-        in_specs=[SMEM_SPEC] + [VMEM_SPEC] * 7 + [ANY_SPEC] * (len(arrays) + len(grads)),
+        in_specs=[SMEM_SPEC] + [VMEM_SPEC] * 7 + [ANY_SPEC] * len(arrays),
         out_specs=[VMEM_SPEC] * 3 + [ANY_SPEC] * len(grads),
         out_shape=[
             jax.ShapeDtypeStruct((rows, width), BF),
@@ -579,9 +579,8 @@
         ],
         compiler_params=pltpu.CompilerParams(vmem_limit_bytes=56 * MIB),
         cost_estimate=pl.CostEstimate(flops=20_000_000_000, bytes_accessed=30_000_000, transcendentals=1_250_000),
-        input_output_aliases={8 + len(arrays) + n: 3 + n for n in range(len(grads))},
         name="att_backward_last",
-    )(meta, x, gmix, ght, n1t, gqa, qkv, mix, *arrays, *first_grads)
+    )(meta, x, gmix, ght, n1t, gqa, qkv, mix, *arrays)
 
 
 def swap(x, axis, bits, what):
@@ -887,31 +886,35 @@
     ffn_three = swap(ffn3, "mp", 1, "ffn_g_z3")
     out_last = from_image(out_half, z, 1, "block_out")
     gmixa, ffn2 = both((gmixa, ffn2))
-    n1t, gqa, bias_a, *att_g = att_backward_first(
+    n1t, gqa, bias_a, *att_ga = att_backward_first(
         meta, gmixa, ght, n1, qkva, mixa, n_q, not square
     )
-    n1t, gqa, reach_f1, ffn_three, out_last = both((n1t, gqa, reach_f1, ffn_three, out_last))
+    n1t, gqa, reach_f1, ffn_three, out_last, att_ga = both(
+        (n1t, gqa, reach_f1, ffn_three, out_last, att_ga)
+    )
+    reach_aa = scatter_reach(att_ga, "att_ga")
     last_f1 = scatter_last(ffn_g1, reach_f1, "ffn_g1")
     ffn_two = swap(add(ffn2, ffn_three), "mp", 2, "ffn_g_z2")
-    gn1, bias_b, more_sums, *att_g = att_backward_last(
-        meta, x, gmixb, ght, n1t, gqa, qkvb, mixb, n_q, att_places, att_parts, att_g
-    )
-    gn1, last_f1, att_g, x, ffn_two = both((gn1, last_f1, att_g, x, ffn_two))
-
+    gn1, bias_b, more_sums, *att_gb = att_backward_last(
+        meta, x, gmixb, ght, n1t, gqa, qkvb, mixb, n_q, att_places, att_parts, not square
+    )
+    gn1, last_f1, att_gb, x, ffn_two, reach_aa = both((gn1, last_f1, att_gb, x, ffn_two, reach_aa))
+
+    reach_ab = scatter_reach(att_gb, "att_gb")
+    gn1_other = swap(row_half(gn1, 1 - core), "dp", 1, "grad_norm_one")
     ffn0, ffn1 = scatter_sum(ffn_g1, reach_f1, last_f1)
     ffn_one = swap(ffn1, "mp", 1, "ffn_g_z1")
-    gn1_other = swap(after(row_half(gn1, 1 - core), ffn1), "dp", 1, "grad_norm_one")
-    reach_a = scatter_reach(att_g, "att_g")
     gn1 = row_half(gn1, core).astype(F32) + gn1_other.astype(F32)
     hat1, inv1 = normalise(after(row_half(x, core), gn1_other).astype(F32))
     input_half = row_half(gh, core) + norm_back(hat1, inv1, gains[0], gn1)
     input_half = rel(input_half.astype(BF))
     in_first = from_image(input_half, z, 0, "input_grad")
-    reach_a, ffn_one, in_first, input_half, upg0, upg1, bias_a, bias_b, sums, more_sums = both(
-        (reach_a, ffn_one, in_first, input_half, upg0, upg1, bias_a, bias_b, sums, more_sums)
+    reach_ab, input_half, in_first, upg0, upg1, bias_a, bias_b, sums, more_sums, reach_aa = both(
+        (reach_ab, input_half, in_first, upg0, upg1, bias_a, bias_b, sums, more_sums, reach_aa)
     )
     in_last = from_image(input_half, z, 1, "input_grad")
-    last_a = scatter_last(att_g, reach_a, "att_g")
+    last_ab = scatter_last(att_gb, reach_ab, "att_gb")
+    last_aa = scatter_last(att_ga, reach_aa, "att_ga")
 
     def placed(values):
         mine = jnp.concatenate([lax.dynamic_slice_in_dim(values, z ^ i, 1, 0) for i in range(n_i)])
@@ -922,22 +925,23 @@
     wide.append(placed(jnp.concatenate([upg0, upg1])))
     values = [*wide, rel(sums), rel(more_sums)]
     vector = jnp.concatenate([v.reshape(-1, 128) for v in values])
-    vector = vector + swap(vector, "dp", 1, "sums_core")
-    last_a, vector = both((last_a, vector))
-    att0, att1, att2, att3 = scatter_sum(att_g, reach_a, last_a)
+    last_ab, last_aa, vector, ffn_one = both((last_ab, last_aa, vector, ffn_one))
+    att0, att1 = scatter_sum(att_ga, reach_aa, last_aa)
+    att2, att3 = scatter_sum(att_gb, reach_ab, last_ab)
     att_three = swap(att3, "mp", 1, "att_g_z3")
     att_one = swap(att1, "mp", 1, "att_g_z1")
     vector = vector + swap(vector, "dp", 2, "sums_dp2")
-    att_three, vector = both((att_three, vector))
-    att_two = swap(add(att2, att_three), "mp", 2, "att_g_z2")
     bit = 4
     while bit < n_dp:
         vector = vector + swap(vector, "dp", bit, "sums_dp" + str(bit))
         bit *= 2
+    ffn_grad = add(ffn0, ffn_one, ffn_two)
+    att_three, vector, in_last, ffn_grad = both((att_three, vector, in_last, ffn_grad))
+    att_two = swap(add(att2, att_three), "mp", 2, "att_g_z2")
+    vector = vector + swap(vector, "dp", 1, "sums_core")
     for bit in (1, 2):
         vector = vector + swap(vector, "mp", bit, "sums_z" + str(bit))
     att_grad = add(att0, att_one, att_two)
-    ffn_grad = add(ffn0, ffn_one, ffn_two)
     in_routes = [in_first, in_last]
     block_out = joined_images([out_first, out_last], z)
     block_out = jnp.where(keep_mine, block_out, jnp.zeros_like(block_out))

time: 371 us -> 365 us (0.984)
  waiting for transfers between devices: 132 us -> 115 us
  starting transfers between devices: 60.9 us -> 74.2 us
    ppermute x51 -> x55, waiting for transfers between devices: 109 us -> 91.4 us  [swap(): return lax.ppermute(x, axis, [(i, i ^ bits) for i in range(n)])]
    ppermute x51 -> x55, starting transfers between devices: 52.3 us -> 65.8 us  [swap(): return lax.ppermute(x, axis, [(i, i ^ bits) for i in range(n)])]
    convert_element_type x13 -> x16, other arithmetic: 15.5 us -> 16.1 us  [add(): return total.astype(parts[0].dtype)]
  transfers between devices with their start and end apart: 59 -> 63, of which waited for: 26 -> 26; matrix products, arithmetic and copies ran while one was open for 11% -> 13% of each run, Pallas kernels for 30% -> 31%
where the time goes in v1:
time: 365 us; the launch traced here: 360 us
  waiting for transfers between devices  115 us (32%)
  Pallas kernels  112 us (31%)
  starting transfers between devices  74.2 us (20%)
  other arithmetic  34.3 us (9%)
  local copies, waits for them, and re-layouts  23 us (6%)
    ppermute x55, waiting for transfers between devices, swap(): return lax.ppermute(x, axis, [(i, i ^ bits) for i in range(n)])  91.4 us
    ppermute x55, starting transfers between devices, swap(): return lax.ppermute(x, axis, [(i, i ^ bits) for i in range(n)])  65.8 us
    pallas_call x2, Pallas kernels, ffn_call(): pl.pallas_call(functools.partial(ffn_kernel, parts, n_i, n_j, len(grads),...  45.3 us
    pallas_call x1, Pallas kernels, att_forward(): pl.pallas_call(functools.partial(att_fwd_kernel, parts, n_i), grid=(image...  19.7 us
    pallas_call x1, Pallas kernels, att_backward_last(): pl.pallas_call(functools.partial(att_bwd_last_kernel, parts, n_i, n_j, le...  19.2 us
    ppermute x4, waiting for transfers between devices, to_image(): return lax.ppermute(send, ('dp', 'mp'), image_routes(n_dp, n_mp, odd))  17.5 us
    convert_element_type x16, other arithmetic, add(): return total.astype(parts[0].dtype)  16.1 us
    pallas_call x1, Pallas kernels, att_backward_first(): pl.pallas_call(functools.partial(att_bwd_first_kernel, n_i, n_j, len(grad...  16 us
  transfers between devices with their start and end apart: 63, of which 26 were waited for; matrix products, arithmetic and copies ran while one was open for 13% of the time, Pallas kernels for 31%

profile of v1, /device:TPU:0, one launch (start us, length us, event | category | flops | bytes accessed | tf_op | source)
XLA Modules:
  0.0 360.4 jit_solution(14028671622874118159)
XLA Ops:
  7.7 3.1 collective-permute-start.1
  10.7 2.6 collective-permute-start.2
  14.3 8.8 %collective-permute-done.1 = bf16[1056,128]{1,0:T(8,128)(2,1)S(1)} collective-permute-done((bf16[1056,128]{1,0:T(8,128)(2,1)S(1)}, bf16[1056,128]{1,0:T(8,128)(2,1)S(1)}, u32[]{:S(2)}, u32[]{:S(2)}) %collective-permute-start.1) | collective-permute-done | bytes 270368 | tf_op jit(solution)/shard_map/att_w_z1/ppermute | solution.py:589
  23.1 2.5 collective-permute-done.2
  26.2 5.9 %collective-permute-done.6 = bf16[1056,128]{1,0:T(8,128)(2,1)S(1)} collective-permute-done((bf16[1056,128]{1,0:T(8,128)(2,1)S(1)}, bf16[1056,128]{1,0:T(8,128)(2,1)S(1)}, u32[]{:S(2)}, u32[]{:S(2)}) %collective-permute-start.6) | collective-permute-done | bytes 270368 | tf_op jit(solution)/shard_map/att_w_z3/ppermute | solution.py:589
  32.3 1.6 collective-permute-start.9
  33.9 1.5 collective-permute-start.11
  35.5 1.6 collective-permute-start.4
  37.0 2.4 collective-permute-start.5
  39.5 18.1 %collective-permute-done.4 = bf16[2,256,512]{2,1,0:T(8,128)(2,1)S(1)} collective-permute-done((bf16[2,256,512]{2,1,0:T(8,128)(2,1)S(1)}, bf16[2,256,512]{2,1,0:T(8,128)(2,1)S(1)}, u32[]{:S(2)}, u32[]{:S(2)}) %collective-permute-start.4) | collective-permute-done | bytes 524320 | tf_op jit(solution)/shard_map/ffn_w_z1/ppermute | solution.py:589
  57.6 3.0 collective-permute-done.5
  60.6 1.7 collective-permute-start.7
  62.3 2.0 collective-permute-start.8
  66.1 17.5 %collective-permute-done.8 = bf16[3,80,1024]{2,1,0:T(8,128)(2,1)S(1)} collective-permute-done((bf16[3,80,1024]{2,1,0:T(8,128)(2,1)}, bf16[3,80,1024]{2,1,0:T(8,128)(2,1)S(1)}, u32[]{:S(2)}, u32[]{:S(2)}) %collective-permute-start.8) | collective-permute-done | bytes 491552 | tf_op jit(solution)/shard_map/tokens_route1/ppermute | solution.py:697
  83.7 3.5 collective-permute-start.14
  92.8 1.6 collective-permute-start.18
  94.3 19.7 %att_forward.1 = (bf16[960,1024]{1,0:T(8,128)(2,1)}, bf16[6,960,128]{2,1,0:T(8,128)(2,1)}, bf16[6,960,128]{2,1,0:T(8,128)(2,1)}, bf16[960,256]{1,0:T(8,128)(2,1)...) custom-call(bf16[3,320,1024]{2,1,0:T(8,128)(2,1)} %bitcast.249, f32[1,1024]{1,0:T(1,128)S(1)} %get-tuple-element.441.g_ref, ...), custom_call_target="tpu_custom_call" | custom-call | flops 16000000000 | bytes 20000000 | tf_op jit(solution)/shard_map/att_forward/pallas_call | solution.py:179
  114.1 2.3 collective-permute-done.15
  118.8 1.6 collective-permute-start.20
  120.4 1.6 collective-permute-start.21
  124.1 9.2 %collective-permute-done.20 = bf16[1,512,512]{2,1,0:T(8,128)(2,1)S(1)} collective-permute-done((bf16[1,512,512]{2,1,0:T(8,128)(2,1)S(1)}, bf16[1,512,512]{2,1,0:T(8,128)(2,1)S(1)}, u32[]{:S(2)}, u32[]{:S(2)}) %collective-permute-start.20) | collective-permute-done | bytes 524320 | tf_op jit(solution)/shard_map/ffn_w2_y2/ppermute | solution.py:589
  134.7 1.5 collective-permute-start.23
  136.7 23.0 %ffn_first.1 = (f32[960,1024]{1,0:T(8,128)}, bf16[960,1024]{1,0:T(8,128)(2,1)}, bf16[1024,960]{1,0:T(8,128)(2,1)}, bf16[1024,960]{1,0:T(8,128)(2,1)}, f32[960,10...) custom-call(bf16[960,1024]{1,0:T(8,128)(2,1)} %bitcast.250, ...), custom_call_target="tpu_custom_call" | custom-call | flops 24000000000 | bytes 30000000 | tf_op jit(solution)/shard_map/ffn_first/pallas_call | solution.py:350
  162.0 10.8 %collective-permute-done.25 = bf16[1,512,512]{2,1,0:T(8,128)(2,1)S(1)} collective-permute-done((bf16[1,512,512]{2,1,0:T(8,128)(2,1)S(1)}, bf16[1,512,512]{2,1,0:T(8,128)(2,1)S(1)}, u32[]{:S(2)}, u32[]{:S(2)}) %collective-permute-start.25) | collective-permute-done | bytes 524320 | tf_op jit(solution)/shard_map/ffn_w0_y2/ppermute | solution.py:589
  176.1 22.3 %ffn_last.1 = (bf16[960,1024]{1,0:T(8,128)(2,1)}, bf16[960,1024]{1,0:T(8,128)(2,1)}, f32[2,512]{1,0:T(2,128)}, bf16[2,2,256,512]{3,2,1,0:T(8,128)(2,1)}, bf16[2,...) custom-call(bf16[960,1024]{1,0:T(8,128)(2,1)} %get-tuple-element.231, ...), custom_call_target="tpu_custom_call" | custom-call | flops 24000000000 | bytes 30000000 | tf_op jit(solution)/shard_map/ffn_last/pallas_call | solution.py:350
  198.5 1.7 constant_dynamic-slice_fusion.36
  201.2 1.7 add_convert_fusion.7
  210.2 11.4 %hidden_backward.1 = (f32[960,1024]{1,0:T(8,128)}, bf16[1024,960]{1,0:T(8,128)(2,1)}, bf16[2,960,128]{2,1,0:T(8,128)(2,1)S(1)}, bf16[2,960,128]{2,1,0:T(8,128)(2,1)S(1)}, f32[8,1024]{1,0:T(8,128)S(1)}) custom-call(s32[5]{0:T(128)S(1)} %copy-done.7, f32[960,1024]{1,0:T(8,128)} %get-tuple-element.215.hid_ref, bf16[960,1024]{1,0:T(8,128)(2,1)} %get-tuple-element.250.ga_ref, ...), custom_call_target="tpu_custom_call" | custom-call | flops 10000000000 | bytes 20000000 | tf_op jit(solution)/shard_map/hidden_backward/pallas_call | solution.py:462
  221.7 2.2 fusion.18
  224.0 1.8 collective-permute-start.36
  226.5 16.0 %att_backward_first.1 = (bf16[1024,960]{1,0:T(8,128)(2,1)}, bf16[960,768]{1,0:T(8,128)(2,1)}, f32[1,768]{1,0:T(1,128)}, bf16[2,4,256,128]{3,2,1,0:T(8,128)(2,1)}...) custom-call(s32[5]{0:T(128)} %copy-done.6, ...), custom_call_target="tpu_custom_call" | custom-call | flops 16000000000 | bytes 20000000 | tf_op jit(solution)/shard_map/att_backward_first/pallas_call | solution.py:505
  242.6 5.9 %collective-permute-done.37 = bf16[3,80,1024]{2,1,0:T(8,128)(2,1)S(1)} collective-permute-done((bf16[3,80,1024]{2,1,0:T(8,128)(2,1)S(1)}, bf16[3,80,1024]{2,1,0:T(8,128)(2,1)S(1)}, u32[]{:S(2)}, u32[]{:S(2)}) %collective-permute-start.37) | collective-permute-done | bytes 491552 | tf_op jit(solution)/shard_map/block_out_route1/ppermute | solution.py:704
  248.6 1.6 collective-permute-start.40
  256.8 19.2 %att_backward_last.1 = (bf16[960,1024]{1,0:T(8,128)(2,1)}, f32[1,768]{1,0:T(1,128)}, f32[8,1024]{1,0:T(8,128)}, bf16[2,4,256,128]{3,2,1,0:T(8,128)(2,1)}, bf16[2...) custom-call(s32[5]{0:T(128)} %copy-done.6, ...), custom_call_target="tpu_custom_call" | custom-call | flops 20000000000 | bytes 30000000 | tf_op jit(solution)/shard_map/att_backward_last/pallas_call | solution.py:563
  276.1 3.1 collective-permute-done.41
  279.2 2.1 constant_dynamic-slice_fusion.30
  287.6 2.3 fusion.13
  289.9 2.1 fusion.8
  294.4 2.2 fusion.19
  310.4 4.1 %collective-permute-done.51 = bf16[2,256,512]{2,1,0:T(8,128)(2,1)} collective-permute-done((bf16[2,256,512]{2,1,0:T(8,128)(2,1)}, bf16[2,256,512]{2,1,0:T(8,128)(2,1)}, u32[]{:S(2)}, u32[]{:S(2)}) %collective-permute-start.51) | collective-permute-done | bytes 524320 | tf_op jit(solution)/shard_map/ffn_g_z1/ppermute | solution.py:589
  316.7 3.5 collective-permute-start.52
  322.3 1.6 fusion.15
  323.8 1.8 collective-permute-done.54
  325.7 7.9 %collective-permute-done.52 = bf16[4,256,128]{2,1,0:T(8,128)(2,1)S(1)} collective-permute-done((bf16[4,256,128]{2,1,0:T(8,128)(2,1)S(1)}, bf16[4,256,128]{2,1,0:T(8,128)(2,1)S(1)}, u32[]{:S(2)}, u32[]{:S(2)}) %collective-permute-start.52) | collective-permute-done | bytes 262176 | tf_op jit(solution)/shard_map/att_g_z3/ppermute | solution.py:589
  333.6 1.6 collective-permute-start.62
  335.3 3.5 collective-permute-start.60
  342.1 4.5 %collective-permute-done.57 = f32[176,128]{1,0:T(8,128)S(1)} collective-permute-done((f32[176,128]{1,0:T(8,128)S(1)}, f32[176,128]{1,0:T(8,128)S(1)}, u32[]{:S(2)}, u32[]{:S(2)}) %collective-permute-start.57) | collective-permute-done | bytes 90144 | tf_op jit(solution)/shard_map/sums_z1/ppermute | solution.py:589
  346.7 4.8 %collective-permute-start.58 = (f32[176,128]{1,0:T(8,128)S(1)}, f32[176,128]{1,0:T(8,128)S(1)}, u32[]{:S(2)}, u32[]{:S(2)}) collective-permute-start(f32[176,128]{1,0:T(8,128)S(1)} %add.355), channel_id=1, source_target_pairs={{0,2},{1,3},{2,0},{3,1},{4,6},{5,7},{6,4},{7,5},{8,10},{9,11},{10,... | collective-permute-start | bytes 270344 | tf_op jit(solution)/shard_map/sums_z2/ppermute | solution.py:589
  (408 shorter events, 82.3 us)
Async XLA Ops:
  7.7 15.5 %collective-permute-start.1 = (bf16[1056,128]{1,0:T(8,128)(2,1)S(1)}, bf16[1056,128]{1,0:T(8,128)(2,1)S(1)}, u32[]{:S(2)}, u32[]{:S(2)}) collective-permute-start(bf16[1056,128]{1,0:T(8,128)(2,1)S(1)} %get-tuple-element.413), channel_id=1, source_target_pairs={{0,1},{1,0},{2,3},{3,2},{4,5},{5,4},{6,7},{7,6},{8,9},{9,8},{10,11... | collective-permute-start | bytes 811016 | tf_op jit(solution)/shard_map/att_w_z1/ppermute | solution.py:589
  10.7 14.9 %collective-permute-start.2 = (bf16[1056,128]{1,0:T(8,128)(2,1)S(1)}, bf16[1056,128]{1,0:T(8,128)(2,1)S(1)}, u32[]{:S(2)}, u32[]{:S(2)}) collective-permute-start(bf16[1056,128]{1,0:T(8,128)(2,1)S(1)} %get-tuple-element.413), channel_id=1, source_target_pairs={{0,2},{1,3},{2,0},{3,1},{4,6},{5,7},{6,4},{7,5},{8,10},{9,11},{10,... | collective-permute-start | bytes 811016 | tf_op jit(solution)/shard_map/att_w_z2/ppermute | solution.py:589
  32.3 31.9 %collective-permute-start.9 = (bf16[4,1056,128]{2,1,0:T(8,128)(2,1)S(1)}, bf16[4,1056,128]{2,1,0:T(8,128)(2,1)S(1)}, u32[]{:S(2)}, u32[]{:S(2)}) collective-permute-start(bf16[4,1056,128]{2,1,0:T(8,128)(2,1)S(1)} %get-tuple-element.375), channel_id=1, source_target_pairs={{0,8},{4,12},{8,0},{12,4},{16,24},{20,28},{24,16},{28,20},{1,9},{5... | collective-permute-start | bytes 3244040 | tf_op jit(solution)/shard_map/att_w_x1/ppermute | solution.py:589
  33.9 31.0 %collective-permute-start.11 = (bf16[4,1056,128]{2,1,0:T(8,128)(2,1)S(1)}, bf16[4,1056,128]{2,1,0:T(8,128)(2,1)S(1)}, u32[]{:S(2)}, u32[]{:S(2)}) collective-permute-start(bf16[4,1056,128]{2,1,0:T(8,128)(2,1)S(1)} %get-tuple-element.375), channel_id=1, source_target_pairs={{0,16},{4,20},{8,24},{12,28},{16,0},{20,4},{24,8},{28,12},{1,17},{... | collective-permute-start | bytes 3244040 | tf_op jit(solution)/shard_map/att_w_y1/ppermute | solution.py:589
  35.5 22.1 %collective-permute-start.4 = (bf16[2,256,512]{2,1,0:T(8,128)(2,1)S(1)}, bf16[2,256,512]{2,1,0:T(8,128)(2,1)S(1)}, u32[]{:S(2)}, u32[]{:S(2)}) collective-permute-start(bf16[2,256,512]{2,1,0:T(8,128)(2,1)S(1)} %bitcast.260), channel_id=1, source_target_pairs={{0,1},{1,0},{2,3},{3,2},{4,5},{5,4},{6,7},{7,6},{8,9},{9,8},{10,11... | collective-permute-start | bytes 1572872 | tf_op jit(solution)/shard_map/ffn_w_z1/ppermute | solution.py:589
  37.0 23.5 %collective-permute-start.5 = (bf16[2,256,512]{2,1,0:T(8,128)(2,1)S(1)}, bf16[2,256,512]{2,1,0:T(8,128)(2,1)S(1)}, u32[]{:S(2)}, u32[]{:S(2)}) collective-permute-start(bf16[2,256,512]{2,1,0:T(8,128)(2,1)S(1)} %bitcast.261), channel_id=1, source_target_pairs={{0,2},{1,3},{2,0},{3,1},{4,6},{5,7},{6,4},{7,5},{8,10},{9,11},{10,... | collective-permute-start | bytes 1572872 | tf_op jit(solution)/shard_map/ffn_w_z2/ppermute | solution.py:589
  60.6 23.0 %collective-permute-start.13 = (bf16[2,256,512]{2,1,0:T(8,128)(2,1)S(1)}, bf16[2,256,512]{2,1,0:T(8,128)(2,1)S(1)}, u32[]{:S(2)}, u32[]{:S(2)}) collective-permute-start(bf16[2,256,512]{2,1,0:T(8,128)(2,1)S(1)} %collective-permute-done.5), channel_id=1, source_target_pairs={{0,1},{1,0},{2,3},{3,2},{4,5},{5,4},{6,7},{7,6},{8,9},{9,8},{10,11... | collective-permute-start | bytes 1572872 | tf_op jit(solution)/shard_map/ffn_w_z3/ppermute | solution.py:589
  62.3 21.3 %collective-permute-start.8 = (bf16[3,80,1024]{2,1,0:T(8,128)(2,1)}, bf16[3,80,1024]{2,1,0:T(8,128)(2,1)S(1)}, u32[]{:S(2)}, u32[]{:S(2)}) collective-permute-start(bf16[3,80,1024]{2,1,0:T(8,128)(2,1)} %get-tuple-element.185), channel_id=1, source_target_pairs={{1,0},{0,1},{7,2},{6,3},{3,4},{2,5},{5,6},{4,7},{9,8},{8,9},{15,10... | collective-permute-start | bytes 1474568 | tf_op jit(solution)/shard_map/tokens_route1/ppermute | solution.py:697
  64.3 19.3 %collective-permute-start.10 = (bf16[2,1056,128]{2,1,0:T(8,128)(2,1)S(1)}, bf16[2,1056,128]{2,1,0:T(8,128)(2,1)S(1)}, u32[]{:S(2)}, u32[]{:S(2)}) collective-permute-start(bf16[2,1056,128]{2,1,0:T(8,128)(2,1)S(1)} %slice.322), channel_id=1, source_target_pairs={{0,16},{4,20},{8,24},{12,28},{16,0},{20,4},{24,8},{28,12},{1,17},{... | collective-permute-start | bytes 1622024 | tf_op jit(solution)/shard_map/att_w_y2/ppermute | solution.py:589
  64.9 18.7 %collective-permute-start.12 = (bf16[2,1056,128]{2,1,0:T(8,128)(2,1)S(1)}, bf16[2,1056,128]{2,1,0:T(8,128)(2,1)S(1)}, u32[]{:S(2)}, u32[]{:S(2)}) collective-permute-start(bf16[2,1056,128]{2,1,0:T(8,128)(2,1)S(1)} %slice.323), channel_id=1, source_target_pairs={{0,8},{4,12},{8,0},{12,4},{16,24},{20,28},{24,16},{28,20},{1,9},{5... | collective-permute-start | bytes 1622024 | tf_op jit(solution)/shard_map/att_w_x2/ppermute | solution.py:589
  91.0 25.4 %collective-permute-start.15 = (bf16[2,512,512]{2,1,0:T(8,128)(2,1)S(1)}, bf16[2,512,512]{2,1,0:T(8,128)(2,1)S(1)}, u32[]{:S(2)}, u32[]{:S(2)}) collective-permute-start(bf16[2,512,512]{2,1,0:T(8,128)(2,1)S(1)} %pad_maximum_fusion.3), channel_id=1, source_target_pairs={{0,8},{4,12},{8,0},{12,4},{16,24},{20,28},{24,16},{28,20},{1,9},{5... | collective-permute-start | bytes 3145736 | tf_op jit(solution)/shard_map/ffn_w2_x1/ppermute | solution.py:589
  91.6 25.1 %collective-permute-start.16 = (bf16[2,512,512]{2,1,0:T(8,128)(2,1)S(1)}, bf16[2,512,512]{2,1,0:T(8,128)(2,1)S(1)}, u32[]{:S(2)}, u32[]{:S(2)}) collective-permute-start(bf16[2,512,512]{2,1,0:T(8,128)(2,1)S(1)} %pad_maximum_fusion.3), channel_id=1, source_target_pairs={{0,16},{4,20},{8,24},{12,28},{16,0},{20,4},{24,8},{28,12},{1,17},{... | collective-permute-start | bytes 3145736 | tf_op jit(solution)/shard_map/ffn_w2_y1/ppermute | solution.py:589
  92.1 22.0 %collective-permute-start.17 = (bf16[3,80,1024]{2,1,0:T(8,128)(2,1)S(1)}, bf16[3,80,1024]{2,1,0:T(8,128)(2,1)S(1)}, u32[]{:S(2)}, u32[]{:S(2)}) collective-permute-start(bf16[3,80,1024]{2,1,0:T(8,128)(2,1)S(1)} %get-tuple-element.199), channel_id=1, source_target_pairs={{0,0},{1,1},{6,2},{7,3},{2,4},{3,5},{4,6},{5,7},{8,8},{9,9},{14,10... | collective-permute-start | bytes 1474568 | tf_op jit(solution)/shard_map/cotangent_route0/ppermute | solution.py:697
  92.8 21.3 %collective-permute-start.18 = (bf16[3,80,1024]{2,1,0:T(8,128)(2,1)S(1)}, bf16[3,80,1024]{2,1,0:T(8,128)(2,1)S(1)}, u32[]{:S(2)}, u32[]{:S(2)}) collective-permute-start(bf16[3,80,1024]{2,1,0:T(8,128)(2,1)S(1)} %get-tuple-element.200), channel_id=1, source_target_pairs={{1,0},{0,1},{7,2},{6,3},{3,4},{2,5},{5,6},{4,7},{9,8},{8,9},{15,10... | collective-permute-start | bytes 1474568 | tf_op jit(solution)/shard_map/cotangent_route1/ppermute | solution.py:697
  116.7 18.0 %collective-permute-start.22 = (bf16[960,1024]{1,0:T(8,128)(2,1)}, bf16[960,1024]{1,0:T(8,128)(2,1)S(1)}, u32[]{:S(2)}, u32[]{:S(2)}) collective-permute-start(bf16[960,1024]{1,0:T(8,128)(2,1)} %get-tuple-element.202.refs_1_), channel_id=1, source_target_pairs={{0,4},{4,0},{8,12},{12,8},{16,20},{20,16},{24,28},{28,24},{1,5},{5... | collective-permute-start | bytes 5898248 | tf_op jit(solution)/shard_map/attended/ppermute | solution.py:589
  118.8 14.5 %collective-permute-start.20 = (bf16[1,512,512]{2,1,0:T(8,128)(2,1)S(1)}, bf16[1,512,512]{2,1,0:T(8,128)(2,1)S(1)}, u32[]{:S(2)}, u32[]{:S(2)}) collective-permute-start(bf16[1,512,512]{2,1,0:T(8,128)(2,1)S(1)} %slice.255), channel_id=1, source_target_pairs={{0,16},{4,20},{8,24},{12,28},{16,0},{20,4},{24,8},{28,12},{1,17},{... | collective-permute-start | bytes 1572872 | tf_op jit(solution)/shard_map/ffn_w2_y2/ppermute | solution.py:589
  120.4 14.2 %collective-permute-start.21 = (bf16[1,512,512]{2,1,0:T(8,128)(2,1)S(1)}, bf16[1,512,512]{2,1,0:T(8,128)(2,1)S(1)}, u32[]{:S(2)}, u32[]{:S(2)}) collective-permute-start(bf16[1,512,512]{2,1,0:T(8,128)(2,1)S(1)} %slice.256), channel_id=1, source_target_pairs={{0,8},{4,12},{8,0},{12,4},{16,24},{20,28},{24,16},{28,20},{1,9},{5... | collective-permute-start | bytes 1572872 | tf_op jit(solution)/shard_map/ffn_w2_x2/ppermute | solution.py:589
  134.7 25.1 %collective-permute-start.23 = (bf16[2,512,512]{2,1,0:T(8,128)(2,1)S(1)}, bf16[2,512,512]{2,1,0:T(8,128)(2,1)S(1)}, u32[]{:S(2)}, u32[]{:S(2)}) collective-permute-start(bf16[2,512,512]{2,1,0:T(8,128)(2,1)S(1)} %pad_maximum_fusion.4), channel_id=1, source_target_pairs={{0,8},{4,12},{8,0},{12,4},{16,24},{20,28},{24,16},{28,20},{1,9},{5... | collective-permute-start | bytes 3145736 | tf_op jit(solution)/shard_map/ffn_w0_x1/ppermute | solution.py:589
  136.2 24.3 %collective-permute-start.24 = (bf16[2,512,512]{2,1,0:T(8,128)(2,1)S(1)}, bf16[2,512,512]{2,1,0:T(8,128)(2,1)S(1)}, u32[]{:S(2)}, u32[]{:S(2)}) collective-permute-start(bf16[2,512,512]{2,1,0:T(8,128)(2,1)S(1)} %pad_maximum_fusion.4), channel_id=1, source_target_pairs={{0,16},{4,20},{8,24},{12,28},{16,0},{20,4},{24,8},{28,12},{1,17},{... | collective-permute-start | bytes 3145736 | tf_op jit(solution)/shard_map/ffn_w0_y1/ppermute | solution.py:589
  160.6 12.2 %collective-permute-start.25 = (bf16[1,512,512]{2,1,0:T(8,128)(2,1)S(1)}, bf16[1,512,512]{2,1,0:T(8,128)(2,1)S(1)}, u32[]{:S(2)}, u32[]{:S(2)}) collective-permute-start(bf16[1,512,512]{2,1,0:T(8,128)(2,1)S(1)} %slice.262), channel_id=1, source_target_pairs={{0,16},{4,20},{8,24},{12,28},{16,0},{20,4},{24,8},{28,12},{1,17},{... | collective-permute-start | bytes 1572872 | tf_op jit(solution)/shard_map/ffn_w0_y2/ppermute | solution.py:589
  161.4 12.6 %collective-permute-start.26 = (bf16[1,512,512]{2,1,0:T(8,128)(2,1)S(1)}, bf16[1,512,512]{2,1,0:T(8,128)(2,1)S(1)}, u32[]{:S(2)}, u32[]{:S(2)}) collective-permute-start(bf16[1,512,512]{2,1,0:T(8,128)(2,1)S(1)} %slice.263), channel_id=1, source_target_pairs={{0,8},{4,12},{8,0},{12,4},{16,24},{20,28},{24,16},{28,20},{1,9},{5... | collective-permute-start | bytes 1572872 | tf_op jit(solution)/shard_map/ffn_w0_x2/ppermute | solution.py:589
  174.0 24.4 %collective-permute-start.27 = (bf16[2,2,256,512]{3,2,1,0:T(8,128)(2,1)}, bf16[2,2,256,512]{3,2,1,0:T(8,128)(2,1)}, u32[]{:S(2)}, u32[]{:S(2)}) collective-permute-start(bf16[2,2,256,512]{3,2,1,0:T(8,128)(2,1)} %get-tuple-element.248), channel_id=1, source_target_pairs={{0,8},{4,12},{8,0},{12,4},{16,24},{20,28},{24,16},{28,20},{1,9},{5... | collective-permute-start | bytes 3145736 | tf_op jit(solution)/shard_map/ffn_g0_x1/ppermute | solution.py:589
  174.6 23.8 %collective-permute-start.28 = (bf16[2,2,256,512]{3,2,1,0:T(8,128)(2,1)S(1)}, bf16[2,2,256,512]{3,2,1,0:T(8,128)(2,1)}, u32[]{:S(2)}, u32[]{:S(2)}) collective-permute-start(bf16[2,2,256,512]{3,2,1,0:T(8,128)(2,1)S(1)} %copy-done.73), channel_id=1, source_target_pairs={{0,16},{4,20},{8,24},{12,28},{16,0},{20,4},{24,8},{28,12},{1,17},{... | collective-permute-start | bytes 3145736 | tf_op jit(solution)/shard_map/ffn_g0_y1/ppermute | solution.py:589
  198.4 9.9 %collective-permute-start.29 = (bf16[960,1024]{1,0:T(8,128)(2,1)}, bf16[960,1024]{1,0:T(8,128)(2,1)}, u32[]{:S(2)}, u32[]{:S(2)}) collective-permute-start(bf16[960,1024]{1,0:T(8,128)(2,1)} %get-tuple-element.250.ga_ref), channel_id=1, source_target_pairs={{0,4},{4,0},{8,12},{12,8},{16,20},{20,16},{24,28},{28,24},{1,5},{5... | collective-permute-start | bytes 5898248 | tf_op jit(solution)/shard_map/grad_norm_two/ppermute | solution.py:589
  202.9 18.8 %collective-permute-start.32 = (bf16[1,2,256,512]{3,2,1,0:T(8,128)(2,1)S(1)}, bf16[1,2,256,512]{3,2,1,0:T(8,128)(2,1)S(1)}, u32[]{:S(2)}, u32[]{:S(2)}) collective-permute-start(bf16[1,2,256,512]{3,2,1,0:T(8,128)(2,1)S(1)} %add_convert_fusion.7), channel_id=1, source_target_pairs={{0,16},{4,20},{8,24},{12,28},{16,0},{20,4},{24,8},{28,12},{1,17},{... | collective-permute-start | bytes 1572872 | tf_op jit(solution)/shard_map/ffn_g0_y2/ppermute | solution.py:589
  204.8 16.9 %collective-permute-start.31 = (bf16[1,2,256,512]{3,2,1,0:T(8,128)(2,1)S(1)}, bf16[1,2,256,512]{3,2,1,0:T(8,128)(2,1)S(1)}, u32[]{:S(2)}, u32[]{:S(2)}) collective-permute-start(bf16[1,2,256,512]{3,2,1,0:T(8,128)(2,1)S(1)} %add_convert_fusion.8), channel_id=1, source_target_pairs={{0,8},{4,12},{8,0},{12,4},{16,24},{20,28},{24,16},{28,20},{1,9},{5... | collective-permute-start | bytes 1572872 | tf_op jit(solution)/shard_map/ffn_g0_x2/ppermute | solution.py:589
  206.2 36.3 %collective-permute-start.34 = (bf16[2,2,256,512]{3,2,1,0:T(8,128)(2,1)}, bf16[2,2,256,512]{3,2,1,0:T(8,128)(2,1)}, u32[]{:S(2)}, u32[]{:S(2)}) collective-permute-start(bf16[2,2,256,512]{3,2,1,0:T(8,128)(2,1)} %get-tuple-element.271), channel_id=1, source_target_pairs={{0,8},{4,12},{8,0},{12,4},{16,24},{20,28},{24,16},{28,20},{1,9},{5... | collective-permute-start | bytes 3145736 | tf_op jit(solution)/shard_map/ffn_g1_x1/ppermute | solution.py:589
  206.8 35.7 %collective-permute-start.35 = (bf16[2,2,256,512]{3,2,1,0:T(8,128)(2,1)}, bf16[2,2,256,512]{3,2,1,0:T(8,128)(2,1)}, u32[]{:S(2)}, u32[]{:S(2)}) collective-permute-start(bf16[2,2,256,512]{3,2,1,0:T(8,128)(2,1)} %get-tuple-element.272), channel_id=1, source_target_pairs={{0,16},{4,20},{8,24},{12,28},{16,0},{20,4},{24,8},{28,12},{1,17},{... | collective-permute-start | bytes 3145736 | tf_op jit(solution)/shard_map/ffn_g1_y1/ppermute | solution.py:589
  209.2 12.5 %collective-permute-start.33 = (bf16[3,80,1024]{2,1,0:T(8,128)(2,1)S(1)}, bf16[3,80,1024]{2,1,0:T(8,128)(2,1)S(1)}, u32[]{:S(2)}, u32[]{:S(2)}) collective-permute-start(bf16[3,80,1024]{2,1,0:T(8,128)(2,1)S(1)} %slice_bitcast_fusion.3), channel_id=1, source_target_pairs={{0,0},{1,1},{2,6},{3,7},{4,2},{5,3},{6,4},{7,5},{8,8},{9,9},{10,14... | collective-permute-start | bytes 1474568 | tf_op jit(solution)/shard_map/block_out_route0/ppermute | solution.py:704
  224.0 24.5 %collective-permute-start.36 = (bf16[2,256,512]{2,1,0:T(8,128)(2,1)S(1)}, bf16[2,256,512]{2,1,0:T(8,128)(2,1)S(1)}, u32[]{:S(2)}, u32[]{:S(2)}) collective-permute-start(bf16[2,256,512]{2,1,0:T(8,128)(2,1)S(1)} %get-tuple-element.378), channel_id=1, source_target_pairs={{0,1},{1,0},{2,3},{3,2},{4,5},{5,4},{6,7},{7,6},{8,9},{9,8},{10,11... | collective-permute-start | bytes 1572872 | tf_op jit(solution)/shard_map/ffn_g_z3/ppermute | solution.py:589
  225.8 22.6 %collective-permute-start.37 = (bf16[3,80,1024]{2,1,0:T(8,128)(2,1)S(1)}, bf16[3,80,1024]{2,1,0:T(8,128)(2,1)S(1)}, u32[]{:S(2)}, u32[]{:S(2)}) collective-permute-start(bf16[3,80,1024]{2,1,0:T(8,128)(2,1)S(1)} %slice_bitcast_fusion.2), channel_id=1, source_target_pairs={{0,1},{1,0},{2,7},{3,6},{4,3},{5,2},{6,5},{7,4},{8,9},{9,8},{10,15... | collective-permute-start | bytes 1474568 | tf_op jit(solution)/shard_map/block_out_route1/ppermute | solution.py:704
  248.6 27.5 %collective-permute-start.40 = (bf16[2,256,512]{2,1,0:T(8,128)(2,1)S(1)}, bf16[2,256,512]{2,1,0:T(8,128)(2,1)S(1)}, u32[]{:S(2)}, u32[]{:S(2)}) collective-permute-start(bf16[2,256,512]{2,1,0:T(8,128)(2,1)S(1)} %add_convert_fusion.2), channel_id=1, source_target_pairs={{0,2},{1,3},{2,0},{3,1},{4,6},{5,7},{6,4},{7,5},{8,10},{9,11},{10,... | collective-permute-start | bytes 1572872 | tf_op jit(solution)/shard_map/ffn_g_z2/ppermute | solution.py:589
  251.4 24.7 %collective-permute-start.39 = (bf16[1,2,256,512]{3,2,1,0:T(8,128)(2,1)S(1)}, bf16[1,2,256,512]{3,2,1,0:T(8,128)(2,1)S(1)}, u32[]{:S(2)}, u32[]{:S(2)}) collective-permute-start(bf16[1,2,256,512]{3,2,1,0:T(8,128)(2,1)S(1)} %add_convert_fusion.3), channel_id=1, source_target_pairs={{0,16},{4,20},{8,24},{12,28},{16,0},{20,4},{24,8},{28,12},{1,17},{... | collective-permute-start | bytes 1572872 | tf_op jit(solution)/shard_map/ffn_g1_y2/ppermute | solution.py:589
  253.2 22.8 %collective-permute-start.38 = (bf16[1,2,256,512]{3,2,1,0:T(8,128)(2,1)S(1)}, bf16[1,2,256,512]{3,2,1,0:T(8,128)(2,1)S(1)}, u32[]{:S(2)}, u32[]{:S(2)}) collective-permute-start(bf16[1,2,256,512]{3,2,1,0:T(8,128)(2,1)S(1)} %add_convert_fusion.4), channel_id=1, source_target_pairs={{0,8},{4,12},{8,0},{12,4},{16,24},{20,28},{24,16},{28,20},{1,9},{5... | collective-permute-start | bytes 1572872 | tf_op jit(solution)/shard_map/ffn_g1_x2/ppermute | solution.py:589
  254.8 24.5 %collective-permute-start.41 = (bf16[2,4,256,128]{3,2,1,0:T(8,128)(2,1)S(1)}, bf16[2,4,256,128]{3,2,1,0:T(8,128)(2,1)S(1)}, u32[]{:S(2)}, u32[]{:S(2)}) collective-permute-start(bf16[2,4,256,128]{3,2,1,0:T(8,128)(2,1)S(1)} %copy-done.77), channel_id=1, source_target_pairs={{0,8},{4,12},{8,0},{12,4},{16,24},{20,28},{24,16},{28,20},{1,9},{5... | collective-permute-start | bytes 1572872 | tf_op jit(solution)/shard_map/att_ga_x1/ppermute | solution.py:589
  255.3 23.9 %collective-permute-start.42 = (bf16[2,4,256,128]{3,2,1,0:T(8,128)(2,1)S(1)}, bf16[2,4,256,128]{3,2,1,0:T(8,128)(2,1)S(1)}, u32[]{:S(2)}, u32[]{:S(2)}) collective-permute-start(bf16[2,4,256,128]{3,2,1,0:T(8,128)(2,1)S(1)} %copy-done.76), channel_id=1, source_target_pairs={{0,16},{4,20},{8,24},{12,28},{16,0},{20,4},{24,8},{28,12},{1,17},{... | collective-permute-start | bytes 1572872 | tf_op jit(solution)/shard_map/att_ga_y1/ppermute | solution.py:589
  284.8 14.3 %collective-permute-start.43 = (bf16[2,4,256,128]{3,2,1,0:T(8,128)(2,1)S(1)}, bf16[2,4,256,128]{3,2,1,0:T(8,128)(2,1)S(1)}, u32[]{:S(2)}, u32[]{:S(2)}) collective-permute-start(bf16[2,4,256,128]{3,2,1,0:T(8,128)(2,1)S(1)} %copy-done.75), channel_id=1, source_target_pairs={{0,8},{4,12},{8,0},{12,4},{16,24},{20,28},{24,16},{28,20},{1,9},{5... | collective-permute-start | bytes 1572872 | tf_op jit(solution)/shard_map/att_gb_x1/ppermute | solution.py:589
  286.2 14.1 %collective-permute-start.44 = (bf16[2,4,256,128]{3,2,1,0:T(8,128)(2,1)S(1)}, bf16[2,4,256,128]{3,2,1,0:T(8,128)(2,1)S(1)}, u32[]{:S(2)}, u32[]{:S(2)}) collective-permute-start(bf16[2,4,256,128]{3,2,1,0:T(8,128)(2,1)S(1)} %copy-done.74), channel_id=1, source_target_pairs={{0,16},{4,20},{8,24},{12,28},{16,0},{20,4},{24,8},{28,12},{1,17},{... | collective-permute-start | bytes 1572872 | tf_op jit(solution)/shard_map/att_gb_y1/ppermute | solution.py:589
  292.4 7.9 %collective-permute-start.46 = (bf16[3,80,1024]{2,1,0:T(8,128)(2,1)S(1)}, bf16[3,80,1024]{2,1,0:T(8,128)(2,1)S(1)}, u32[]{:S(2)}, u32[]{:S(2)}) collective-permute-start(bf16[3,80,1024]{2,1,0:T(8,128)(2,1)S(1)} %slice_bitcast_fusion), channel_id=1, source_target_pairs={{0,0},{1,1},{2,6},{3,7},{4,2},{5,3},{6,4},{7,5},{8,8},{9,9},{10,14... | collective-permute-start | bytes 1474568 | tf_op jit(solution)/shard_map/input_grad_route0/ppermute | solution.py:704
  296.6 17.9 %collective-permute-start.51 = (bf16[2,256,512]{2,1,0:T(8,128)(2,1)}, bf16[2,256,512]{2,1,0:T(8,128)(2,1)}, u32[]{:S(2)}, u32[]{:S(2)}) collective-permute-start(bf16[2,256,512]{2,1,0:T(8,128)(2,1)} %fusion.19), channel_id=1, source_target_pairs={{0,1},{1,0},{2,3},{3,2},{4,5},{5,4},{6,7},{7,6},{8,9},{9,8},{10,11... | collective-permute-start | bytes 1572872 | tf_op jit(solution)/shard_map/ffn_g_z1/ppermute | solution.py:589
  304.6 9.8 %collective-permute-start.50 = (bf16[1,4,256,128]{3,2,1,0:T(8,128)(2,1)S(1)}, bf16[1,4,256,128]{3,2,1,0:T(8,128)(2,1)S(1)}, u32[]{:S(2)}, u32[]{:S(2)}) collective-permute-start(bf16[1,4,256,128]{3,2,1,0:T(8,128)(2,1)S(1)} %add_convert_fusion.13), channel_id=1, source_target_pairs={{0,16},{4,20},{8,24},{12,28},{16,0},{20,4},{24,8},{28,12},{1,17},{... | collective-permute-start | bytes 786440 | tf_op jit(solution)/shard_map/att_ga_y2/ppermute | solution.py:589
  305.5 9.0 %collective-permute-start.49 = (bf16[1,4,256,128]{3,2,1,0:T(8,128)(2,1)S(1)}, bf16[1,4,256,128]{3,2,1,0:T(8,128)(2,1)S(1)}, u32[]{:S(2)}, u32[]{:S(2)}) collective-permute-start(bf16[1,4,256,128]{3,2,1,0:T(8,128)(2,1)S(1)} %add_convert_fusion.14), channel_id=1, source_target_pairs={{0,8},{4,12},{8,0},{12,4},{16,24},{20,28},{24,16},{28,20},{1,9},{5... | collective-permute-start | bytes 786440 | tf_op jit(solution)/shard_map/att_ga_x2/ppermute | solution.py:589
  314.5 11.2 %collective-permute-start.55 = (bf16[3,80,1024]{2,1,0:T(8,128)(2,1)S(1)}, bf16[3,80,1024]{2,1,0:T(8,128)(2,1)S(1)}, u32[]{:S(2)}, u32[]{:S(2)}) collective-permute-start(bf16[3,80,1024]{2,1,0:T(8,128)(2,1)S(1)} %slice_bitcast_fusion.1), channel_id=1, source_target_pairs={{0,1},{1,0},{2,7},{3,6},{4,3},{5,2},{6,5},{7,4},{8,9},{9,8},{10,15... | collective-permute-start | bytes 1474568 | tf_op jit(solution)/shard_map/input_grad_route1/ppermute | solution.py:704
  316.7 16.8 %collective-permute-start.52 = (bf16[4,256,128]{2,1,0:T(8,128)(2,1)S(1)}, bf16[4,256,128]{2,1,0:T(8,128)(2,1)S(1)}, u32[]{:S(2)}, u32[]{:S(2)}) collective-permute-start(bf16[4,256,128]{2,1,0:T(8,128)(2,1)S(1)} %fusion.25), channel_id=1, source_target_pairs={{0,1},{1,0},{2,3},{3,2},{4,5},{5,4},{6,7},{7,6},{8,9},{9,8},{10,11... | collective-permute-start | bytes 786440 | tf_op jit(solution)/shard_map/att_g_z3/ppermute | solution.py:589
  321.0 32.8 %collective-permute-start.59 = (bf16[4,256,128]{2,1,0:T(8,128)(2,1)}, bf16[4,256,128]{2,1,0:T(8,128)(2,1)}, u32[]{:S(2)}, u32[]{:S(2)}) collective-permute-start(bf16[4,256,128]{2,1,0:T(8,128)(2,1)} %fusion.27), channel_id=1, source_target_pairs={{0,1},{1,0},{2,3},{3,2},{4,5},{5,4},{6,7},{7,6},{8,9},{9,8},{10,11... | collective-permute-start | bytes 786440 | tf_op jit(solution)/shard_map/att_g_z1/ppermute | solution.py:589
  333.6 17.9 %collective-permute-start.62 = (bf16[2,128,512]{2,1,0:T(8,128)(2,1)S(1)}, bf16[2,128,512]{2,1,0:T(8,128)(2,1)S(1)}, u32[]{:S(2)}, u32[]{:S(2)}) collective-permute-start(bf16[2,128,512]{2,1,0:T(8,128)(2,1)S(1)} %dynamic-slice_bitcast_fusion.4), channel_id=1, source_target_pairs={{0,4},{4,0},{8,12},{12,8},{16,20},{20,16},{24,28},{28,24},{1,5},{5... | collective-permute-start | bytes 786440 | tf_op jit(solution)/shard_map/ffn_g_core/ppermute | solution.py:589
  335.3 18.6 %collective-permute-start.60 = (bf16[4,256,128]{2,1,0:T(8,128)(2,1)S(1)}, bf16[4,256,128]{2,1,0:T(8,128)(2,1)}, u32[]{:S(2)}, u32[]{:S(2)}) collective-permute-start(bf16[4,256,128]{2,1,0:T(8,128)(2,1)S(1)} %fusion.21), channel_id=1, source_target_pairs={{0,2},{1,3},{2,0},{3,1},{4,6},{5,7},{6,4},{7,5},{8,10},{9,11},{10,... | collective-permute-start | bytes 786440 | tf_op jit(solution)/shard_map/att_g_z2/ppermute | solution.py:589
  346.7 8.8 %collective-permute-start.58 = (f32[176,128]{1,0:T(8,128)S(1)}, f32[176,128]{1,0:T(8,128)S(1)}, u32[]{:S(2)}, u32[]{:S(2)}) collective-permute-start(f32[176,128]{1,0:T(8,128)S(1)} %add.355), channel_id=1, source_target_pairs={{0,2},{1,3},{2,0},{3,1},{4,6},{5,7},{6,4},{7,5},{8,10},{9,11},{10,... | collective-permute-start | bytes 270344 | tf_op jit(solution)/shard_map/sums_z2/ppermute | solution.py:589
  (97 other events, 1121.1 us)

commit v2 on v1

--- a/solution.py
+++ b/solution.py
@@ -513,7 +513,7 @@
         ]
         + grads,
         scratch_shapes=[pltpu.VMEM((4, width, 2 * he), BF), pltpu.SemaphoreType.DMA],
-        compiler_params=pltpu.CompilerParams(vmem_limit_bytes=60 * MIB),
+        compiler_params=pltpu.CompilerParams(vmem_limit_bytes=48 * MIB),
         cost_estimate=pl.CostEstimate(flops=16_000_000_000, bytes_accessed=20_000_000, transcendentals=1_250_000),
         name="att_backward_first",
     )(meta, gmix, ght, n1, qkv, mix)
@@ -791,16 +791,18 @@
     one = swap(att_mine, "mp", 1, "att_w_z1")
     token_groups = image_groups(rel(tokens))
     sends = [for_route(token_groups, z, odd) for odd in (0, 1)]
+    own_near = gather_near(ffn_own, "ffn_w0") if square else ()
     one, two, sends, ffn_own = both((one, two, sends, ffn_own))
     three = swap(two, "mp", 1, "att_w_z3")
-    far_one, far_two = swap(ffn_own, "mp", 1, "ffn_w_z1"), swap(ffn_own, "mp", 2, "ffn_w_z2")
+    far_two = swap(ffn_own, "mp", 2, "ffn_w_z2")
     att_z = jnp.stack([att_mine, one, two, three])
     bias_all = att_z[:, 4 * wq : 4 * wq + 3 * n_bias].astype(F32).reshape(n_i, 3, n_bias, he)
     bias_all = bias_all[:, 0] + (bias_all[:, 1] + bias_all[:, 2])
     bias_three = jnp.stack([bias_all[:, 0], jnp.zeros((n_i, he), F32), bias_all[:, 1]])
     bias_rows = jnp.transpose(bias_three.reshape(3, 2, 2, he), (1, 0, 2, 3)).reshape(1, -1)
-    att_near = gather_near(att_z, "att_w") if square else ()
-    far_one, far_two, sends, bias_rows = both((far_one, far_two, sends, bias_rows))
+    att_near = gather_near(after(att_z, *own_near), "att_w") if square else ()
+    own_far = gather_far(*own_near, "ffn_w0") if square else ()
+    far_two, sends, bias_rows = both((far_two, sends, bias_rows))
     far_three = swap(far_two, "mp", 1, "ffn_w_z3")
     token_rows = [to_image(sends[odd], odd, "tokens") for odd in (0, 1)]
 
@@ -812,7 +814,10 @@
     cot = rel(jnp.where(keep_mine, cotangent, jnp.zeros_like(cotangent)))
     cot_groups = image_groups(cot)
     sends = [for_route(cot_groups, z, odd) for odd in (0, 1)]
-    token_rows, att_far, far_three, sends = both((token_rows, att_far, far_three, sends))
+    token_rows, att_far, far_three, sends, own_far = both(
+        (token_rows, att_far, far_three, sends, own_far)
+    )
+    far_one = swap(after(ffn_own, *token_rows), "mp", 1, "ffn_w_z1")
     att_parts = [v[None] for v in (att_z, *att_near, *att_far)] if square else list(att_far)
     x = whole_rows(jnp.stack(token_rows, 1), "tokens_core")
     ffn_far = flat(jnp.stack([far_two, far_three]))
@@ -828,7 +833,7 @@
         att_places,
         att_parts,
     )
-    part, n1, x, far_near, cot_rows = both((part, n1, x, far_near, cot_rows))
+    part, n1, x, far_near, cot_rows, far_one = both((part, n1, x, far_near, cot_rows, far_one))
     part_other = swap(part, "dp", 1, "attended")
     if square:
         far_far = gather_far(*far_near, "ffn_w2")
@@ -837,9 +842,8 @@
     else:
         parts0, places = [gather_plane(ffn_far, "ffn_w2")], [(0, 0, 0, 2, True)]
     go = whole_rows(jnp.stack(cot_rows, 1), "cotangent_core")
-    ffn_here = flat(jnp.stack([ffn_own, far_one]))
-    go, parts0, part_other, ffn_here = both((go, parts0, part_other, ffn_here))
-    here_near = gather_near(ffn_here, "ffn_w0") if square else ()
+    go, parts0, part_other, far_one = both((go, parts0, part_other, far_one))
+    here_near = gather_near(far_one, "ffn_w1") if square else ()
     up_rows = bias_all[:, 2:].reshape(n_i, fh)
     hidden, n2, n2t, got, sum_b, sum_g, upg1, *ffn_g0 = ffn_call(
         [x, part, part_other, out_b[0:1], gains[1:2], shifts[1:2], go, up_rows[2:], meta],
@@ -853,9 +857,13 @@
     )
     n2, ffn_g0, here_near = both((n2, ffn_g0, here_near))
     if square:
-        parts1 = [v[None] for v in (ffn_here, *here_near, *gather_far(*here_near, "ffn_w0"))]
+        here_far = gather_far(*here_near, "ffn_w1")
+        parts1 = [ffn_own, *own_near, *own_far, far_one, *here_near, *here_far]
+        parts1 = [flat(v)[None, None] for v in parts1]
+        halves = ((0, 0, 2), (1, 0, 2), (2, 0, 2), (3, 0, 1), (3, 1, 1))
+        places = [(j, i, t, n, False) for i in (0, 1) for j, t, n in halves]
     else:
-        parts1 = [gather_plane(ffn_here, "ffn_w0")]
+        parts1 = [gather_plane(flat(jnp.stack([ffn_own, far_one])), "ffn_w0")]
     n2, parts1, ffn_g0 = both((n2, parts1, ffn_g0))
     reach_f0 = scatter_reach(ffn_g0, "ffn_g0")
     branch, gn2, upg0, *ffn_g1 = ffn_call(

time: 365 us -> 365 us (level)
  waiting for transfers between devices: 115 us -> 107 us
  local copies, waits for them, and re-layouts: 23 us -> 28.2 us
  starting transfers between devices: 74.2 us -> 78.4 us
    ppermute x55 -> x59, waiting for transfers between devices: 91.4 us -> 81.5 us  [swap(): return lax.ppermute(x, axis, [(i, i ^ bits) for i in range(n)])]
    ppermute x55 -> x59, starting transfers between devices: 65.8 us -> 70.5 us  [swap(): return lax.ppermute(x, axis, [(i, i ^ bits) for i in range(n)])]
    unnamed x174 -> x193, local copies, waits for them, and re-layouts: 6.42 us -> 9.65 us
  transfers between devices with their start and end apart: 63 -> 67, of which waited for: 26 -> 26; matrix products, arithmetic and copies ran while one was open for 13% -> 13% of each run, Pallas kernels for 31% -> 31%
where the time goes in v2:
time: 365 us; the launch traced here: 360 us
  Pallas kernels  110 us (30%)
  waiting for transfers between devices  107 us (29%)
  starting transfers between devices  78.4 us (21%)
  other arithmetic  33.9 us (9%)
  local copies, waits for them, and re-layouts  28.2 us (8%)
    ppermute x59, waiting for transfers between devices, swap(): return lax.ppermute(x, axis, [(i, i ^ bits) for i in range(n)])  81.5 us
    ppermute x59, starting transfers between devices, swap(): return lax.ppermute(x, axis, [(i, i ^ bits) for i in range(n)])  70.5 us
    pallas_call x2, Pallas kernels, ffn_call(): pl.pallas_call(functools.partial(ffn_kernel, parts, n_i, n_j, len(grads),...  45.3 us
    pallas_call x1, Pallas kernels, att_forward(): pl.pallas_call(functools.partial(att_fwd_kernel, parts, n_i), grid=(image...  19.7 us
    pallas_call x1, Pallas kernels, att_backward_last(): pl.pallas_call(functools.partial(att_bwd_last_kernel, parts, n_i, n_j, le...  19.3 us
    ppermute x4, waiting for transfers between devices, to_image(): return lax.ppermute(send, ('dp', 'mp'), image_routes(n_dp, n_mp, odd))  16.6 us
    convert_element_type x16, other arithmetic, add(): return total.astype(parts[0].dtype)  14.5 us
    pallas_call x1, Pallas kernels, att_backward_first(): pl.pallas_call(functools.partial(att_bwd_first_kernel, n_i, n_j, len(grad...  14.3 us
  transfers between devices with their start and end apart: 67, of which 26 were waited for; matrix products, arithmetic and copies ran while one was open for 13% of the time, Pallas kernels for 31%

profile of v2, /device:TPU:0, one launch (start us, length us, event | category | flops | bytes accessed | tf_op | source)
XLA Modules:
  0.0 360.1 jit_solution(1346268098723285931)
XLA Ops:
  7.7 3.1 collective-permute-start.1
  10.8 2.6 collective-permute-start.2
  13.8 1.6 collective-permute-start.8
  15.4 1.5 collective-permute-start.9
  16.9 6.3 %collective-permute-done.1 = bf16[1056,128]{1,0:T(8,128)(2,1)S(1)} collective-permute-done((bf16[1056,128]{1,0:T(8,128)(2,1)S(1)}, bf16[1056,128]{1,0:T(8,128)(2,1)S(1)}, u32[]{:S(2)}, u32[]{:S(2)}) %collective-permute-start.1) | collective-permute-done | bytes 270368 | tf_op jit(solution)/shard_map/att_w_z1/ppermute | solution.py:589
  23.2 2.5 collective-permute-done.2
  26.2 5.9 %collective-permute-done.5 = bf16[1056,128]{1,0:T(8,128)(2,1)S(1)} collective-permute-done((bf16[1056,128]{1,0:T(8,128)(2,1)S(1)}, bf16[1056,128]{1,0:T(8,128)(2,1)S(1)}, u32[]{:S(2)}, u32[]{:S(2)}) %collective-permute-start.5) | collective-permute-done | bytes 270368 | tf_op jit(solution)/shard_map/att_w_z3/ppermute | solution.py:589
  34.7 1.5 collective-permute-start.12
  36.3 2.2 collective-permute-start.4
  41.7 18.1 %collective-permute-done.4 = bf16[2,256,512]{2,1,0:T(8,128)(2,1)S(1)} collective-permute-done((bf16[2,256,512]{2,1,0:T(8,128)(2,1)}, bf16[2,256,512]{2,1,0:T(8,128)(2,1)S(1)}, u32[]{:S(2)}, u32[]{:S(2)}) %collective-permute-start.4) | collective-permute-done | bytes 524320 | tf_op jit(solution)/shard_map/ffn_w_z2/ppermute | solution.py:589
  63.1 1.5 collective-permute-start.11
  66.8 16.6 %collective-permute-done.7 = bf16[3,80,1024]{2,1,0:T(8,128)(2,1)S(1)} collective-permute-done((bf16[3,80,1024]{2,1,0:T(8,128)(2,1)S(1)}, bf16[3,80,1024]{2,1,0:T(8,128)(2,1)S(1)}, u32[]{:S(2)}, u32[]{:S(2)}) %collective-permute-start.7) | collective-permute-done | bytes 491552 | tf_op jit(solution)/shard_map/tokens_route1/ppermute | solution.py:697
  83.5 7.7 %collective-permute-start.17 = (bf16[3,2,80,1024]{3,2,1,0:T(8,128)(2,1)S(1)}, bf16[3,2,80,1024]{3,2,1,0:T(8,128)(2,1)S(1)}, u32[]{:S(2)}, u32[]{:S(2)}) collective-permute-start(bf16[3,2,80,1024]{3,2,1,0:T(8,128)(2,1)S(1)} %pad_maximum_fusion.6), channel_id=1, source_target_pairs={{0,4},{4,0},{8,12},{12,8},{16,20},{20,16},{24,28},{28,24},{1,5},{5... | collective-permute-start | bytes 2949128 | tf_op jit(solution)/shard_map/tokens_core/ppermute | solution.py:589
  96.7 1.9 collective-permute-start.21
  98.7 19.7 %att_forward.1 = (bf16[960,1024]{1,0:T(8,128)(2,1)}, bf16[6,960,128]{2,1,0:T(8,128)(2,1)}, bf16[6,960,128]{2,1,0:T(8,128)(2,1)}, bf16[960,256]{1,0:T(8,128)(2,1)...) custom-call(bf16[3,320,1024]{2,1,0:T(8,128)(2,1)} %bitcast.249, f32[1,1024]{1,0:T(1,128)S(1)} %get-tuple-element.450.g_ref, ...), custom_call_target="tpu_custom_call" | custom-call | flops 16000000000 | bytes 20000000 | tf_op jit(solution)/shard_map/att_forward/pallas_call | solution.py:179
  118.4 2.0 collective-permute-done.18
  120.7 2.2 collective-permute-start.26
  125.7 2.2 collective-permute-done.23
  129.6 8.4 %collective-permute-done.24 = bf16[1,512,512]{2,1,0:T(8,128)(2,1)S(1)} collective-permute-done((bf16[1,512,512]{2,1,0:T(8,128)(2,1)S(1)}, bf16[1,512,512]{2,1,0:T(8,128)(2,1)S(1)}, u32[]{:S(2)}, u32[]{:S(2)}) %collective-permute-start.24) | collective-permute-done | bytes 524320 | tf_op jit(solution)/shard_map/ffn_w2_y2/ppermute | solution.py:589
  141.4 22.9 %ffn_first.1 = (f32[960,1024]{1,0:T(8,128)}, bf16[960,1024]{1,0:T(8,128)(2,1)}, bf16[1024,960]{1,0:T(8,128)(2,1)}, bf16[1024,960]{1,0:T(8,128)(2,1)}, f32[960,10...) custom-call(bf16[960,1024]{1,0:T(8,128)(2,1)} %bitcast.250, ...), custom_call_target="tpu_custom_call" | custom-call | flops 24000000000 | bytes 30000000 | tf_op jit(solution)/shard_map/ffn_first/pallas_call | solution.py:350
  166.6 4.9 %collective-permute-done.29 = bf16[1,256,512]{2,1,0:T(8,128)(2,1)S(1)} collective-permute-done((bf16[1,256,512]{2,1,0:T(8,128)(2,1)S(1)}, bf16[1,256,512]{2,1,0:T(8,128)(2,1)S(1)}, u32[]{:S(2)}, u32[]{:S(2)}) %collective-permute-start.29) | collective-permute-done | bytes 262176 | tf_op jit(solution)/shard_map/ffn_w1_y2/ppermute | solution.py:589
  174.7 22.4 %ffn_last.1 = (bf16[960,1024]{1,0:T(8,128)(2,1)}, bf16[960,1024]{1,0:T(8,128)(2,1)}, f32[2,512]{1,0:T(2,128)}, bf16[2,2,256,512]{3,2,1,0:T(8,128)(2,1)}, bf16[2,...) custom-call(bf16[960,1024]{1,0:T(8,128)(2,1)} %get-tuple-element.244, ...), custom_call_target="tpu_custom_call" | custom-call | flops 24000000000 | bytes 30000000 | tf_op jit(solution)/shard_map/ffn_last/pallas_call | solution.py:350
  197.3 1.8 constant_dynamic-slice_fusion.37
  200.1 1.6 add_convert_fusion.7
  209.0 11.5 %hidden_backward.1 = (f32[960,1024]{1,0:T(8,128)}, bf16[1024,960]{1,0:T(8,128)(2,1)}, bf16[2,960,128]{2,1,0:T(8,128)(2,1)S(1)}, bf16[2,960,128]{2,1,0:T(8,128)(2,1)S(1)}, f32[8,1024]{1,0:T(8,128)S(1)}) custom-call(s32[5]{0:T(128)S(1)} %copy-done.7, f32[960,1024]{1,0:T(8,128)} %get-tuple-element.226.hid_ref, bf16[960,1024]{1,0:T(8,128)(2,1)} %get-tuple-element.268.ga_ref, ...), custom_call_target="tpu_custom_call" | custom-call | flops 10000000000 | bytes 20000000 | tf_op jit(solution)/shard_map/hidden_backward/pallas_call | solution.py:462
  221.4 1.8 fusion.18
  225.6 14.3 %att_backward_first.1 = (bf16[1024,960]{1,0:T(8,128)(2,1)}, bf16[960,768]{1,0:T(8,128)(2,1)S(1)}, f32[1,768]{1,0:T(1,128)S(1)}, bf16[2,4,256,128]{3,2,1,0:T(8,12...) custom-call(s32[5]{0:T(128)S(1)} %copy-done.7, ...), custom_call_target="tpu_custom_call" | custom-call | flops 16000000000 | bytes 20000000 | tf_op jit(solution)/shard_map/att_backward_first/pallas_call | solution.py:505
  240.1 8.5 %collective-permute-done.41 = bf16[3,80,1024]{2,1,0:T(8,128)(2,1)S(1)} collective-permute-done((bf16[3,80,1024]{2,1,0:T(8,128)(2,1)S(1)}, bf16[3,80,1024]{2,1,0:T(8,128)(2,1)S(1)}, u32[]{:S(2)}, u32[]{:S(2)}) %collective-permute-start.41) | collective-permute-done | bytes 491552 | tf_op jit(solution)/shard_map/block_out_route1/ppermute | solution.py:704
  249.8 1.8 collective-permute-start.42
  253.3 19.3 %att_backward_last.1 = (bf16[960,1024]{1,0:T(8,128)(2,1)}, f32[1,768]{1,0:T(1,128)}, f32[8,1024]{1,0:T(8,128)}, bf16[2,4,256,128]{3,2,1,0:T(8,128)(2,1)}, bf16[2...) custom-call(s32[5]{0:T(128)} %copy-done.6, ...), custom_call_target="tpu_custom_call" | custom-call | flops 20000000000 | bytes 30000000 | tf_op jit(solution)/shard_map/att_backward_last/pallas_call | solution.py:563
  272.7 2.9 collective-permute-done.45
  275.6 2.0 constant_dynamic-slice_fusion.31
  281.6 1.9 collective-permute-start.47
  284.4 2.3 fusion.13
  286.7 2.1 fusion.8
  293.6 2.4 collective-permute-done.47
  304.9 1.6 collective-permute-start.51
  306.7 3.3 collective-permute-done.55
  311.4 1.6 collective-permute-start.57
  313.1 3.7 %collective-permute-start.56 = (bf16[4,256,128]{2,1,0:T(8,128)(2,1)S(1)}, bf16[4,256,128]{2,1,0:T(8,128)(2,1)S(1)}, u32[]{:S(2)}, u32[]{:S(2)}) collective-permute-start(bf16[4,256,128]{2,1,0:T(8,128)(2,1)S(1)} %fusion.25), channel_id=1, source_target_pairs={{0,1},{1,0},{2,3},{3,2},{4,5},{5,4},{6,7},{7,6},{8,9},{9,8},{10,11... | collective-permute-start | bytes 786440 | tf_op jit(solution)/shard_map/att_g_z3/ppermute | solution.py:589
  319.4 2.8 collective-permute-done.58
  322.3 6.6 %collective-permute-done.56 = bf16[4,256,128]{2,1,0:T(8,128)(2,1)S(1)} collective-permute-done((bf16[4,256,128]{2,1,0:T(8,128)(2,1)S(1)}, bf16[4,256,128]{2,1,0:T(8,128)(2,1)S(1)}, u32[]{:S(2)}, u32[]{:S(2)}) %collective-permute-start.56) | collective-permute-done | bytes 262176 | tf_op jit(solution)/shard_map/att_g_z3/ppermute | solution.py:589
  330.4 2.1 collective-permute-start.66
  332.5 1.8 fusion.21
  334.3 3.9 %collective-permute-start.64 = (bf16[4,256,128]{2,1,0:T(8,128)(2,1)}, bf16[4,256,128]{2,1,0:T(8,128)(2,1)S(1)}, u32[]{:S(2)}, u32[]{:S(2)}) collective-permute-start(bf16[4,256,128]{2,1,0:T(8,128)(2,1)} %fusion.21), channel_id=1, source_target_pairs={{0,2},{1,3},{2,0},{3,1},{4,6},{5,7},{6,4},{7,5},{8,10},{9,11},{10,... | collective-permute-start | bytes 786440 | tf_op jit(solution)/shard_map/att_g_z2/ppermute | solution.py:589
  341.6 5.0 %collective-permute-done.61 = f32[176,128]{1,0:T(8,128)S(1)} collective-permute-done((f32[176,128]{1,0:T(8,128)S(1)}, f32[176,128]{1,0:T(8,128)S(1)}, u32[]{:S(2)}, u32[]{:S(2)}) %collective-permute-start.61) | collective-permute-done | bytes 90144 | tf_op jit(solution)/shard_map/sums_z1/ppermute | solution.py:589
  346.7 1.6 collective-permute-start.62
  352.5 2.4 collective-permute-done.62
  (438 shorter events, 89.1 us)
Async XLA Ops:
  7.7 15.5 %collective-permute-start.1 = (bf16[1056,128]{1,0:T(8,128)(2,1)S(1)}, bf16[1056,128]{1,0:T(8,128)(2,1)S(1)}, u32[]{:S(2)}, u32[]{:S(2)}) collective-permute-start(bf16[1056,128]{1,0:T(8,128)(2,1)S(1)} %get-tuple-element.422), channel_id=1, source_target_pairs={{0,1},{1,0},{2,3},{3,2},{4,5},{5,4},{6,7},{7,6},{8,9},{9,8},{10,11... | collective-permute-start | bytes 811016 | tf_op jit(solution)/shard_map/att_w_z1/ppermute | solution.py:589
  10.8 14.9 %collective-permute-start.2 = (bf16[1056,128]{1,0:T(8,128)(2,1)S(1)}, bf16[1056,128]{1,0:T(8,128)(2,1)S(1)}, u32[]{:S(2)}, u32[]{:S(2)}) collective-permute-start(bf16[1056,128]{1,0:T(8,128)(2,1)S(1)} %get-tuple-element.422), channel_id=1, source_target_pairs={{0,2},{1,3},{2,0},{3,1},{4,6},{5,7},{6,4},{7,5},{8,10},{9,11},{10,... | collective-permute-start | bytes 811016 | tf_op jit(solution)/shard_map/att_w_z2/ppermute | solution.py:589
  13.8 18.6 %collective-permute-start.8 = (bf16[2,256,512]{2,1,0:T(8,128)(2,1)S(1)}, bf16[2,256,512]{2,1,0:T(8,128)(2,1)S(1)}, u32[]{:S(2)}, u32[]{:S(2)}) collective-permute-start(bf16[2,256,512]{2,1,0:T(8,128)(2,1)S(1)} %bitcast.281), channel_id=1, source_target_pairs={{0,8},{4,12},{8,0},{12,4},{16,24},{20,28},{24,16},{28,20},{1,9},{5... | collective-permute-start | bytes 1572872 | tf_op jit(solution)/shard_map/ffn_w0_x1/ppermute | solution.py:589
  15.4 17.0 %collective-permute-start.9 = (bf16[2,256,512]{2,1,0:T(8,128)(2,1)S(1)}, bf16[2,256,512]{2,1,0:T(8,128)(2,1)}, u32[]{:S(2)}, u32[]{:S(2)}) collective-permute-start(bf16[2,256,512]{2,1,0:T(8,128)(2,1)S(1)} %bitcast.282), channel_id=1, source_target_pairs={{0,16},{4,20},{8,24},{12,28},{16,0},{20,4},{24,8},{28,12},{1,17},{... | collective-permute-start | bytes 1572872 | tf_op jit(solution)/shard_map/ffn_w0_y1/ppermute | solution.py:589
  33.2 27.4 %collective-permute-start.10 = (bf16[4,1056,128]{2,1,0:T(8,128)(2,1)S(1)}, bf16[4,1056,128]{2,1,0:T(8,128)(2,1)S(1)}, u32[]{:S(2)}, u32[]{:S(2)}) collective-permute-start(bf16[4,1056,128]{2,1,0:T(8,128)(2,1)S(1)} %get-tuple-element.195), channel_id=1, source_target_pairs={{0,8},{4,12},{8,0},{12,4},{16,24},{20,28},{24,16},{28,20},{1,9},{5... | collective-permute-start | bytes 3244040 | tf_op jit(solution)/shard_map/att_w_x1/ppermute | solution.py:589
  34.7 26.6 %collective-permute-start.12 = (bf16[4,1056,128]{2,1,0:T(8,128)(2,1)S(1)}, bf16[4,1056,128]{2,1,0:T(8,128)(2,1)S(1)}, u32[]{:S(2)}, u32[]{:S(2)}) collective-permute-start(bf16[4,1056,128]{2,1,0:T(8,128)(2,1)S(1)} %get-tuple-element.195), channel_id=1, source_target_pairs={{0,16},{4,20},{8,24},{12,28},{16,0},{20,4},{24,8},{28,12},{1,17},{... | collective-permute-start | bytes 3244040 | tf_op jit(solution)/shard_map/att_w_y1/ppermute | solution.py:589
  36.3 23.5 %collective-permute-start.4 = (bf16[2,256,512]{2,1,0:T(8,128)(2,1)}, bf16[2,256,512]{2,1,0:T(8,128)(2,1)S(1)}, u32[]{:S(2)}, u32[]{:S(2)}) collective-permute-start(bf16[2,256,512]{2,1,0:T(8,128)(2,1)} %bitcast.283), channel_id=1, source_target_pairs={{0,2},{1,3},{2,0},{3,1},{4,6},{5,7},{6,4},{7,5},{8,10},{9,11},{10,... | collective-permute-start | bytes 1572872 | tf_op jit(solution)/shard_map/ffn_w_z2/ppermute | solution.py:589
  39.5 23.7 %collective-permute-start.15 = (bf16[1,256,512]{2,1,0:T(8,128)(2,1)S(1)}, bf16[1,256,512]{2,1,0:T(8,128)(2,1)S(1)}, u32[]{:S(2)}, u32[]{:S(2)}) collective-permute-start(bf16[1,256,512]{2,1,0:T(8,128)(2,1)S(1)} %slice.332), channel_id=1, source_target_pairs={{0,16},{4,20},{8,24},{12,28},{16,0},{20,4},{24,8},{28,12},{1,17},{... | collective-permute-start | bytes 786440 | tf_op jit(solution)/shard_map/ffn_w0_y2/ppermute | solution.py:589
  41.0 23.6 %collective-permute-start.16 = (bf16[1,256,512]{2,1,0:T(8,128)(2,1)S(1)}, bf16[1,256,512]{2,1,0:T(8,128)(2,1)S(1)}, u32[]{:S(2)}, u32[]{:S(2)}) collective-permute-start(bf16[1,256,512]{2,1,0:T(8,128)(2,1)S(1)} %slice.333), channel_id=1, source_target_pairs={{0,8},{4,12},{8,0},{12,4},{16,24},{20,28},{24,16},{28,20},{1,9},{5... | collective-permute-start | bytes 786440 | tf_op jit(solution)/shard_map/ffn_w0_x2/ppermute | solution.py:589
  59.7 23.7 %collective-permute-start.14 = (bf16[2,256,512]{2,1,0:T(8,128)(2,1)S(1)}, bf16[2,256,512]{2,1,0:T(8,128)(2,1)S(1)}, u32[]{:S(2)}, u32[]{:S(2)}) collective-permute-start(bf16[2,256,512]{2,1,0:T(8,128)(2,1)S(1)} %collective-permute-done.4), channel_id=1, source_target_pairs={{0,1},{1,0},{2,3},{3,2},{4,5},{5,4},{6,7},{7,6},{8,9},{9,8},{10,11... | collective-permute-start | bytes 1572872 | tf_op jit(solution)/shard_map/ffn_w_z3/ppermute | solution.py:589
  61.3 22.1 %collective-permute-start.7 = (bf16[3,80,1024]{2,1,0:T(8,128)(2,1)S(1)}, bf16[3,80,1024]{2,1,0:T(8,128)(2,1)S(1)}, u32[]{:S(2)}, u32[]{:S(2)}) collective-permute-start(bf16[3,80,1024]{2,1,0:T(8,128)(2,1)S(1)} %copy-done.55), channel_id=1, source_target_pairs={{1,0},{0,1},{7,2},{6,3},{3,4},{2,5},{5,6},{4,7},{9,8},{8,9},{15,10... | collective-permute-start | bytes 1474568 | tf_op jit(solution)/shard_map/tokens_route1/ppermute | solution.py:697
  63.1 20.3 %collective-permute-start.11 = (bf16[2,1056,128]{2,1,0:T(8,128)(2,1)S(1)}, bf16[2,1056,128]{2,1,0:T(8,128)(2,1)S(1)}, u32[]{:S(2)}, u32[]{:S(2)}) collective-permute-start(bf16[2,1056,128]{2,1,0:T(8,128)(2,1)S(1)} %slice.330), channel_id=1, source_target_pairs={{0,16},{4,20},{8,24},{12,28},{16,0},{20,4},{24,8},{28,12},{1,17},{... | collective-permute-start | bytes 1622024 | tf_op jit(solution)/shard_map/att_w_y2/ppermute | solution.py:589
  65.3 18.1 %collective-permute-start.13 = (bf16[2,1056,128]{2,1,0:T(8,128)(2,1)S(1)}, bf16[2,1056,128]{2,1,0:T(8,128)(2,1)S(1)}, u32[]{:S(2)}, u32[]{:S(2)}) collective-permute-start(bf16[2,1056,128]{2,1,0:T(8,128)(2,1)S(1)} %slice.331), channel_id=1, source_target_pairs={{0,8},{4,12},{8,0},{12,4},{16,24},{20,28},{24,16},{28,20},{1,9},{5... | collective-permute-start | bytes 1622024 | tf_op jit(solution)/shard_map/att_w_x2/ppermute | solution.py:589
  83.5 9.9 %collective-permute-start.17 = (bf16[3,2,80,1024]{3,2,1,0:T(8,128)(2,1)S(1)}, bf16[3,2,80,1024]{3,2,1,0:T(8,128)(2,1)S(1)}, u32[]{:S(2)}, u32[]{:S(2)}) collective-permute-start(bf16[3,2,80,1024]{3,2,1,0:T(8,128)(2,1)S(1)} %pad_maximum_fusion.6), channel_id=1, source_target_pairs={{0,4},{4,0},{8,12},{12,8},{16,20},{20,16},{24,28},{28,24},{1,5},{5... | collective-permute-start | bytes 2949128 | tf_op jit(solution)/shard_map/tokens_core/ppermute | solution.py:589
  92.6 25.8 %collective-permute-start.22 = (bf16[2,256,512]{2,1,0:T(8,128)(2,1)S(1)}, bf16[2,256,512]{2,1,0:T(8,128)(2,1)S(1)}, u32[]{:S(2)}, u32[]{:S(2)}) collective-permute-start(bf16[2,256,512]{2,1,0:T(8,128)(2,1)S(1)} %bitcast.285), channel_id=1, source_target_pairs={{0,1},{1,0},{2,3},{3,2},{4,5},{5,4},{6,7},{7,6},{8,9},{9,8},{10,11... | collective-permute-start | bytes 1572872 | tf_op jit(solution)/shard_map/ffn_w_z1/ppermute | solution.py:589
  95.0 25.4 %collective-permute-start.18 = (bf16[2,512,512]{2,1,0:T(8,128)(2,1)S(1)}, bf16[2,512,512]{2,1,0:T(8,128)(2,1)S(1)}, u32[]{:S(2)}, u32[]{:S(2)}) collective-permute-start(bf16[2,512,512]{2,1,0:T(8,128)(2,1)S(1)} %pad_maximum_fusion.3), channel_id=1, source_target_pairs={{0,8},{4,12},{8,0},{12,4},{16,24},{20,28},{24,16},{28,20},{1,9},{5... | collective-permute-start | bytes 3145736 | tf_op jit(solution)/shard_map/ffn_w2_x1/ppermute | solution.py:589
  95.5 25.1 %collective-permute-start.19 = (bf16[2,512,512]{2,1,0:T(8,128)(2,1)S(1)}, bf16[2,512,512]{2,1,0:T(8,128)(2,1)S(1)}, u32[]{:S(2)}, u32[]{:S(2)}) collective-permute-start(bf16[2,512,512]{2,1,0:T(8,128)(2,1)S(1)} %pad_maximum_fusion.3), channel_id=1, source_target_pairs={{0,16},{4,20},{8,24},{12,28},{16,0},{20,4},{24,8},{28,12},{1,17},{... | collective-permute-start | bytes 3145736 | tf_op jit(solution)/shard_map/ffn_w2_y1/ppermute | solution.py:589
  96.0 22.4 %collective-permute-start.20 = (bf16[3,80,1024]{2,1,0:T(8,128)(2,1)S(1)}, bf16[3,80,1024]{2,1,0:T(8,128)(2,1)S(1)}, u32[]{:S(2)}, u32[]{:S(2)}) collective-permute-start(bf16[3,80,1024]{2,1,0:T(8,128)(2,1)S(1)} %get-tuple-element.209), channel_id=1, source_target_pairs={{0,0},{1,1},{6,2},{7,3},{2,4},{3,5},{4,6},{5,7},{8,8},{9,9},{14,10... | collective-permute-start | bytes 1474568 | tf_op jit(solution)/shard_map/cotangent_route0/ppermute | solution.py:697
  96.7 21.7 %collective-permute-start.21 = (bf16[3,80,1024]{2,1,0:T(8,128)(2,1)S(1)}, bf16[3,80,1024]{2,1,0:T(8,128)(2,1)S(1)}, u32[]{:S(2)}, u32[]{:S(2)}) collective-permute-start(bf16[3,80,1024]{2,1,0:T(8,128)(2,1)S(1)} %get-tuple-element.210), channel_id=1, source_target_pairs={{1,0},{0,1},{7,2},{6,3},{3,4},{2,5},{5,6},{4,7},{9,8},{8,9},{15,10... | collective-permute-start | bytes 1474568 | tf_op jit(solution)/shard_map/cotangent_route1/ppermute | solution.py:697
  120.7 17.9 %collective-permute-start.26 = (bf16[960,1024]{1,0:T(8,128)(2,1)}, bf16[960,1024]{1,0:T(8,128)(2,1)S(1)}, u32[]{:S(2)}, u32[]{:S(2)}) collective-permute-start(bf16[960,1024]{1,0:T(8,128)(2,1)} %get-tuple-element.213.refs_1_), channel_id=1, source_target_pairs={{0,4},{4,0},{8,12},{12,8},{16,20},{20,16},{24,28},{28,24},{1,5},{5... | collective-permute-start | bytes 5898248 | tf_op jit(solution)/shard_map/attended/ppermute | solution.py:589
  123.7 14.4 %collective-permute-start.24 = (bf16[1,512,512]{2,1,0:T(8,128)(2,1)S(1)}, bf16[1,512,512]{2,1,0:T(8,128)(2,1)S(1)}, u32[]{:S(2)}, u32[]{:S(2)}) collective-permute-start(bf16[1,512,512]{2,1,0:T(8,128)(2,1)S(1)} %slice.263), channel_id=1, source_target_pairs={{0,16},{4,20},{8,24},{12,28},{16,0},{20,4},{24,8},{28,12},{1,17},{... | collective-permute-start | bytes 1572872 | tf_op jit(solution)/shard_map/ffn_w2_y2/ppermute | solution.py:589
  124.5 14.1 %collective-permute-start.25 = (bf16[1,512,512]{2,1,0:T(8,128)(2,1)S(1)}, bf16[1,512,512]{2,1,0:T(8,128)(2,1)S(1)}, u32[]{:S(2)}, u32[]{:S(2)}) collective-permute-start(bf16[1,512,512]{2,1,0:T(8,128)(2,1)S(1)} %slice.264), channel_id=1, source_target_pairs={{0,8},{4,12},{8,0},{12,4},{16,24},{20,28},{24,16},{28,20},{1,9},{5... | collective-permute-start | bytes 1572872 | tf_op jit(solution)/shard_map/ffn_w2_x2/ppermute | solution.py:589
  139.3 25.0 %collective-permute-start.27 = (bf16[2,256,512]{2,1,0:T(8,128)(2,1)S(1)}, bf16[2,256,512]{2,1,0:T(8,128)(2,1)S(1)}, u32[]{:S(2)}, u32[]{:S(2)}) collective-permute-start(bf16[2,256,512]{2,1,0:T(8,128)(2,1)S(1)} %copy-done.83), channel_id=1, source_target_pairs={{0,8},{4,12},{8,0},{12,4},{16,24},{20,28},{24,16},{28,20},{1,9},{5... | collective-permute-start | bytes 1572872 | tf_op jit(solution)/shard_map/ffn_w1_x1/ppermute | solution.py:589
  140.1 24.2 %collective-permute-start.28 = (bf16[2,256,512]{2,1,0:T(8,128)(2,1)S(1)}, bf16[2,256,512]{2,1,0:T(8,128)(2,1)S(1)}, u32[]{:S(2)}, u32[]{:S(2)}) collective-permute-start(bf16[2,256,512]{2,1,0:T(8,128)(2,1)S(1)} %copy-done.83), channel_id=1, source_target_pairs={{0,16},{4,20},{8,24},{12,28},{16,0},{20,4},{24,8},{28,12},{1,17},{... | collective-permute-start | bytes 1572872 | tf_op jit(solution)/shard_map/ffn_w1_y1/ppermute | solution.py:589
  172.3 24.8 %collective-permute-start.31 = (bf16[2,2,256,512]{3,2,1,0:T(8,128)(2,1)}, bf16[2,2,256,512]{3,2,1,0:T(8,128)(2,1)}, u32[]{:S(2)}, u32[]{:S(2)}) collective-permute-start(bf16[2,2,256,512]{3,2,1,0:T(8,128)(2,1)} %get-tuple-element.266), channel_id=1, source_target_pairs={{0,8},{4,12},{8,0},{12,4},{16,24},{20,28},{24,16},{28,20},{1,9},{5... | collective-permute-start | bytes 3145736 | tf_op jit(solution)/shard_map/ffn_g0_x1/ppermute | solution.py:589
  173.3 23.9 %collective-permute-start.32 = (bf16[2,2,256,512]{3,2,1,0:T(8,128)(2,1)}, bf16[2,2,256,512]{3,2,1,0:T(8,128)(2,1)}, u32[]{:S(2)}, u32[]{:S(2)}) collective-permute-start(bf16[2,2,256,512]{3,2,1,0:T(8,128)(2,1)} %get-tuple-element.267), channel_id=1, source_target_pairs={{0,16},{4,20},{8,24},{12,28},{16,0},{20,4},{24,8},{28,12},{1,17},{... | collective-permute-start | bytes 3145736 | tf_op jit(solution)/shard_map/ffn_g0_y1/ppermute | solution.py:589
  197.2 9.9 %collective-permute-start.33 = (bf16[960,1024]{1,0:T(8,128)(2,1)}, bf16[960,1024]{1,0:T(8,128)(2,1)}, u32[]{:S(2)}, u32[]{:S(2)}) collective-permute-start(bf16[960,1024]{1,0:T(8,128)(2,1)} %get-tuple-element.268.ga_ref), channel_id=1, source_target_pairs={{0,4},{4,0},{8,12},{12,8},{16,20},{20,16},{24,28},{28,24},{1,5},{5... | collective-permute-start | bytes 5898248 | tf_op jit(solution)/shard_map/grad_norm_two/ppermute | solution.py:589
  201.6 18.9 %collective-permute-start.36 = (bf16[1,2,256,512]{3,2,1,0:T(8,128)(2,1)S(1)}, bf16[1,2,256,512]{3,2,1,0:T(8,128)(2,1)S(1)}, u32[]{:S(2)}, u32[]{:S(2)}) collective-permute-start(bf16[1,2,256,512]{3,2,1,0:T(8,128)(2,1)S(1)} %add_convert_fusion.7), channel_id=1, source_target_pairs={{0,16},{4,20},{8,24},{12,28},{16,0},{20,4},{24,8},{28,12},{1,17},{... | collective-permute-start | bytes 1572872 | tf_op jit(solution)/shard_map/ffn_g0_y2/ppermute | solution.py:589
  203.5 17.0 %collective-permute-start.35 = (bf16[1,2,256,512]{3,2,1,0:T(8,128)(2,1)S(1)}, bf16[1,2,256,512]{3,2,1,0:T(8,128)(2,1)S(1)}, u32[]{:S(2)}, u32[]{:S(2)}) collective-permute-start(bf16[1,2,256,512]{3,2,1,0:T(8,128)(2,1)S(1)} %add_convert_fusion.8), channel_id=1, source_target_pairs={{0,8},{4,12},{8,0},{12,4},{16,24},{20,28},{24,16},{28,20},{1,9},{5... | collective-permute-start | bytes 1572872 | tf_op jit(solution)/shard_map/ffn_g0_x2/ppermute | solution.py:589
  204.6 35.5 %collective-permute-start.38 = (bf16[2,2,256,512]{3,2,1,0:T(8,128)(2,1)}, bf16[2,2,256,512]{3,2,1,0:T(8,128)(2,1)S(1)}, u32[]{:S(2)}, u32[]{:S(2)}) collective-permute-start(bf16[2,2,256,512]{3,2,1,0:T(8,128)(2,1)} %get-tuple-element.289), channel_id=1, source_target_pairs={{0,8},{4,12},{8,0},{12,4},{16,24},{20,28},{24,16},{28,20},{1,9},{5... | collective-permute-start | bytes 3145736 | tf_op jit(solution)/shard_map/ffn_g1_x1/ppermute | solution.py:589
  205.6 34.5 %collective-permute-start.39 = (bf16[2,2,256,512]{3,2,1,0:T(8,128)(2,1)S(1)}, bf16[2,2,256,512]{3,2,1,0:T(8,128)(2,1)S(1)}, u32[]{:S(2)}, u32[]{:S(2)}) collective-permute-start(bf16[2,2,256,512]{3,2,1,0:T(8,128)(2,1)S(1)} %copy-done.81), channel_id=1, source_target_pairs={{0,16},{4,20},{8,24},{12,28},{16,0},{20,4},{24,8},{28,12},{1,17},{... | collective-permute-start | bytes 3145736 | tf_op jit(solution)/shard_map/ffn_g1_y1/ppermute | solution.py:589
  207.9 12.6 %collective-permute-start.37 = (bf16[3,80,1024]{2,1,0:T(8,128)(2,1)S(1)}, bf16[3,80,1024]{2,1,0:T(8,128)(2,1)S(1)}, u32[]{:S(2)}, u32[]{:S(2)}) collective-permute-start(bf16[3,80,1024]{2,1,0:T(8,128)(2,1)S(1)} %slice_bitcast_fusion.3), channel_id=1, source_target_pairs={{0,0},{1,1},{2,6},{3,7},{4,2},{5,3},{6,4},{7,5},{8,8},{9,9},{10,14... | collective-permute-start | bytes 1474568 | tf_op jit(solution)/shard_map/block_out_route0/ppermute | solution.py:704
  223.2 25.4 %collective-permute-start.40 = (bf16[2,256,512]{2,1,0:T(8,128)(2,1)S(1)}, bf16[2,256,512]{2,1,0:T(8,128)(2,1)S(1)}, u32[]{:S(2)}, u32[]{:S(2)}) collective-permute-start(bf16[2,256,512]{2,1,0:T(8,128)(2,1)S(1)} %get-tuple-element.385), channel_id=1, source_target_pairs={{0,1},{1,0},{2,3},{3,2},{4,5},{5,4},{6,7},{7,6},{8,9},{9,8},{10,11... | collective-permute-start | bytes 1572872 | tf_op jit(solution)/shard_map/ffn_g_z3/ppermute | solution.py:589
  224.1 24.5 %collective-permute-start.41 = (bf16[3,80,1024]{2,1,0:T(8,128)(2,1)S(1)}, bf16[3,80,1024]{2,1,0:T(8,128)(2,1)S(1)}, u32[]{:S(2)}, u32[]{:S(2)}) collective-permute-start(bf16[3,80,1024]{2,1,0:T(8,128)(2,1)S(1)} %slice_bitcast_fusion.2), channel_id=1, source_target_pairs={{0,1},{1,0},{2,7},{3,6},{4,3},{5,2},{6,5},{7,4},{8,9},{9,8},{10,15... | collective-permute-start | bytes 1474568 | tf_op jit(solution)/shard_map/block_out_route1/ppermute | solution.py:704
  248.7 23.9 %collective-permute-start.44 = (bf16[2,256,512]{2,1,0:T(8,128)(2,1)S(1)}, bf16[2,256,512]{2,1,0:T(8,128)(2,1)S(1)}, u32[]{:S(2)}, u32[]{:S(2)}) collective-permute-start(bf16[2,256,512]{2,1,0:T(8,128)(2,1)S(1)} %add_convert_fusion.2), channel_id=1, source_target_pairs={{0,2},{1,3},{2,0},{3,1},{4,6},{5,7},{6,4},{7,5},{8,10},{9,11},{10,... | collective-permute-start | bytes 1572872 | tf_op jit(solution)/shard_map/ffn_g_z2/ppermute | solution.py:589
  248.9 23.7 %collective-permute-start.43 = (bf16[1,2,256,512]{3,2,1,0:T(8,128)(2,1)S(1)}, bf16[1,2,256,512]{3,2,1,0:T(8,128)(2,1)S(1)}, u32[]{:S(2)}, u32[]{:S(2)}) collective-permute-start(bf16[1,2,256,512]{3,2,1,0:T(8,128)(2,1)S(1)} %add_convert_fusion.3), channel_id=1, source_target_pairs={{0,16},{4,20},{8,24},{12,28},{16,0},{20,4},{24,8},{28,12},{1,17},{... | collective-permute-start | bytes 1572872 | tf_op jit(solution)/shard_map/ffn_g1_y2/ppermute | solution.py:589
  249.8 22.9 %collective-permute-start.42 = (bf16[1,2,256,512]{3,2,1,0:T(8,128)(2,1)S(1)}, bf16[1,2,256,512]{3,2,1,0:T(8,128)(2,1)S(1)}, u32[]{:S(2)}, u32[]{:S(2)}) collective-permute-start(bf16[1,2,256,512]{3,2,1,0:T(8,128)(2,1)S(1)} %add_convert_fusion.4), channel_id=1, source_target_pairs={{0,8},{4,12},{8,0},{12,4},{16,24},{20,28},{24,16},{28,20},{1,9},{5... | collective-permute-start | bytes 1572872 | tf_op jit(solution)/shard_map/ffn_g1_x2/ppermute | solution.py:589
  251.6 24.0 %collective-permute-start.45 = (bf16[2,4,256,128]{3,2,1,0:T(8,128)(2,1)S(1)}, bf16[2,4,256,128]{3,2,1,0:T(8,128)(2,1)S(1)}, u32[]{:S(2)}, u32[]{:S(2)}) collective-permute-start(bf16[2,4,256,128]{3,2,1,0:T(8,128)(2,1)S(1)} %get-tuple-element.317), channel_id=1, source_target_pairs={{0,8},{4,12},{8,0},{12,4},{16,24},{20,28},{24,16},{28,20},{1,9},{5... | collective-permute-start | bytes 1572872 | tf_op jit(solution)/shard_map/att_ga_x1/ppermute | solution.py:589
  251.9 23.7 %collective-permute-start.46 = (bf16[2,4,256,128]{3,2,1,0:T(8,128)(2,1)S(1)}, bf16[2,4,256,128]{3,2,1,0:T(8,128)(2,1)S(1)}, u32[]{:S(2)}, u32[]{:S(2)}) collective-permute-start(bf16[2,4,256,128]{3,2,1,0:T(8,128)(2,1)S(1)} %get-tuple-element.318), channel_id=1, source_target_pairs={{0,16},{4,20},{8,24},{12,28},{16,0},{20,4},{24,8},{28,12},{1,17},{... | collective-permute-start | bytes 1572872 | tf_op jit(solution)/shard_map/att_ga_y1/ppermute | solution.py:589
  281.6 14.4 %collective-permute-start.47 = (bf16[2,4,256,128]{3,2,1,0:T(8,128)(2,1)S(1)}, bf16[2,4,256,128]{3,2,1,0:T(8,128)(2,1)S(1)}, u32[]{:S(2)}, u32[]{:S(2)}) collective-permute-start(bf16[2,4,256,128]{3,2,1,0:T(8,128)(2,1)S(1)} %copy-done.85), channel_id=1, source_target_pairs={{0,8},{4,12},{8,0},{12,4},{16,24},{20,28},{24,16},{28,20},{1,9},{5... | collective-permute-start | bytes 1572872 | tf_op jit(solution)/shard_map/att_gb_x1/ppermute | solution.py:589
  283.5 13.9 %collective-permute-start.48 = (bf16[2,4,256,128]{3,2,1,0:T(8,128)(2,1)S(1)}, bf16[2,4,256,128]{3,2,1,0:T(8,128)(2,1)S(1)}, u32[]{:S(2)}, u32[]{:S(2)}) collective-permute-start(bf16[2,4,256,128]{3,2,1,0:T(8,128)(2,1)S(1)} %copy-done.84), channel_id=1, source_target_pairs={{0,16},{4,20},{8,24},{12,28},{16,0},{20,4},{24,8},{28,12},{1,17},{... | collective-permute-start | bytes 1572872 | tf_op jit(solution)/shard_map/att_gb_y1/ppermute | solution.py:589
  292.1 17.8 %collective-permute-start.55 = (bf16[2,256,512]{2,1,0:T(8,128)(2,1)}, bf16[2,256,512]{2,1,0:T(8,128)(2,1)}, u32[]{:S(2)}, u32[]{:S(2)}) collective-permute-start(bf16[2,256,512]{2,1,0:T(8,128)(2,1)} %fusion.19), channel_id=1, source_target_pairs={{0,1},{1,0},{2,3},{3,2},{4,5},{5,4},{6,7},{7,6},{8,9},{9,8},{10,11... | collective-permute-start | bytes 1572872 | tf_op jit(solution)/shard_map/ffn_g_z1/ppermute | solution.py:589
  300.0 10.0 %collective-permute-start.54 = (bf16[1,4,256,128]{3,2,1,0:T(8,128)(2,1)S(1)}, bf16[1,4,256,128]{3,2,1,0:T(8,128)(2,1)S(1)}, u32[]{:S(2)}, u32[]{:S(2)}) collective-permute-start(bf16[1,4,256,128]{3,2,1,0:T(8,128)(2,1)S(1)} %add_convert_fusion.13), channel_id=1, source_target_pairs={{0,16},{4,20},{8,24},{12,28},{16,0},{20,4},{24,8},{28,12},{1,17},{... | collective-permute-start | bytes 786440 | tf_op jit(solution)/shard_map/att_ga_y2/ppermute | solution.py:589
  310.0 12.3 %collective-permute-start.59 = (bf16[3,80,1024]{2,1,0:T(8,128)(2,1)S(1)}, bf16[3,80,1024]{2,1,0:T(8,128)(2,1)S(1)}, u32[]{:S(2)}, u32[]{:S(2)}) collective-permute-start(bf16[3,80,1024]{2,1,0:T(8,128)(2,1)S(1)} %slice_bitcast_fusion.1), channel_id=1, source_target_pairs={{0,1},{1,0},{2,7},{3,6},{4,3},{5,2},{6,5},{7,4},{8,9},{9,8},{10,15... | collective-permute-start | bytes 1474568 | tf_op jit(solution)/shard_map/input_grad_route1/ppermute | solution.py:704
  313.1 15.8 %collective-permute-start.56 = (bf16[4,256,128]{2,1,0:T(8,128)(2,1)S(1)}, bf16[4,256,128]{2,1,0:T(8,128)(2,1)S(1)}, u32[]{:S(2)}, u32[]{:S(2)}) collective-permute-start(bf16[4,256,128]{2,1,0:T(8,128)(2,1)S(1)} %fusion.25), channel_id=1, source_target_pairs={{0,1},{1,0},{2,3},{3,2},{4,5},{5,4},{6,7},{7,6},{8,9},{9,8},{10,11... | collective-permute-start | bytes 786440 | tf_op jit(solution)/shard_map/att_g_z3/ppermute | solution.py:589
  317.6 33.6 %collective-permute-start.63 = (bf16[4,256,128]{2,1,0:T(8,128)(2,1)}, bf16[4,256,128]{2,1,0:T(8,128)(2,1)}, u32[]{:S(2)}, u32[]{:S(2)}) collective-permute-start(bf16[4,256,128]{2,1,0:T(8,128)(2,1)} %fusion.27), channel_id=1, source_target_pairs={{0,1},{1,0},{2,3},{3,2},{4,5},{5,4},{6,7},{7,6},{8,9},{9,8},{10,11... | collective-permute-start | bytes 786440 | tf_op jit(solution)/shard_map/att_g_z1/ppermute | solution.py:589
  330.4 17.8 %collective-permute-start.66 = (bf16[2,128,512]{1,2,0:T(8,128)(2,1)}, bf16[2,128,512]{1,2,0:T(8,128)(2,1)}, u32[]{:S(2)}, u32[]{:S(2)}) collective-permute-start(bf16[2,128,512]{1,2,0:T(8,128)(2,1)} %bitcast.132), channel_id=1, source_target_pairs={{0,4},{4,0},{8,12},{12,8},{16,20},{20,16},{24,28},{28,24},{1,5},{5... | collective-permute-start | bytes 786440 | tf_op jit(solution)/shard_map/ffn_g_core/ppermute | solution.py:589
  334.3 16.9 %collective-permute-start.64 = (bf16[4,256,128]{2,1,0:T(8,128)(2,1)}, bf16[4,256,128]{2,1,0:T(8,128)(2,1)S(1)}, u32[]{:S(2)}, u32[]{:S(2)}) collective-permute-start(bf16[4,256,128]{2,1,0:T(8,128)(2,1)} %fusion.21), channel_id=1, source_target_pairs={{0,2},{1,3},{2,0},{3,1},{4,6},{5,7},{6,4},{7,5},{8,10},{9,11},{10,... | collective-permute-start | bytes 786440 | tf_op jit(solution)/shard_map/att_g_z2/ppermute | solution.py:589
  (111 other events, 1256.9 us)

commit v3 on v2

--- a/solution.py
+++ b/solution.py
@@ -944,9 +944,12 @@
         vector = vector + swap(vector, "dp", bit, "sums_dp" + str(bit))
         bit *= 2
     ffn_grad = add(ffn0, ffn_one, ffn_two)
-    att_three, vector, in_last, ffn_grad = both((att_three, vector, in_last, ffn_grad))
+    att_three, vector, in_last, ffn_grad, out_first, out_last = both(
+        (att_three, vector, in_last, ffn_grad, out_first, out_last)
+    )
     att_two = swap(add(att2, att_three), "mp", 2, "att_g_z2")
     vector = vector + swap(vector, "dp", 1, "sums_core")
+    vector, ffn_grad = both((vector, ffn_grad))
     for bit in (1, 2):
         vector = vector + swap(vector, "mp", bit, "sums_z" + str(bit))
     att_grad = add(att0, att_one, att_two)

time: 365 us -> 366 us (level)
  waiting for transfers between devices: 107 us -> 114 us
    ppermute x4, waiting for transfers between devices: 8.48 us -> 14.6 us  [from_image(): return lax.ppermute(y[:, odd], ('dp', 'mp'), routes)]
    ppermute x59, starting transfers between devices: 70.5 us -> 65.5 us  [swap(): return lax.ppermute(x, axis, [(i, i ^ bits) for i in range(n)])]
    ppermute x4, starting transfers between devices: 3.14 us -> 6.82 us  [from_image(): return lax.ppermute(y[:, odd], ('dp', 'mp'), routes)]
    unnamed x193 -> x175, local copies, waits for them, and re-layouts: 9.65 us -> 7.69 us
  transfers between devices with their start and end apart: 67 -> 67, of which waited for: 26 -> 25; matrix products, arithmetic and copies ran while one was open for 13% -> 12% of each run, Pallas kernels for 31% -> 31%
where the time goes in v3:
time: 366 us; the launch traced here: 361 us
  waiting for transfers between devices  114 us (31%)
  Pallas kernels  110 us (30%)
  starting transfers between devices  77.1 us (21%)
  other arithmetic  30.6 us (8%)
  local copies, waits for them, and re-layouts  26 us (7%)
    ppermute x59, waiting for transfers between devices, swap(): return lax.ppermute(x, axis, [(i, i ^ bits) for i in range(n)])  82.2 us
    ppermute x59, starting transfers between devices, swap(): return lax.ppermute(x, axis, [(i, i ^ bits) for i in range(n)])  65.5 us
    pallas_call x2, Pallas kernels, ffn_call(): pl.pallas_call(functools.partial(ffn_kernel, parts, n_i, n_j, len(grads),...  45.4 us
    pallas_call x1, Pallas kernels, att_forward(): pl.pallas_call(functools.partial(att_fwd_kernel, parts, n_i), grid=(image...  19.7 us
    pallas_call x1, Pallas kernels, att_backward_last(): pl.pallas_call(functools.partial(att_bwd_last_kernel, parts, n_i, n_j, le...  19.3 us
    ppermute x4, waiting for transfers between devices, to_image(): return lax.ppermute(send, ('dp', 'mp'), image_routes(n_dp, n_mp, odd))  17.3 us
    convert_element_type x16, other arithmetic, add(): return total.astype(parts[0].dtype)  16 us
    ppermute x4, waiting for transfers between devices, from_image(): return lax.ppermute(y[:, odd], ('dp', 'mp'), routes)  14.6 us
  transfers between devices with their start and end apart: 67, of which 25 were waited for; matrix products, arithmetic and copies ran while one was open for 12% of the time, Pallas kernels for 31%

profile of v3, /device:TPU:0, one launch (start us, length us, event | category | flops | bytes accessed | tf_op | source)
XLA Modules:
  0.0 360.8 jit_solution(12731171302638475914)
XLA Ops:
  7.7 3.1 collective-permute-start.1
  10.8 2.6 collective-permute-start.2
  13.8 1.6 collective-permute-start.8
  15.4 1.5 collective-permute-start.9
  16.9 6.3 %collective-permute-done.1 = bf16[1056,128]{1,0:T(8,128)(2,1)S(1)} collective-permute-done((bf16[1056,128]{1,0:T(8,128)(2,1)S(1)}, bf16[1056,128]{1,0:T(8,128)(2,1)S(1)}, u32[]{:S(2)}, u32[]{:S(2)}) %collective-permute-start.1) | collective-permute-done | bytes 270368 | tf_op jit(solution)/shard_map/att_w_z1/ppermute | solution.py:589
  23.2 2.5 collective-permute-done.2
  26.2 5.9 %collective-permute-done.5 = bf16[1056,128]{1,0:T(8,128)(2,1)S(1)} collective-permute-done((bf16[1056,128]{1,0:T(8,128)(2,1)S(1)}, bf16[1056,128]{1,0:T(8,128)(2,1)S(1)}, u32[]{:S(2)}, u32[]{:S(2)}) %collective-permute-start.5) | collective-permute-done | bytes 270368 | tf_op jit(solution)/shard_map/att_w_z3/ppermute | solution.py:589
  33.2 1.5 collective-permute-start.10
  34.7 1.5 collective-permute-start.12
  36.3 2.2 collective-permute-start.4
  41.7 18.1 %collective-permute-done.4 = bf16[2,256,512]{2,1,0:T(8,128)(2,1)S(1)} collective-permute-done((bf16[2,256,512]{2,1,0:T(8,128)(2,1)}, bf16[2,256,512]{2,1,0:T(8,128)(2,1)S(1)}, u32[]{:S(2)}, u32[]{:S(2)}) %collective-permute-start.4) | collective-permute-done | bytes 524320 | tf_op jit(solution)/shard_map/ffn_w_z2/ppermute | solution.py:589
  63.1 1.5 collective-permute-start.11
  66.1 17.3 %collective-permute-done.7 = bf16[3,80,1024]{2,1,0:T(8,128)(2,1)S(1)} collective-permute-done((bf16[3,80,1024]{2,1,0:T(8,128)(2,1)S(1)}, bf16[3,80,1024]{2,1,0:T(8,128)(2,1)S(1)}, u32[]{:S(2)}, u32[]{:S(2)}) %collective-permute-start.7) | collective-permute-done | bytes 491552 | tf_op jit(solution)/shard_map/tokens_route1/ppermute | solution.py:697
  83.5 7.7 %collective-permute-start.17 = (bf16[3,2,80,1024]{3,2,1,0:T(8,128)(2,1)S(1)}, bf16[3,2,80,1024]{3,2,1,0:T(8,128)(2,1)S(1)}, u32[]{:S(2)}, u32[]{:S(2)}) collective-permute-start(bf16[3,2,80,1024]{3,2,1,0:T(8,128)(2,1)S(1)} %pad_maximum_fusion.6), channel_id=1, source_target_pairs={{0,4},{4,0},{8,12},{12,8},{16,20},{20,16},{24,28},{28,24},{1,5},{5... | collective-permute-start | bytes 2949128 | tf_op jit(solution)/shard_map/tokens_core/ppermute | solution.py:589
  96.7 2.0 collective-permute-start.21
  98.7 19.7 %att_forward.1 = (bf16[960,1024]{1,0:T(8,128)(2,1)}, bf16[6,960,128]{2,1,0:T(8,128)(2,1)}, bf16[6,960,128]{2,1,0:T(8,128)(2,1)}, bf16[960,256]{1,0:T(8,128)(2,1)...) custom-call(bf16[3,320,1024]{2,1,0:T(8,128)(2,1)} %bitcast.249, f32[1,1024]{1,0:T(1,128)S(1)} %get-tuple-element.458.g_ref, ...), custom_call_target="tpu_custom_call" | custom-call | flops 16000000000 | bytes 20000000 | tf_op jit(solution)/shard_map/att_forward/pallas_call | solution.py:179
  118.5 1.9 collective-permute-done.18
  120.7 2.2 collective-permute-start.26
  125.7 2.1 collective-permute-done.23
  129.6 8.5 %collective-permute-done.24 = bf16[1,512,512]{2,1,0:T(8,128)(2,1)S(1)} collective-permute-done((bf16[1,512,512]{2,1,0:T(8,128)(2,1)S(1)}, bf16[1,512,512]{2,1,0:T(8,128)(2,1)S(1)}, u32[]{:S(2)}, u32[]{:S(2)}) %collective-permute-start.24) | collective-permute-done | bytes 524320 | tf_op jit(solution)/shard_map/ffn_w2_y2/ppermute | solution.py:589
  140.7 23.0 %ffn_first.1 = (f32[960,1024]{1,0:T(8,128)}, bf16[960,1024]{1,0:T(8,128)(2,1)}, bf16[1024,960]{1,0:T(8,128)(2,1)}, bf16[1024,960]{1,0:T(8,128)(2,1)}, f32[960,10...) custom-call(bf16[960,1024]{1,0:T(8,128)(2,1)} %bitcast.250, ...), custom_call_target="tpu_custom_call" | custom-call | flops 24000000000 | bytes 30000000 | tf_op jit(solution)/shard_map/ffn_first/pallas_call | solution.py:350
  164.7 1.5 collective-permute-start.30
  166.1 4.7 %collective-permute-done.29 = bf16[1,256,512]{2,1,0:T(8,128)(2,1)S(1)} collective-permute-done((bf16[1,256,512]{2,1,0:T(8,128)(2,1)S(1)}, bf16[1,256,512]{2,1,0:T(8,128)(2,1)S(1)}, u32[]{:S(2)}, u32[]{:S(2)}) %collective-permute-start.29) | collective-permute-done | bytes 262176 | tf_op jit(solution)/shard_map/ffn_w1_y2/ppermute | solution.py:589
  174.1 22.5 %ffn_last.1 = (bf16[960,1024]{1,0:T(8,128)(2,1)}, bf16[960,1024]{1,0:T(8,128)(2,1)}, f32[2,512]{1,0:T(2,128)}, bf16[2,2,256,512]{3,2,1,0:T(8,128)(2,1)}, bf16[2,...) custom-call(bf16[960,1024]{1,0:T(8,128)(2,1)} %get-tuple-element.248, ...), custom_call_target="tpu_custom_call" | custom-call | flops 24000000000 | bytes 30000000 | tf_op jit(solution)/shard_map/ffn_last/pallas_call | solution.py:350
  196.7 1.8 constant_dynamic-slice_fusion.37
  199.5 2.4 add_convert_fusion.7
  209.1 11.4 %hidden_backward.1 = (f32[960,1024]{1,0:T(8,128)}, bf16[1024,960]{1,0:T(8,128)(2,1)}, bf16[2,960,128]{2,1,0:T(8,128)(2,1)S(1)}, bf16[2,960,128]{2,1,0:T(8,128)(2,1)S(1)}, f32[8,1024]{1,0:T(8,128)S(1)}) custom-call(s32[5]{0:T(128)S(1)} %copy-done.7, f32[960,1024]{1,0:T(8,128)} %get-tuple-element.230.hid_ref, bf16[960,1024]{1,0:T(8,128)(2,1)} %get-tuple-element.272.ga_ref, ...), custom_call_target="tpu_custom_call" | custom-call | flops 10000000000 | bytes 20000000 | tf_op jit(solution)/shard_map/hidden_backward/pallas_call | solution.py:462
  221.5 1.8 fusion.18
  223.3 1.6 collective-permute-start.40
  225.6 14.2 %att_backward_first.1 = (bf16[1024,960]{1,0:T(8,128)(2,1)}, bf16[960,768]{1,0:T(8,128)(2,1)S(1)}, f32[1,768]{1,0:T(1,128)S(1)}, bf16[2,4,256,128]{3,2,1,0:T(8,12...) custom-call(s32[5]{0:T(128)S(1)} %copy-done.7, ...), custom_call_target="tpu_custom_call" | custom-call | flops 16000000000 | bytes 20000000 | tf_op jit(solution)/shard_map/att_backward_first/pallas_call | solution.py:505
  240.8 7.8 %collective-permute-done.41 = bf16[3,80,1024]{2,1,0:T(8,128)(2,1)S(1)} collective-permute-done((bf16[3,80,1024]{2,1,0:T(8,128)(2,1)S(1)}, bf16[3,80,1024]{2,1,0:T(8,128)(2,1)S(1)}, u32[]{:S(2)}, u32[]{:S(2)}) %collective-permute-start.41) | collective-permute-done | bytes 491552 | tf_op jit(solution)/shard_map/block_out_route1/ppermute | solution.py:704
  253.4 19.3 %att_backward_last.1 = (bf16[960,1024]{1,0:T(8,128)(2,1)}, f32[1,768]{1,0:T(1,128)}, f32[8,1024]{1,0:T(8,128)}, bf16[2,4,256,128]{3,2,1,0:T(8,128)(2,1)}, bf16[2...) custom-call(s32[5]{0:T(128)} %copy-done.6, ...), custom_call_target="tpu_custom_call" | custom-call | flops 20000000000 | bytes 30000000 | tf_op jit(solution)/shard_map/att_backward_last/pallas_call | solution.py:563
  272.7 1.5 collective-permute-done.44
  274.3 2.0 collective-permute-done.45
  277.2 1.7 constant_dynamic-slice_fusion.31
  281.6 1.6 collective-permute-start.48
  287.6 5.2 %collective-permute-start.50 = (bf16[3,80,1024]{2,1,0:T(8,128)(2,1)}, bf16[3,80,1024]{2,1,0:T(8,128)(2,1)}, u32[]{:S(2)}, u32[]{:S(2)}) collective-permute-start(bf16[3,80,1024]{2,1,0:T(8,128)(2,1)} %slice_bitcast_fusion), channel_id=1, source_target_pairs={{0,0},{1,1},{2,6},{3,7},{4,2},{5,3},{6,4},{7,5},{8,8},{9,9},{10,14... | collective-permute-start | bytes 1474568 | tf_op jit(solution)/shard_map/input_grad_route0/ppermute | solution.py:704
  292.8 2.3 fusion.19
  301.4 1.5 collective-permute-start.52
  303.9 1.6 collective-permute-start.51
  305.6 6.3 %collective-permute-done.55 = bf16[2,256,512]{2,1,0:T(8,128)(2,1)S(1)} collective-permute-done((bf16[2,256,512]{2,1,0:T(8,128)(2,1)}, bf16[2,256,512]{2,1,0:T(8,128)(2,1)S(1)}, u32[]{:S(2)}, u32[]{:S(2)}) %collective-permute-start.55) | collective-permute-done | bytes 524320 | tf_op jit(solution)/shard_map/ffn_g_z1/ppermute | solution.py:589
  312.0 1.9 collective-permute-start.57
  318.5 3.3 collective-permute-done.58
  321.9 6.8 %collective-permute-done.59 = bf16[3,80,1024]{2,1,0:T(8,128)(2,1)S(1)} collective-permute-done((bf16[3,80,1024]{2,1,0:T(8,128)(2,1)S(1)}, bf16[3,80,1024]{2,1,0:T(8,128)(2,1)S(1)}, u32[]{:S(2)}, u32[]{:S(2)}) %collective-permute-start.59) | collective-permute-done | bytes 491552 | tf_op jit(solution)/shard_map/input_grad_route1/ppermute | solution.py:704
  328.7 5.6 %collective-permute-done.56 = bf16[4,256,128]{2,1,0:T(8,128)(2,1)S(1)} collective-permute-done((bf16[4,256,128]{2,1,0:T(8,128)(2,1)S(1)}, bf16[4,256,128]{2,1,0:T(8,128)(2,1)S(1)}, u32[]{:S(2)}, u32[]{:S(2)}) %collective-permute-start.56) | collective-permute-done | bytes 262176 | tf_op jit(solution)/shard_map/att_g_z3/ppermute | solution.py:589
  339.9 4.1 %collective-permute-done.61 = f32[176,128]{1,0:T(8,128)S(1)} collective-permute-done((f32[176,128]{1,0:T(8,128)S(1)}, f32[176,128]{1,0:T(8,128)S(1)}, u32[]{:S(2)}, u32[]{:S(2)}) %collective-permute-start.61) | collective-permute-done | bytes 90144 | tf_op jit(solution)/shard_map/sums_z1/ppermute | solution.py:589
  344.0 2.7 collective-permute-start.62
  346.7 5.1 %collective-permute-done.64 = bf16[4,256,128]{2,1,0:T(8,128)(2,1)} collective-permute-done((bf16[4,256,128]{2,1,0:T(8,128)(2,1)S(1)}, bf16[4,256,128]{2,1,0:T(8,128)(2,1)}, u32[]{:S(2)}, u32[]{:S(2)}) %collective-permute-start.64) | collective-permute-done | bytes 262176 | tf_op jit(solution)/shard_map/att_g_z2/ppermute | solution.py:589
  (420 shorter events, 83.1 us)
Async XLA Ops:
  7.7 15.5 %collective-permute-start.1 = (bf16[1056,128]{1,0:T(8,128)(2,1)S(1)}, bf16[1056,128]{1,0:T(8,128)(2,1)S(1)}, u32[]{:S(2)}, u32[]{:S(2)}) collective-permute-start(bf16[1056,128]{1,0:T(8,128)(2,1)S(1)} %get-tuple-element.430), channel_id=1, source_target_pairs={{0,1},{1,0},{2,3},{3,2},{4,5},{5,4},{6,7},{7,6},{8,9},{9,8},{10,11... | collective-permute-start | bytes 811016 | tf_op jit(solution)/shard_map/att_w_z1/ppermute | solution.py:589
  10.8 14.9 %collective-permute-start.2 = (bf16[1056,128]{1,0:T(8,128)(2,1)S(1)}, bf16[1056,128]{1,0:T(8,128)(2,1)S(1)}, u32[]{:S(2)}, u32[]{:S(2)}) collective-permute-start(bf16[1056,128]{1,0:T(8,128)(2,1)S(1)} %get-tuple-element.430), channel_id=1, source_target_pairs={{0,2},{1,3},{2,0},{3,1},{4,6},{5,7},{6,4},{7,5},{8,10},{9,11},{10,... | collective-permute-start | bytes 811016 | tf_op jit(solution)/shard_map/att_w_z2/ppermute | solution.py:589
  13.8 18.6 %collective-permute-start.8 = (bf16[2,256,512]{2,1,0:T(8,128)(2,1)S(1)}, bf16[2,256,512]{2,1,0:T(8,128)(2,1)S(1)}, u32[]{:S(2)}, u32[]{:S(2)}) collective-permute-start(bf16[2,256,512]{2,1,0:T(8,128)(2,1)S(1)} %bitcast.281), channel_id=1, source_target_pairs={{0,8},{4,12},{8,0},{12,4},{16,24},{20,28},{24,16},{28,20},{1,9},{5... | collective-permute-start | bytes 1572872 | tf_op jit(solution)/shard_map/ffn_w0_x1/ppermute | solution.py:589
  15.4 17.0 %collective-permute-start.9 = (bf16[2,256,512]{2,1,0:T(8,128)(2,1)S(1)}, bf16[2,256,512]{2,1,0:T(8,128)(2,1)}, u32[]{:S(2)}, u32[]{:S(2)}) collective-permute-start(bf16[2,256,512]{2,1,0:T(8,128)(2,1)S(1)} %bitcast.282), channel_id=1, source_target_pairs={{0,16},{4,20},{8,24},{12,28},{16,0},{20,4},{24,8},{28,12},{1,17},{... | collective-permute-start | bytes 1572872 | tf_op jit(solution)/shard_map/ffn_w0_y1/ppermute | solution.py:589
  33.2 27.4 %collective-permute-start.10 = (bf16[4,1056,128]{2,1,0:T(8,128)(2,1)S(1)}, bf16[4,1056,128]{2,1,0:T(8,128)(2,1)S(1)}, u32[]{:S(2)}, u32[]{:S(2)}) collective-permute-start(bf16[4,1056,128]{2,1,0:T(8,128)(2,1)S(1)} %get-tuple-element.199), channel_id=1, source_target_pairs={{0,8},{4,12},{8,0},{12,4},{16,24},{20,28},{24,16},{28,20},{1,9},{5... | collective-permute-start | bytes 3244040 | tf_op jit(solution)/shard_map/att_w_x1/ppermute | solution.py:589
  34.7 26.6 %collective-permute-start.12 = (bf16[4,1056,128]{2,1,0:T(8,128)(2,1)S(1)}, bf16[4,1056,128]{2,1,0:T(8,128)(2,1)S(1)}, u32[]{:S(2)}, u32[]{:S(2)}) collective-permute-start(bf16[4,1056,128]{2,1,0:T(8,128)(2,1)S(1)} %get-tuple-element.199), channel_id=1, source_target_pairs={{0,16},{4,20},{8,24},{12,28},{16,0},{20,4},{24,8},{28,12},{1,17},{... | collective-permute-start | bytes 3244040 | tf_op jit(solution)/shard_map/att_w_y1/ppermute | solution.py:589
  36.3 23.5 %collective-permute-start.4 = (bf16[2,256,512]{2,1,0:T(8,128)(2,1)}, bf16[2,256,512]{2,1,0:T(8,128)(2,1)S(1)}, u32[]{:S(2)}, u32[]{:S(2)}) collective-permute-start(bf16[2,256,512]{2,1,0:T(8,128)(2,1)} %bitcast.283), channel_id=1, source_target_pairs={{0,2},{1,3},{2,0},{3,1},{4,6},{5,7},{6,4},{7,5},{8,10},{9,11},{10,... | collective-permute-start | bytes 1572872 | tf_op jit(solution)/shard_map/ffn_w_z2/ppermute | solution.py:589
  39.5 23.7 %collective-permute-start.15 = (bf16[1,256,512]{2,1,0:T(8,128)(2,1)S(1)}, bf16[1,256,512]{2,1,0:T(8,128)(2,1)S(1)}, u32[]{:S(2)}, u32[]{:S(2)}) collective-permute-start(bf16[1,256,512]{2,1,0:T(8,128)(2,1)S(1)} %slice.332), channel_id=1, source_target_pairs={{0,16},{4,20},{8,24},{12,28},{16,0},{20,4},{24,8},{28,12},{1,17},{... | collective-permute-start | bytes 786440 | tf_op jit(solution)/shard_map/ffn_w0_y2/ppermute | solution.py:589
  41.0 23.6 %collective-permute-start.16 = (bf16[1,256,512]{2,1,0:T(8,128)(2,1)S(1)}, bf16[1,256,512]{2,1,0:T(8,128)(2,1)S(1)}, u32[]{:S(2)}, u32[]{:S(2)}) collective-permute-start(bf16[1,256,512]{2,1,0:T(8,128)(2,1)S(1)} %slice.333), channel_id=1, source_target_pairs={{0,8},{4,12},{8,0},{12,4},{16,24},{20,28},{24,16},{28,20},{1,9},{5... | collective-permute-start | bytes 786440 | tf_op jit(solution)/shard_map/ffn_w0_x2/ppermute | solution.py:589
  59.7 23.7 %collective-permute-start.14 = (bf16[2,256,512]{2,1,0:T(8,128)(2,1)S(1)}, bf16[2,256,512]{2,1,0:T(8,128)(2,1)S(1)}, u32[]{:S(2)}, u32[]{:S(2)}) collective-permute-start(bf16[2,256,512]{2,1,0:T(8,128)(2,1)S(1)} %collective-permute-done.4), channel_id=1, source_target_pairs={{0,1},{1,0},{2,3},{3,2},{4,5},{5,4},{6,7},{7,6},{8,9},{9,8},{10,11... | collective-permute-start | bytes 1572872 | tf_op jit(solution)/shard_map/ffn_w_z3/ppermute | solution.py:589
  61.3 22.1 %collective-permute-start.7 = (bf16[3,80,1024]{2,1,0:T(8,128)(2,1)S(1)}, bf16[3,80,1024]{2,1,0:T(8,128)(2,1)S(1)}, u32[]{:S(2)}, u32[]{:S(2)}) collective-permute-start(bf16[3,80,1024]{2,1,0:T(8,128)(2,1)S(1)} %copy-done.52), channel_id=1, source_target_pairs={{1,0},{0,1},{7,2},{6,3},{3,4},{2,5},{5,6},{4,7},{9,8},{8,9},{15,10... | collective-permute-start | bytes 1474568 | tf_op jit(solution)/shard_map/tokens_route1/ppermute | solution.py:697
  63.1 20.3 %collective-permute-start.11 = (bf16[2,1056,128]{2,1,0:T(8,128)(2,1)S(1)}, bf16[2,1056,128]{2,1,0:T(8,128)(2,1)S(1)}, u32[]{:S(2)}, u32[]{:S(2)}) collective-permute-start(bf16[2,1056,128]{2,1,0:T(8,128)(2,1)S(1)} %slice.330), channel_id=1, source_target_pairs={{0,16},{4,20},{8,24},{12,28},{16,0},{20,4},{24,8},{28,12},{1,17},{... | collective-permute-start | bytes 1622024 | tf_op jit(solution)/shard_map/att_w_y2/ppermute | solution.py:589
  64.6 18.8 %collective-permute-start.13 = (bf16[2,1056,128]{2,1,0:T(8,128)(2,1)S(1)}, bf16[2,1056,128]{2,1,0:T(8,128)(2,1)S(1)}, u32[]{:S(2)}, u32[]{:S(2)}) collective-permute-start(bf16[2,1056,128]{2,1,0:T(8,128)(2,1)S(1)} %slice.331), channel_id=1, source_target_pairs={{0,8},{4,12},{8,0},{12,4},{16,24},{20,28},{24,16},{28,20},{1,9},{5... | collective-permute-start | bytes 1622024 | tf_op jit(solution)/shard_map/att_w_x2/ppermute | solution.py:589
  92.6 25.9 %collective-permute-start.22 = (bf16[2,256,512]{2,1,0:T(8,128)(2,1)S(1)}, bf16[2,256,512]{2,1,0:T(8,128)(2,1)S(1)}, u32[]{:S(2)}, u32[]{:S(2)}) collective-permute-start(bf16[2,256,512]{2,1,0:T(8,128)(2,1)S(1)} %bitcast.285), channel_id=1, source_target_pairs={{0,1},{1,0},{2,3},{3,2},{4,5},{5,4},{6,7},{7,6},{8,9},{9,8},{10,11... | collective-permute-start | bytes 1572872 | tf_op jit(solution)/shard_map/ffn_w_z1/ppermute | solution.py:589
  95.0 25.4 %collective-permute-start.18 = (bf16[2,512,512]{2,1,0:T(8,128)(2,1)S(1)}, bf16[2,512,512]{2,1,0:T(8,128)(2,1)S(1)}, u32[]{:S(2)}, u32[]{:S(2)}) collective-permute-start(bf16[2,512,512]{2,1,0:T(8,128)(2,1)S(1)} %pad_maximum_fusion.3), channel_id=1, source_target_pairs={{0,8},{4,12},{8,0},{12,4},{16,24},{20,28},{24,16},{28,20},{1,9},{5... | collective-permute-start | bytes 3145736 | tf_op jit(solution)/shard_map/ffn_w2_x1/ppermute | solution.py:589
  95.5 25.1 %collective-permute-start.19 = (bf16[2,512,512]{2,1,0:T(8,128)(2,1)S(1)}, bf16[2,512,512]{2,1,0:T(8,128)(2,1)S(1)}, u32[]{:S(2)}, u32[]{:S(2)}) collective-permute-start(bf16[2,512,512]{2,1,0:T(8,128)(2,1)S(1)} %pad_maximum_fusion.3), channel_id=1, source_target_pairs={{0,16},{4,20},{8,24},{12,28},{16,0},{20,4},{24,8},{28,12},{1,17},{... | collective-permute-start | bytes 3145736 | tf_op jit(solution)/shard_map/ffn_w2_y1/ppermute | solution.py:589
  96.0 22.5 %collective-permute-start.20 = (bf16[3,80,1024]{2,1,0:T(8,128)(2,1)S(1)}, bf16[3,80,1024]{2,1,0:T(8,128)(2,1)S(1)}, u32[]{:S(2)}, u32[]{:S(2)}) collective-permute-start(bf16[3,80,1024]{2,1,0:T(8,128)(2,1)S(1)} %get-tuple-element.213), channel_id=1, source_target_pairs={{0,0},{1,1},{6,2},{7,3},{2,4},{3,5},{4,6},{5,7},{8,8},{9,9},{14,10... | collective-permute-start | bytes 1474568 | tf_op jit(solution)/shard_map/cotangent_route0/ppermute | solution.py:697
  96.7 21.8 %collective-permute-start.21 = (bf16[3,80,1024]{2,1,0:T(8,128)(2,1)S(1)}, bf16[3,80,1024]{2,1,0:T(8,128)(2,1)S(1)}, u32[]{:S(2)}, u32[]{:S(2)}) collective-permute-start(bf16[3,80,1024]{2,1,0:T(8,128)(2,1)S(1)} %get-tuple-element.214), channel_id=1, source_target_pairs={{1,0},{0,1},{7,2},{6,3},{3,4},{2,5},{5,6},{4,7},{9,8},{8,9},{15,10... | collective-permute-start | bytes 1474568 | tf_op jit(solution)/shard_map/cotangent_route1/ppermute | solution.py:697
  120.7 17.9 %collective-permute-start.26 = (bf16[960,1024]{1,0:T(8,128)(2,1)}, bf16[960,1024]{1,0:T(8,128)(2,1)S(1)}, u32[]{:S(2)}, u32[]{:S(2)}) collective-permute-start(bf16[960,1024]{1,0:T(8,128)(2,1)} %get-tuple-element.217.refs_1_), channel_id=1, source_target_pairs={{0,4},{4,0},{8,12},{12,8},{16,20},{20,16},{24,28},{28,24},{1,5},{5... | collective-permute-start | bytes 5898248 | tf_op jit(solution)/shard_map/attended/ppermute | solution.py:589
  123.7 14.4 %collective-permute-start.24 = (bf16[1,512,512]{2,1,0:T(8,128)(2,1)S(1)}, bf16[1,512,512]{2,1,0:T(8,128)(2,1)S(1)}, u32[]{:S(2)}, u32[]{:S(2)}) collective-permute-start(bf16[1,512,512]{2,1,0:T(8,128)(2,1)S(1)} %slice.263), channel_id=1, source_target_pairs={{0,16},{4,20},{8,24},{12,28},{16,0},{20,4},{24,8},{28,12},{1,17},{... | collective-permute-start | bytes 1572872 | tf_op jit(solution)/shard_map/ffn_w2_y2/ppermute | solution.py:589
  124.5 14.1 %collective-permute-start.25 = (bf16[1,512,512]{2,1,0:T(8,128)(2,1)S(1)}, bf16[1,512,512]{2,1,0:T(8,128)(2,1)S(1)}, u32[]{:S(2)}, u32[]{:S(2)}) collective-permute-start(bf16[1,512,512]{2,1,0:T(8,128)(2,1)S(1)} %slice.264), channel_id=1, source_target_pairs={{0,8},{4,12},{8,0},{12,4},{16,24},{20,28},{24,16},{28,20},{1,9},{5... | collective-permute-start | bytes 1572872 | tf_op jit(solution)/shard_map/ffn_w2_x2/ppermute | solution.py:589
  138.9 24.8 %collective-permute-start.27 = (bf16[2,256,512]{2,1,0:T(8,128)(2,1)S(1)}, bf16[2,256,512]{2,1,0:T(8,128)(2,1)S(1)}, u32[]{:S(2)}, u32[]{:S(2)}) collective-permute-start(bf16[2,256,512]{2,1,0:T(8,128)(2,1)S(1)} %copy-done.76), channel_id=1, source_target_pairs={{0,8},{4,12},{8,0},{12,4},{16,24},{20,28},{24,16},{28,20},{1,9},{5... | collective-permute-start | bytes 1572872 | tf_op jit(solution)/shard_map/ffn_w1_x1/ppermute | solution.py:589
  139.5 24.2 %collective-permute-start.28 = (bf16[2,256,512]{2,1,0:T(8,128)(2,1)S(1)}, bf16[2,256,512]{2,1,0:T(8,128)(2,1)S(1)}, u32[]{:S(2)}, u32[]{:S(2)}) collective-permute-start(bf16[2,256,512]{2,1,0:T(8,128)(2,1)S(1)} %copy-done.76), channel_id=1, source_target_pairs={{0,16},{4,20},{8,24},{12,28},{16,0},{20,4},{24,8},{28,12},{1,17},{... | collective-permute-start | bytes 1572872 | tf_op jit(solution)/shard_map/ffn_w1_y1/ppermute | solution.py:589
  172.0 24.5 %collective-permute-start.31 = (bf16[2,2,256,512]{3,2,1,0:T(8,128)(2,1)}, bf16[2,2,256,512]{3,2,1,0:T(8,128)(2,1)}, u32[]{:S(2)}, u32[]{:S(2)}) collective-permute-start(bf16[2,2,256,512]{3,2,1,0:T(8,128)(2,1)} %get-tuple-element.270), channel_id=1, source_target_pairs={{0,8},{4,12},{8,0},{12,4},{16,24},{20,28},{24,16},{28,20},{1,9},{5... | collective-permute-start | bytes 3145736 | tf_op jit(solution)/shard_map/ffn_g0_x1/ppermute | solution.py:589
  173.2 23.4 %collective-permute-start.32 = (bf16[2,2,256,512]{3,2,1,0:T(8,128)(2,1)}, bf16[2,2,256,512]{3,2,1,0:T(8,128)(2,1)}, u32[]{:S(2)}, u32[]{:S(2)}) collective-permute-start(bf16[2,2,256,512]{3,2,1,0:T(8,128)(2,1)} %get-tuple-element.271), channel_id=1, source_target_pairs={{0,16},{4,20},{8,24},{12,28},{16,0},{20,4},{24,8},{28,12},{1,17},{... | collective-permute-start | bytes 3145736 | tf_op jit(solution)/shard_map/ffn_g0_y1/ppermute | solution.py:589
  196.6 10.7 %collective-permute-start.33 = (bf16[960,1024]{1,0:T(8,128)(2,1)}, bf16[960,1024]{1,0:T(8,128)(2,1)}, u32[]{:S(2)}, u32[]{:S(2)}) collective-permute-start(bf16[960,1024]{1,0:T(8,128)(2,1)} %get-tuple-element.272.ga_ref), channel_id=1, source_target_pairs={{0,4},{4,0},{8,12},{12,8},{16,20},{20,16},{24,28},{28,24},{1,5},{5... | collective-permute-start | bytes 5898248 | tf_op jit(solution)/shard_map/grad_norm_two/ppermute | solution.py:589
  201.9 18.7 %collective-permute-start.36 = (bf16[1,2,256,512]{3,2,1,0:T(8,128)(2,1)}, bf16[1,2,256,512]{3,2,1,0:T(8,128)(2,1)S(1)}, u32[]{:S(2)}, u32[]{:S(2)}) collective-permute-start(bf16[1,2,256,512]{3,2,1,0:T(8,128)(2,1)} %add_convert_fusion.7), channel_id=1, source_target_pairs={{0,16},{4,20},{8,24},{12,28},{16,0},{20,4},{24,8},{28,12},{1,17},{... | collective-permute-start | bytes 1572872 | tf_op jit(solution)/shard_map/ffn_g0_y2/ppermute | solution.py:589
  204.2 16.3 %collective-permute-start.35 = (bf16[1,2,256,512]{3,2,1,0:T(8,128)(2,1)S(1)}, bf16[1,2,256,512]{3,2,1,0:T(8,128)(2,1)S(1)}, u32[]{:S(2)}, u32[]{:S(2)}) collective-permute-start(bf16[1,2,256,512]{3,2,1,0:T(8,128)(2,1)S(1)} %add_convert_fusion.8), channel_id=1, source_target_pairs={{0,8},{4,12},{8,0},{12,4},{16,24},{20,28},{24,16},{28,20},{1,9},{5... | collective-permute-start | bytes 1572872 | tf_op jit(solution)/shard_map/ffn_g0_x2/ppermute | solution.py:589
  205.2 35.6 %collective-permute-start.38 = (bf16[2,2,256,512]{3,2,1,0:T(8,128)(2,1)S(1)}, bf16[2,2,256,512]{3,2,1,0:T(8,128)(2,1)S(1)}, u32[]{:S(2)}, u32[]{:S(2)}) collective-permute-start(bf16[2,2,256,512]{3,2,1,0:T(8,128)(2,1)S(1)} %copy-done.74), channel_id=1, source_target_pairs={{0,8},{4,12},{8,0},{12,4},{16,24},{20,28},{24,16},{28,20},{1,9},{5... | collective-permute-start | bytes 3145736 | tf_op jit(solution)/shard_map/ffn_g1_x1/ppermute | solution.py:589
  206.3 34.5 %collective-permute-start.39 = (bf16[2,2,256,512]{3,2,1,0:T(8,128)(2,1)S(1)}, bf16[2,2,256,512]{3,2,1,0:T(8,128)(2,1)S(1)}, u32[]{:S(2)}, u32[]{:S(2)}) collective-permute-start(bf16[2,2,256,512]{3,2,1,0:T(8,128)(2,1)S(1)} %copy-done.73), channel_id=1, source_target_pairs={{0,16},{4,20},{8,24},{12,28},{16,0},{20,4},{24,8},{28,12},{1,17},{... | collective-permute-start | bytes 3145736 | tf_op jit(solution)/shard_map/ffn_g1_y1/ppermute | solution.py:589
  208.1 12.5 %collective-permute-start.37 = (bf16[3,80,1024]{2,1,0:T(8,128)(2,1)S(1)}, bf16[3,80,1024]{2,1,0:T(8,128)(2,1)S(1)}, u32[]{:S(2)}, u32[]{:S(2)}) collective-permute-start(bf16[3,80,1024]{2,1,0:T(8,128)(2,1)S(1)} %slice_bitcast_fusion.3), channel_id=1, source_target_pairs={{0,0},{1,1},{2,6},{3,7},{4,2},{5,3},{6,4},{7,5},{8,8},{9,9},{10,14... | collective-permute-start | bytes 1474568 | tf_op jit(solution)/shard_map/block_out_route0/ppermute | solution.py:704
  223.3 25.4 %collective-permute-start.40 = (bf16[2,256,512]{2,1,0:T(8,128)(2,1)S(1)}, bf16[2,256,512]{2,1,0:T(8,128)(2,1)S(1)}, u32[]{:S(2)}, u32[]{:S(2)}) collective-permute-start(bf16[2,256,512]{2,1,0:T(8,128)(2,1)S(1)} %get-tuple-element.393), channel_id=1, source_target_pairs={{0,1},{1,0},{2,3},{3,2},{4,5},{5,4},{6,7},{7,6},{8,9},{9,8},{10,11... | collective-permute-start | bytes 1572872 | tf_op jit(solution)/shard_map/ffn_g_z3/ppermute | solution.py:589
  224.9 23.8 %collective-permute-start.41 = (bf16[3,80,1024]{2,1,0:T(8,128)(2,1)S(1)}, bf16[3,80,1024]{2,1,0:T(8,128)(2,1)S(1)}, u32[]{:S(2)}, u32[]{:S(2)}) collective-permute-start(bf16[3,80,1024]{2,1,0:T(8,128)(2,1)S(1)} %slice_bitcast_fusion.2), channel_id=1, source_target_pairs={{0,1},{1,0},{2,7},{3,6},{4,3},{5,2},{6,5},{7,4},{8,9},{9,8},{10,15... | collective-permute-start | bytes 1474568 | tf_op jit(solution)/shard_map/block_out_route1/ppermute | solution.py:704
  248.8 25.4 %collective-permute-start.44 = (bf16[2,256,512]{2,1,0:T(8,128)(2,1)S(1)}, bf16[2,256,512]{2,1,0:T(8,128)(2,1)S(1)}, u32[]{:S(2)}, u32[]{:S(2)}) collective-permute-start(bf16[2,256,512]{2,1,0:T(8,128)(2,1)S(1)} %add_convert_fusion.2), channel_id=1, source_target_pairs={{0,2},{1,3},{2,0},{3,1},{4,6},{5,7},{6,4},{7,5},{8,10},{9,11},{10,... | collective-permute-start | bytes 1572872 | tf_op jit(solution)/shard_map/ffn_g_z2/ppermute | solution.py:589
  249.0 25.2 %collective-permute-start.43 = (bf16[1,2,256,512]{3,2,1,0:T(8,128)(2,1)S(1)}, bf16[1,2,256,512]{3,2,1,0:T(8,128)(2,1)S(1)}, u32[]{:S(2)}, u32[]{:S(2)}) collective-permute-start(bf16[1,2,256,512]{3,2,1,0:T(8,128)(2,1)S(1)} %add_convert_fusion.3), channel_id=1, source_target_pairs={{0,16},{4,20},{8,24},{12,28},{16,0},{20,4},{24,8},{28,12},{1,17},{... | collective-permute-start | bytes 1572872 | tf_op jit(solution)/shard_map/ffn_g1_y2/ppermute | solution.py:589
  250.5 23.8 %collective-permute-start.42 = (bf16[1,2,256,512]{3,2,1,0:T(8,128)(2,1)S(1)}, bf16[1,2,256,512]{3,2,1,0:T(8,128)(2,1)S(1)}, u32[]{:S(2)}, u32[]{:S(2)}) collective-permute-start(bf16[1,2,256,512]{3,2,1,0:T(8,128)(2,1)S(1)} %add_convert_fusion.4), channel_id=1, source_target_pairs={{0,8},{4,12},{8,0},{12,4},{16,24},{20,28},{24,16},{28,20},{1,9},{5... | collective-permute-start | bytes 1572872 | tf_op jit(solution)/shard_map/ffn_g1_x2/ppermute | solution.py:589
  251.4 24.8 %collective-permute-start.45 = (bf16[2,4,256,128]{3,2,1,0:T(8,128)(2,1)S(1)}, bf16[2,4,256,128]{3,2,1,0:T(8,128)(2,1)S(1)}, u32[]{:S(2)}, u32[]{:S(2)}) collective-permute-start(bf16[2,4,256,128]{3,2,1,0:T(8,128)(2,1)S(1)} %get-tuple-element.319), channel_id=1, source_target_pairs={{0,8},{4,12},{8,0},{12,4},{16,24},{20,28},{24,16},{28,20},{1,9},{5... | collective-permute-start | bytes 1572872 | tf_op jit(solution)/shard_map/att_ga_x1/ppermute | solution.py:589
  252.5 23.7 %collective-permute-start.46 = (bf16[2,4,256,128]{3,2,1,0:T(8,128)(2,1)S(1)}, bf16[2,4,256,128]{3,2,1,0:T(8,128)(2,1)S(1)}, u32[]{:S(2)}, u32[]{:S(2)}) collective-permute-start(bf16[2,4,256,128]{3,2,1,0:T(8,128)(2,1)S(1)} %get-tuple-element.320), channel_id=1, source_target_pairs={{0,16},{4,20},{8,24},{12,28},{16,0},{20,4},{24,8},{28,12},{1,17},{... | collective-permute-start | bytes 1572872 | tf_op jit(solution)/shard_map/att_ga_y1/ppermute | solution.py:589
  280.6 15.9 %collective-permute-start.47 = (bf16[2,4,256,128]{3,2,1,0:T(8,128)(2,1)}, bf16[2,4,256,128]{3,2,1,0:T(8,128)(2,1)}, u32[]{:S(2)}, u32[]{:S(2)}) collective-permute-start(bf16[2,4,256,128]{3,2,1,0:T(8,128)(2,1)} %get-tuple-element.322), channel_id=1, source_target_pairs={{0,8},{4,12},{8,0},{12,4},{16,24},{20,28},{24,16},{28,20},{1,9},{5... | collective-permute-start | bytes 1572872 | tf_op jit(solution)/shard_map/att_gb_x1/ppermute | solution.py:589
  281.6 14.9 %collective-permute-start.48 = (bf16[2,4,256,128]{3,2,1,0:T(8,128)(2,1)}, bf16[2,4,256,128]{3,2,1,0:T(8,128)(2,1)}, u32[]{:S(2)}, u32[]{:S(2)}) collective-permute-start(bf16[2,4,256,128]{3,2,1,0:T(8,128)(2,1)} %get-tuple-element.323), channel_id=1, source_target_pairs={{0,16},{4,20},{8,24},{12,28},{16,0},{20,4},{24,8},{28,12},{1,17},{... | collective-permute-start | bytes 1572872 | tf_op jit(solution)/shard_map/att_gb_y1/ppermute | solution.py:589
  295.1 16.8 %collective-permute-start.55 = (bf16[2,256,512]{2,1,0:T(8,128)(2,1)}, bf16[2,256,512]{2,1,0:T(8,128)(2,1)S(1)}, u32[]{:S(2)}, u32[]{:S(2)}) collective-permute-start(bf16[2,256,512]{2,1,0:T(8,128)(2,1)} %fusion.19), channel_id=1, source_target_pairs={{0,1},{1,0},{2,3},{3,2},{4,5},{5,4},{6,7},{7,6},{8,9},{9,8},{10,11... | collective-permute-start | bytes 1572872 | tf_op jit(solution)/shard_map/ffn_g_z1/ppermute | solution.py:589
  298.1 13.9 %collective-permute-start.54 = (bf16[1,4,256,128]{3,2,1,0:T(8,128)(2,1)S(1)}, bf16[1,4,256,128]{3,2,1,0:T(8,128)(2,1)S(1)}, u32[]{:S(2)}, u32[]{:S(2)}) collective-permute-start(bf16[1,4,256,128]{3,2,1,0:T(8,128)(2,1)S(1)} %add_convert_fusion.13), channel_id=1, source_target_pairs={{0,16},{4,20},{8,24},{12,28},{16,0},{20,4},{24,8},{28,12},{1,17},{... | collective-permute-start | bytes 786440 | tf_op jit(solution)/shard_map/att_ga_y2/ppermute | solution.py:589
  299.7 12.2 %collective-permute-start.53 = (bf16[1,4,256,128]{3,2,1,0:T(8,128)(2,1)S(1)}, bf16[1,4,256,128]{3,2,1,0:T(8,128)(2,1)S(1)}, u32[]{:S(2)}, u32[]{:S(2)}) collective-permute-start(bf16[1,4,256,128]{3,2,1,0:T(8,128)(2,1)S(1)} %add_convert_fusion.14), channel_id=1, source_target_pairs={{0,8},{4,12},{8,0},{12,4},{16,24},{20,28},{24,16},{28,20},{1,9},{5... | collective-permute-start | bytes 786440 | tf_op jit(solution)/shard_map/att_ga_x2/ppermute | solution.py:589
  311.9 16.7 %collective-permute-start.59 = (bf16[3,80,1024]{2,1,0:T(8,128)(2,1)S(1)}, bf16[3,80,1024]{2,1,0:T(8,128)(2,1)S(1)}, u32[]{:S(2)}, u32[]{:S(2)}) collective-permute-start(bf16[3,80,1024]{2,1,0:T(8,128)(2,1)S(1)} %slice_bitcast_fusion.1), channel_id=1, source_target_pairs={{0,1},{1,0},{2,7},{3,6},{4,3},{5,2},{6,5},{7,4},{8,9},{9,8},{10,15... | collective-permute-start | bytes 1474568 | tf_op jit(solution)/shard_map/input_grad_route1/ppermute | solution.py:704
  315.0 19.3 %collective-permute-start.56 = (bf16[4,256,128]{2,1,0:T(8,128)(2,1)S(1)}, bf16[4,256,128]{2,1,0:T(8,128)(2,1)S(1)}, u32[]{:S(2)}, u32[]{:S(2)}) collective-permute-start(bf16[4,256,128]{2,1,0:T(8,128)(2,1)S(1)} %fusion.25), channel_id=1, source_target_pairs={{0,1},{1,0},{2,3},{3,2},{4,5},{5,4},{6,7},{7,6},{8,9},{9,8},{10,11... | collective-permute-start | bytes 786440 | tf_op jit(solution)/shard_map/att_g_z3/ppermute | solution.py:589
  316.4 30.3 %collective-permute-start.63 = (bf16[4,256,128]{2,1,0:T(8,128)(2,1)S(1)}, bf16[4,256,128]{2,1,0:T(8,128)(2,1)S(1)}, u32[]{:S(2)}, u32[]{:S(2)}) collective-permute-start(bf16[4,256,128]{2,1,0:T(8,128)(2,1)S(1)} %fusion.27), channel_id=1, source_target_pairs={{0,1},{1,0},{2,3},{3,2},{4,5},{5,4},{6,7},{7,6},{8,9},{9,8},{10,11... | collective-permute-start | bytes 786440 | tf_op jit(solution)/shard_map/att_g_z1/ppermute | solution.py:589
  335.4 16.4 %collective-permute-start.64 = (bf16[4,256,128]{2,1,0:T(8,128)(2,1)S(1)}, bf16[4,256,128]{2,1,0:T(8,128)(2,1)}, u32[]{:S(2)}, u32[]{:S(2)}) collective-permute-start(bf16[4,256,128]{2,1,0:T(8,128)(2,1)S(1)} %fusion.21), channel_id=1, source_target_pairs={{0,2},{1,3},{2,0},{3,1},{4,6},{5,7},{6,4},{7,5},{8,10},{9,11},{10,... | collective-permute-start | bytes 786440 | tf_op jit(solution)/shard_map/att_g_z2/ppermute | solution.py:589
  339.3 17.4 %collective-permute-start.66 = (bf16[2,128,512]{1,2,0:T(8,128)(2,1)S(1)}, bf16[2,128,512]{1,2,0:T(8,128)(2,1)S(1)}, u32[]{:S(2)}, u32[]{:S(2)}) collective-permute-start(bf16[2,128,512]{1,2,0:T(8,128)(2,1)S(1)} %bitcast.295), channel_id=1, source_target_pairs={{0,4},{4,0},{8,12},{12,8},{16,20},{20,16},{24,28},{28,24},{1,5},{5... | collective-permute-start | bytes 786440 | tf_op jit(solution)/shard_map/ffn_g_core/ppermute | solution.py:589
  (102 other events, 1316.0 us)
